TPU v7x, 32 devices: a whole 2x2x4 slice. The times are simulated.
32 devices in a mesh: reg: 8 (over z, y), ep: 4 (over x, core).
Axes of the slice: x: 2, y: 2, z: 4, core: 2. Of those that a mesh axis runs over, the one named last changes fastest.
Arguments:
- log_prices: bfloat16 [32, 64, 256], P('reg', 'ep'), may hold values from -3 to 3
- log_wages: float32 [32, 64], P('reg', 'ep'), may hold values from -12 to 1
- labor_share: float32 [32, 256], P('reg'), may hold values from 0.3 to 0.7
- io_coeffs: bfloat16 [32, 256, 256], P('reg'), may hold values from -0.375 to 0.375
- pair_blocks: bfloat16 [32, 32, 256, 256], P('reg'), may hold values from -0.0201 to 0.801
- log_tau: float32 [32, 32, 256], P('reg'), may hold values from 0.05 to 2
- elasticity: float32 [256], replicated, may hold values from 2 to 40
- partners: int32 [32, 32], replicated, may hold values from 0 to 31, as said below
- list_lengths: int32 [32], replicated, may hold values from 1 to 32, as said below
- price_cotangent: float32 [32, 64, 256], P('reg', 'ep'), may hold values from -6 to 6
Outputs:
- new_prices: bfloat16 [32, 64, 256], P('reg', 'ep')
- price_grad: float32 [32, 64, 256], P('reg', 'ep')
- wage_grad: float32 [32, 64], P('reg', 'ep')
- tau_grad: float32 [32, 32, 256], P('reg')
Inputs may be any that keep to these rules, and one draw needn't show every extreme that they name: `partners`: each list names distinct regions. Over their live entries, the 4 importers of an aligned block name at most 16 regions of any one aligned block of 4 regions, and this is reached in every draw. `list_lengths`: in some aligned block of 4 regions every list has 32 live entries.
All inputs are finite; a program needn't handle non-finite values.
Results may differ from a plain program's by a relative error of at most 0.0064.
Values may be sent and summed in bfloat16 or wider, within the bound.
No kernel may reach another device: no remote copies, remote signals or barrier semaphores. Data moves between devices by JAX's collectives and lax.ppermute only.
A program may use at most 64 MiB of HBM per device.

v0:
```python
import jax
import jax.numpy as jnp
from jax import lax
from jax.sharding import PartitionSpec as P


def shards(
    log_prices,
    log_wages,
    labor_share,
    io_coeffs,
    pair_blocks,
    log_tau,
    elasticity,
    partners,
    list_lengths,
    price_cotangent,
):
    own_regions, episodes, sectors = log_prices.shape
    max_slots = pair_blocks.shape[1]
    slot_total = own_regions * max_slots
    row_width = episodes * sectors
    reg_count = lax.axis_size("reg")
    my_index = lax.axis_index("reg")
    unit_cost = (
        labor_share[:, None, :] * log_wages[:, :, None]
        + jnp.einsum("iek,ikj->iej", log_prices, io_coeffs, preferred_element_type=jnp.float32)
    ).astype(jnp.bfloat16)
    first_region = my_index * own_regions
    my_partners = lax.dynamic_slice_in_dim(partners, first_region, own_regions, 0)
    my_lengths = lax.dynamic_slice_in_dim(list_lengths, first_region, own_regions, 0)
    slot_index = jnp.arange(max_slots, dtype=jnp.int32)
    live = slot_index[None, :] < my_lengths[:, None]
    flat_partners = my_partners.reshape(-1)
    flat_live = live.reshape(-1)
    capacity = -(-slot_total // reg_count)
    all_live = (slot_index[None, :] < list_lengths[:, None]).reshape(reg_count, slot_total)
    all_partners = partners.reshape(reg_count, slot_total)
    all_owner = all_partners // own_regions
    owner_hits = (
        (all_owner[:, :, None] == jnp.arange(reg_count, dtype=jnp.int32)[None, None, :])
        & all_live[:, :, None]
    ).astype(jnp.int32)
    all_rank = jnp.sum((jnp.cumsum(owner_hits, axis=1) - owner_hits) * owner_hits, axis=2)
    my_rank = lax.dynamic_index_in_dim(all_rank, my_index, 0, keepdims=False)
    my_position = jnp.where(flat_live, flat_partners // own_regions * capacity + my_rank, 0)
    sending = (all_owner == my_index) & all_live
    matches = sending[:, :, None] & (
        all_rank[:, :, None] == jnp.arange(capacity, dtype=jnp.int32)[None, None, :]
    )
    local_region = jnp.sum(
        matches.astype(jnp.int32) * (all_partners - first_region)[:, :, None], axis=1
    ).reshape(-1)
    valid = jnp.any(matches, axis=1).reshape(-1)
    outgoing = jnp.where(
        valid[:, None, None],
        jnp.take(unit_cost, local_region, axis=0, mode="clip"),
        jnp.zeros((), jnp.bfloat16),
    )
    incoming = lax.all_to_all(outgoing, "reg", split_axis=0, concat_axis=0, tiled=True)
    exporter_rows = jnp.take(incoming, my_position, axis=0, mode="clip")
    exporter_rows = exporter_rows.reshape(own_regions, max_slots, episodes, sectors)
    landed = log_tau[:, :, None, :] + jnp.einsum(
        "rsek,rskj->rsej", exporter_rows, pair_blocks, preferred_element_type=jnp.float32
    )
    live_mask = live[:, :, None, None]
    scores = jnp.where(live_mask, -elasticity * landed, -jnp.inf)
    top_score = jnp.max(scores, axis=1)
    weights = jnp.exp(scores - top_score[:, None])
    total = jnp.sum(weights, axis=1)
    new_prices = (-(top_score + jnp.log(total)) / elasticity).astype(jnp.bfloat16)
    adjoint = price_cotangent[:, None] * (weights / total[:, None])
    tau_grad = lax.psum(jnp.sum(adjoint, axis=2), "ep")
    pushed = jnp.einsum(
        "rsej,rskj->rsek",
        adjoint.astype(jnp.bfloat16),
        pair_blocks,
        preferred_element_type=jnp.float32,
    ).astype(jnp.bfloat16)
    pushed = jnp.where(live_mask, pushed, jnp.zeros((), jnp.bfloat16)).reshape(
        slot_total, row_width
    )
    placer = (
        (my_position[None, :] == jnp.arange(reg_count * capacity, dtype=jnp.int32)[:, None])
        & flat_live[None, :]
    ).astype(jnp.bfloat16)
    returning = (
        jnp.dot(placer, pushed, preferred_element_type=jnp.float32)
        .astype(jnp.bfloat16)
        .reshape(reg_count * capacity, episodes, sectors)
    )
    returned = lax.all_to_all(returning, "reg", split_axis=0, concat_axis=0, tiled=True)
    collector = (
        (local_region[None, :] == jnp.arange(own_regions, dtype=jnp.int32)[:, None])
        & valid[None, :]
    ).astype(jnp.bfloat16)
    cost_adjoint = jnp.dot(
        collector,
        returned.reshape(reg_count * capacity, row_width),
        preferred_element_type=jnp.float32,
    )
    cost_adjoint = cost_adjoint.reshape(own_regions, episodes, sectors)
    price_grad = jnp.einsum(
        "iej,ikj->iek",
        cost_adjoint.astype(jnp.bfloat16),
        io_coeffs,
        preferred_element_type=jnp.float32,
    )
    wage_grad = jnp.sum(cost_adjoint * labor_share[:, None, :], axis=2)
    return (new_prices, price_grad, wage_grad, tau_grad)


def solution(mesh):
    return jax.shard_map(
        shards,
        mesh=mesh,
        in_specs=(
            P("reg", "ep", None),
            P("reg", "ep"),
            P("reg", None),
            P("reg", None, None),
            P("reg", None, None, None),
            P("reg", None, None),
            P(),
            P(),
            P(),
            P("reg", "ep", None),
        ),
        out_specs=(
            P("reg", "ep", None),
            P("reg", "ep", None),
            P("reg", "ep"),
            P("reg", None, None),
        ),
        check_vma=False,
    )
```

profile of v0, /device:TPU:0, one launch (start us, length us, event | category | flops | bytes accessed | tf_op | source)
XLA Modules:
  0.0 123.5 jit_solution(9210995686404370569)
XLA Ops:
  7.2 0.0 copy-start
  7.2 0.1 lt.106
  7.3 0.1 lt.99
  7.4 0.8 reshape.357
  8.2 0.7 lt.101
  8.9 0.1 lt.102
  9.0 0.1 lt.103
  9.1 0.1 copy.78
  9.2 0.1 copy.77
  9.3 2.8 %select_reduce_fusion = s32[8,128]{0,1:T(8,128)S(1)} fusion(s32[8,128]{0,1:T(8,128)S(1)} %copy.77, pred[8,128]{0,1:T(8,128)(4,1)S(1)} %copy.78), kind=kOutput, calls=%fused_computation.18 | output fusion | flops 1113088 | bytes 9216 | tf_op jit(solution)/shard_map/jit(cumsum)/reduce_window_sum | solution.py:44
  12.2 0.2 fusion.22
  12.4 0.2 select_reduce_fusion.1
  12.6 0.1 reshape.366
  12.7 0.1 broadcast_in_dim.41
  12.8 0.0 copy-done
  12.8 1.0 fusion.2
  13.8 0.7 gather_fusion
  14.4 0.0 copy-start.5
  14.4 0.0 copy-start.4
  14.5 1.2 broadcast_select_fusion
  15.7 0.0 copy-start.2
  15.7 7.4 %all-to-all-start = ((bf16[128,16,256]{2,1,0:T(8,128)(2,1)}), bf16[128,16,256]{2,1,0:T(8,128)(2,1)S(1)}, u32[]{:S(2)}, u32[]{:S(2)}) async-start(bf16[128,16,256]{2,1,0:T(8,128)(2,1)} %broadcast_select_fusion), calls=%async_computation | async-start | bytes 2097152 | tf_op jit(solution)/shard_map/all_to_all | solution.py:60
  23.1 0.0 copy-done.5
  23.1 0.1 dynamic_slice.10
  23.2 0.1 iota_compare_fusion.4
  23.2 0.1 lt.109
  23.3 0.1 lt.114
  23.4 0.7 constant_dynamic-slice_fusion
  24.1 0.1 reshape.358
  24.2 0.1 reshape.382
  24.3 0.0 copy-done.4
  24.4 0.1 lt.96
  24.4 0.1 lt.112
  24.5 0.2 fusion.19
  24.8 24.1 %all-to-all-done = bf16[128,16,256]{2,1,0:T(8,128)(2,1)S(1)} async-done(((bf16[128,16,256]{2,1,0:T(8,128)(2,1)}), bf16[128,16,256]{2,1,0:T(8,128)(2,1)S(1)}, u32[]{:S(2)}, u32[]{:S(2)}) %all-to-all-start) | async-done | bytes 1048608 | tf_op jit(solution)/shard_map/all_to_all | solution.py:60
  48.8 1.6 %gather_fusion.1 = bf16[128,16,256]{2,1,0:T(8,128)(2,1)} fusion(bf16[128,16,256]{2,1,0:T(8,128)(2,1)S(1)} %all-to-all-done, s32[1024]{0:T(1024)S(1)} %pad_clamp_fusion), kind=kCustom, calls=%fused_computation.1 | custom fusion | bytes 2097664 | tf_op jit(solution)/shard_map/jit(_take)/gather | solution.py:61
  50.5 0.0 copy-done.2
  50.5 8.4 %fusion.39 = (f32[4,16,256]{2,1,0:T(8,128)S(1)}, f32[4,32,16,256]{3,2,1,0:T(8,128)S(1)}) fusion(bf16[4,32,16,256]{3,2,1,0:T(8,128)(2,1)} %bitcast.38, bf16[4,32,256,256]{3,2,1,0:T(8,128)(2,1)} %param.14, f32[4,32,256]{2,1,0:T(8,128)S(1)} %copy-done.2, f32[256]{0:T(256)S(1)} %neg.6, pred[4,32]{1,0:T(4,128)(4,1)S(1)} %iota_compare_fusion.4), kind=kOutput, calls=%fused_computation.75 | convolution fusion | flops 270516224 | bytes 20120704 | tf_op jit(solution)/shard_map/rsek,rskj->rsej/dot_general | solution.py:63
  58.9 0.0 copy-start.1
  58.9 0.3 fusion
  59.2 0.5 copy-done.1
  59.8 11.2 %fusion.1 = bf16[4,32,16,256]{3,2,1,0:T(8,128)(2,1)} fusion(bf16[4,32,256,256]{3,2,1,0:T(8,128)(2,1)} %param.14, pred[4,32]{1,0:T(4,128)(4,1)S(1)} %iota_compare_fusion.4, f32[4,32,16,256]{3,2,1,0:T(8,128)S(1)} %get-tuple-element.11, f32[4,16,256]{2,1,0:T(8,128)S(1)} %fusion, f32[4,16,256]{2,1,0:T(8,128)S(1)} %copy-done.1, ...), kind=kOutput, calls=%fused_computation.8 | convolution fusion | flops 271581184 | bytes 20119680 | tf_op jit(solution)/shard_map/rsej,rskj->rsek/dot_general | solution.py:74
  71.0 1.6 %copy.89 = bf16[16,8,16,256]{3,1,2,0:T(8,128)(2,1)S(1)} copy(bf16[16,8,16,256]{3,2,1,0:T(8,128)(2,1)} %bitcast.37) | data formatting | bytes 2097152
  72.6 0.4 convolution_convert_fusion
  73.1 1.3 %copy.90 = bf16[16,8,16,256]{3,2,1,0:T(8,128)(2,1)} copy(bf16[16,8,16,256]{3,1,2,0:T(8,128)(2,1)S(1)} %bitcast.41) | data formatting | bytes 2097152
  74.4 4.2 %all-to-all-start.1 = ((bf16[128,16,256]{2,1,0:T(8,128)(2,1)}), bf16[128,16,256]{2,1,0:T(8,128)(2,1)}, u32[]{:S(2)}, u32[]{:S(2)}) async-start(bf16[128,16,256]{2,1,0:T(8,128)(2,1)} %bitcast.39), calls=%async_computation.1 | async-start | bytes 2097152 | tf_op jit(solution)/shard_map/all_to_all | solution.py:92
  78.6 0.0 all-reduce.2.cloned.1.call-start
  78.7 1.3 %fusion.12 = f32[4,32,256]{2,1,0:T(8,128)} fusion(f32[4,16,256]{2,1,0:T(8,128)S(1)} %fusion, f32[4,32,16,256]{3,2,1,0:T(8,128)S(1)} %get-tuple-element.11, f32[4,16,256]{2,1,0:T(8,128)S(1)} %get-tuple-element.10, f32[4,16,256]{2,1,0:T(8,128)S(1)} %copy-done.1), kind=kLoop, calls=%fused_computation.21 | loop fusion | flops 2064384 | bytes 2424832 | tf_op jit(solution)/shard_map/reduce_sum | solution.py:73
  80.0 0.0 copy-start.3
  80.0 0.0 all-reduce.2.cloned.1.call-update
  80.0 24.2 %all-to-all-done.1 = bf16[128,16,256]{2,1,0:T(8,128)(2,1)} async-done(((bf16[128,16,256]{2,1,0:T(8,128)(2,1)}), bf16[128,16,256]{2,1,0:T(8,128)(2,1)}, u32[]{:S(2)}, u32[]{:S(2)}) %all-to-all-start.1) | async-done | bytes 1048608 | tf_op jit(solution)/shard_map/all_to_all | solution.py:92
  104.2 1.9 %copy.88 = bf16[128,16,256]{0,2,1:T(8,128)(2,1)S(1)} copy(bf16[128,16,256]{2,1,0:T(8,128)(2,1)} %all-to-all-done.1) | data formatting | bytes 2097152 | tf_op jit(solution)/shard_map/reshape | solution.py:99
  106.2 0.4 fusion.40
  106.5 0.9 fusion.26
  107.4 0.0 copy-done.3
  107.4 1.2 fusion.20
  108.7 6.4 %all-reduce.2.cloned.1.call-done = f32[4,32,256]{2,1,0:T(8,128)} async-done(((f32[4,32,256]{2,1,0:T(8,128)}), f32[4,32,256]{2,1,0:T(8,128)}) %all-reduce.2.cloned.1.call-update) | async-done | bytes 131088 | tf_op jit(solution)/shard_map/psum | solution.py:73
  115.1 1.6 %copy.97 = f32[4,32,256]{2,1,0:T(8,128)} copy(f32[4,32,256]{2,1,0:T(8,128)} %all-reduce.2.cloned.1.call-done) | data formatting | bytes 262144
  (10 shorter events, 0.1 us)
Async XLA Ops:
  7.2 5.6 %copy-start = (bf16[4,256,256]{2,1,0:T(8,128)(2,1)S(1)}, bf16[4,256,256]{2,1,0:T(8,128)(2,1)}, u32[]{:S(2)}) copy-start(bf16[4,256,256]{2,1,0:T(8,128)(2,1)} %param.13) | copy-start | bytes 1572868
  14.4 8.6 %copy-start.5 = (s32[32]{0:T(128)S(1)}, s32[32]{0:T(128)}, u32[]{:S(2)}) copy-start(s32[32]{0:T(128)} %param.18) | copy-start | bytes 388
  14.4 9.9 %copy-start.4 = (f32[256]{0:T(256)S(1)}, f32[256]{0:T(256)}, u32[]{:S(2)}) copy-start(f32[256]{0:T(256)} %param.16) | copy-start | bytes 3076
  15.7 34.8 %copy-start.2 = (f32[4,32,256]{2,1,0:T(8,128)S(1)}, f32[4,32,256]{2,1,0:T(8,128)}, u32[]{:S(2)}) copy-start(f32[4,32,256]{2,1,0:T(8,128)} %param.15) | copy-start | bytes 393220
  15.7 33.2 %all-to-all-start = ((bf16[128,16,256]{2,1,0:T(8,128)(2,1)}), bf16[128,16,256]{2,1,0:T(8,128)(2,1)S(1)}, u32[]{:S(2)}, u32[]{:S(2)}) async-start(bf16[128,16,256]{2,1,0:T(8,128)(2,1)} %broadcast_select_fusion), calls=%async_computation | async-start | bytes 2097152 | tf_op jit(solution)/shard_map/all_to_all | solution.py:60
  58.9 0.8 copy-start.1
  74.4 29.8 %all-to-all-start.1 = ((bf16[128,16,256]{2,1,0:T(8,128)(2,1)}), bf16[128,16,256]{2,1,0:T(8,128)(2,1)}, u32[]{:S(2)}, u32[]{:S(2)}) async-start(bf16[128,16,256]{2,1,0:T(8,128)(2,1)} %bitcast.39), calls=%async_computation.1 | async-start | bytes 2097152 | tf_op jit(solution)/shard_map/all_to_all | solution.py:92
  78.6 36.5 %all-reduce.2.cloned.1.call-start = ((), (), s32[]{:S(2)}) async-start(), calls=%async_computation.2 | async-start | bytes 262144 | tf_op jit(solution)/shard_map/psum | solution.py:73
  80.0 27.5 %copy-start.3 = (f32[4,256]{1,0:T(4,128)S(1)}, f32[4,256]{1,0:T(4,128)}, u32[]{:S(2)}) copy-start(f32[4,256]{1,0:T(4,128)} %param.12) | copy-start | bytes 12292
Sparse Core Ops, SparseCore 0:
  82.3 32.6 all-reduce.1
where the time goes:
time: 124 us; the launch traced here: 123 us
  waiting for transfers between devices  54.7 us (44%)
  matrix products  22.3 us (18%)
  between operations  14.2 us (11%)
  local copies, waits for them, and re-layouts  12.9 us (10%)
  starting transfers between devices  11.7 us (9%)
  other arithmetic  7.61 us (6%)
    all_to_all x1, waiting for transfers between devices, shards(): lax.all_to_all(returning, 'reg', split_axis=0, concat_axis=0, tiled=True)  24.2 us
    all_to_all x1, waiting for transfers between devices, shards(): lax.all_to_all(outgoing, 'reg', split_axis=0, concat_axis=0, tiled=True)  24.1 us
    dot_general x1, matrix products, shards(): jnp.einsum('rsej,rskj->rsek', adjoint.astype(jnp.bfloat16), pair_blocks,...  11.2 us
    dot_general x1, matrix products, shards(): jnp.einsum('rsek,rskj->rsej', exporter_rows, pair_blocks, preferred_eleme...  8.44 us
    all_to_all x1, starting transfers between devices, shards(): lax.all_to_all(outgoing, 'reg', split_axis=0, concat_axis=0, tiled=True)  7.41 us
    psum x1, waiting for transfers between devices, shards(): tau_grad = lax.psum(jnp.sum(adjoint, axis=2), 'ep')  6.41 us
    unnamed x15, local copies, waits for them, and re-layouts  5.08 us
    all_to_all x1, starting transfers between devices, shards(): lax.all_to_all(returning, 'reg', split_axis=0, concat_axis=0, tiled=True)  4.23 us
  transfers between devices with their start and end apart: 3, of which 3 were waited for; matrix products, arithmetic and copies ran while one was open for 6% of the time, Pallas kernels for 0%

commit v1 on v0

v1 whole, which is shorter than its diff:
```python
import functools

import jax
import jax.numpy as jnp
from jax import lax
from jax.experimental import pallas as pl
from jax.experimental.pallas import tpu as pltpu
from jax.sharding import PartitionSpec as P

F32 = jnp.float32
BF16 = jnp.bfloat16
CONTRACT_LAST = (((1,), (1,)), ((), ()))


def is_power_of_two(n):
    return n & (n - 1) == 0


def peer(i, distance, n):
    return i ^ distance if is_power_of_two(n) else (i + distance) % n


def offset_of(owner, me, n):
    return owner ^ me if is_power_of_two(n) else lax.rem(owner - me + n, n)


def radices(n):
    stages = []
    if n % 2 == 0 and n % 4 == 0 and (n.bit_length() % 2 == 0):
        stages.append(2)
        n //= 2
    while n % 4 == 0 and n > 1:
        stages.append(4)
        n //= 4
    if n > 1:
        stages.append(n)
    return stages


def from_peer(x, distance, axis, n):
    return lax.ppermute(x, axis, [(peer(i, distance, n), i) for i in range(n)])


def to_peer(x, distance, axis, n):
    return lax.ppermute(x, axis, [(i, peer(i, distance, n)) for i in range(n)])


def gather_by_distance(x, axis, n):
    stride = 1
    for radix in radices(n):
        parts = [x] + [from_peer(x, j * stride, axis, n) for j in range(1, radix)]
        x = jnp.concatenate(parts, axis=0)
        stride *= radix
    return x


def scatter_by_distance(x, axis, n):
    stride = n
    for radix in reversed(radices(n)):
        stride //= radix
        blocks = jnp.split(x, radix, axis=0)
        received = [to_peer(blocks[j].astype(BF16), j * stride, axis, n) for j in range(1, radix)]
        x = blocks[0].astype(F32)
        for block in received:
            x = x + block.astype(F32)
    return x


def importers_kernel(
    reg_count,
    me_ref,
    partners_ref,
    lengths_ref,
    costs_ref,
    blocks_ref,
    tau_ref,
    elasticity_ref,
    cotangent_ref,
    prices_ref,
    tau_grad_ref,
    partial_ref,
    weights_ref,
    total_ref,
):
    own, slots, sectors, _ = blocks_ref.shape
    episodes = costs_ref.shape[1]
    me = me_ref[0]
    elasticity = elasticity_ref[...]
    total_ref[...] = jnp.zeros_like(total_ref)
    for r in range(own):
        length = lengths_ref[me * own + r]
        top = jnp.full((episodes, sectors), -jnp.inf, F32)
        places = []
        for s in range(slots):
            partner = partners_ref[me * own + r, s]
            place = offset_of(partner // own, me, reg_count) * own + lax.rem(partner, own)
            places.append(place)
            landed = tau_ref[r, pl.ds(s, 1)] + jnp.dot(
                costs_ref[place], blocks_ref[r, s], preferred_element_type=F32
            )
            score = jnp.where(s < length, -elasticity * landed, -jnp.inf)
            weights_ref[s] = score
            top = jnp.maximum(top, score)
        norm = jnp.zeros((episodes, sectors), F32)
        for s in range(slots):
            weight = jnp.exp(weights_ref[s] - top)
            weights_ref[s] = weight
            norm = norm + weight
        prices_ref[r] = (-(top + jnp.log(norm)) / elasticity).astype(BF16)
        scale = cotangent_ref[r] / norm
        for s in range(slots):
            adjoint = scale * weights_ref[s]
            tau_grad_ref[r, pl.ds(s, 1)] = jnp.sum(adjoint, axis=0, keepdims=True)
            total_ref[places[s]] += lax.dot_general(
                adjoint.astype(BF16), blocks_ref[r, s], CONTRACT_LAST, preferred_element_type=F32
            )
    partial_ref[...] = total_ref[...].astype(BF16)


def shards(
    log_prices,
    log_wages,
    labor_share,
    io_coeffs,
    pair_blocks,
    log_tau,
    elasticity,
    partners,
    list_lengths,
    price_cotangent,
):
    own, episodes, sectors = log_prices.shape
    slots = pair_blocks.shape[1]
    regions = partners.shape[0]
    reg_count = lax.axis_size("reg")
    ep_count = lax.axis_size("ep")
    unit_cost = (
        labor_share[:, None, :] * log_wages[:, :, None]
        + jnp.einsum("iek,ikj->iej", log_prices, io_coeffs, preferred_element_type=F32)
    ).astype(BF16)
    costs = gather_by_distance(unit_cost, "reg", reg_count)
    vmem = pl.BlockSpec(memory_space=pltpu.VMEM)
    smem = pl.BlockSpec(memory_space=pltpu.SMEM)
    new_prices, tau_part, partial = pl.pallas_call(
        functools.partial(importers_kernel, reg_count),
        out_shape=(
            jax.ShapeDtypeStruct((own, episodes, sectors), BF16),
            jax.ShapeDtypeStruct((own, slots, sectors), F32),
            jax.ShapeDtypeStruct((regions, episodes, sectors), BF16),
        ),
        in_specs=[smem, smem, smem, vmem, vmem, vmem, vmem, vmem],
        out_specs=(vmem, vmem, vmem),
        scratch_shapes=[
            pltpu.VMEM((slots, episodes, sectors), F32),
            pltpu.VMEM((regions, episodes, sectors), F32),
        ],
        compiler_params=pltpu.CompilerParams(vmem_limit_bytes=16 << 20),
        name="importers",
    )(
        lax.axis_index("reg").reshape(1),
        partners,
        list_lengths,
        costs,
        pltpu.with_memory_space_constraint(pair_blocks, pltpu.VMEM),
        log_tau,
        elasticity.reshape(1, -1),
        price_cotangent,
    )
    tau_grad = tau_part
    distance = 1
    while distance < ep_count:
        tau_grad = tau_grad + to_peer(tau_grad, distance, "ep", ep_count)
        distance *= 2
    cost_adjoint = scatter_by_distance(partial, "reg", reg_count)
    price_grad = jnp.einsum(
        "iej,ikj->iek", cost_adjoint.astype(BF16), io_coeffs, preferred_element_type=F32
    )
    wage_grad = jnp.sum(cost_adjoint * labor_share[:, None, :], axis=2)
    return new_prices, price_grad, wage_grad, tau_grad


def solution(mesh):
    return jax.shard_map(
        shards,
        mesh=mesh,
        in_specs=(
            P("reg", "ep", None),
            P("reg", "ep"),
            P("reg", None),
            P("reg", None, None),
            P("reg", None, None, None),
            P("reg", None, None),
            P(),
            P(),
            P(),
            P("reg", "ep", None),
        ),
        out_specs=(
            P("reg", "ep", None),
            P("reg", "ep", None),
            P("reg", "ep"),
            P("reg", None, None),
        ),
        check_vma=False,
    )
```

time: 124 us -> 51.7 us (0.42)
  waiting for transfers between devices: 54.7 us -> 13.5 us
  matrix products: 22.3 us -> 1.84 us
  between operations: 14.2 us -> 0.71 us
  Pallas kernels: 0 us -> 8.73 us
  other arithmetic: 7.61 us -> 1.41 us
  starting transfers between devices: 11.7 us -> 14.5 us
  local copies, waits for them, and re-layouts: 12.9 us -> 10.6 us
    all_to_all x2 -> x0, waiting for transfers between devices: 48.3 us -> none  [the longest x1 24.2 us: shards(): lax.all_to_all(returning, 'reg', split_axis=0, concat_axis=0, tiled=True)]
    dot_general x5 -> x1, matrix products: 21.4 us -> 0.88 us  [shards(): jnp.einsum('iej,ikj->iek', cost_adjoint.astype(BF16), io_coeffs, preferre...]
    ppermute x0 -> x10, starting transfers between devices: none -> 14.5 us  [the longest x4 7.82 us: from_peer(): return lax.ppermute(x, axis, [(peer(i, distance, n), i) for i in range(n)])]
    ppermute x0 -> x10, waiting for transfers between devices: none -> 13.5 us  [the longest x6 7.08 us: to_peer(): return lax.ppermute(x, axis, [(i, peer(i, distance, n)) for i in range(n)])]
    all_to_all x2 -> x0, starting transfers between devices: 11.6 us -> none  [the longest x1 7.41 us: shards(): lax.all_to_all(outgoing, 'reg', split_axis=0, concat_axis=0, tiled=True)]
    pallas_call x0 -> x1, Pallas kernels: none -> 8.73 us  [shards(): pl.pallas_call(functools.partial(importers_kernel, reg_count), out_shape=...]
    psum x1 -> x0, waiting for transfers between devices: 6.41 us -> none  [shards(): tau_grad = lax.psum(jnp.sum(adjoint, axis=2), 'ep')]
    unnamed x15 -> x19, local copies, waits for them, and re-layouts: 5.08 us -> 10.6 us
  transfers between devices with their start and end apart: 3 -> 10, of which waited for: 3 -> 8; matrix products, arithmetic and copies ran while one was open for 6% -> 3% of each run, Pallas kernels for 0% -> 0%
where the time goes in v1:
time: 51.7 us; the launch traced here: 51.4 us
  starting transfers between devices  14.5 us (28%)
  waiting for transfers between devices  13.5 us (26%)
  local copies, waits for them, and re-layouts  10.6 us (21%)
  Pallas kernels  8.73 us (17%)
  matrix products  1.84 us (4%)
  other arithmetic  1.41 us (3%)
  between operations  0.71 us (1%)
    unnamed x19, local copies, waits for them, and re-layouts  10.6 us
    pallas_call x1, Pallas kernels, shards(): pl.pallas_call(functools.partial(importers_kernel, reg_count), out_shape=...  8.73 us
    ppermute x4, starting transfers between devices, from_peer(): return lax.ppermute(x, axis, [(peer(i, distance, n), i) for i in range(n)])  7.82 us
    ppermute x6, waiting for transfers between devices, to_peer(): return lax.ppermute(x, axis, [(i, peer(i, distance, n)) for i in range(n)])  7.08 us
    ppermute x6, starting transfers between devices, to_peer(): return lax.ppermute(x, axis, [(i, peer(i, distance, n)) for i in range(n)])  6.71 us
    ppermute x4, waiting for transfers between devices, from_peer(): return lax.ppermute(x, axis, [(peer(i, distance, n), i) for i in range(n)])  6.43 us
  transfers between devices with their start and end apart: 10, of which 8 were waited for; matrix products, arithmetic and copies ran while one was open for 3% of the time, Pallas kernels for 0%

profile of v1, /device:TPU:0, one launch (start us, length us, event | category | flops | bytes accessed | tf_op | source)
XLA Modules:
  0.0 51.4 jit_solution(16918299937343224316)
XLA Ops:
  0.6 0.0 copy-start
  0.6 0.0 copy-start.7
  0.7 1.0 %copy-done = bf16[4,256,256]{2,1,0:T(8,128)(2,1)S(1)} copy-done((bf16[4,256,256]{2,1,0:T(8,128)(2,1)S(1)}, bf16[4,256,256]{2,1,0:T(8,128)(2,1)}, u32[]{:S(2)}) %copy-start) | copy-done | bytes 524312
  1.7 1.0 %constant_dynamic-update-slice_fusion.4 = (bf16[32,16,256]{2,1,0:T(8,128)(2,1)S(1)}, bf16[4,16,256]{2,1,0:T(8,128)(2,1)S(1)}) fusion(bf16[4,16,256]{2,1,0:T(8,128)(2,1)} %param.10, bf16[4,256,256]{2,1,0:T(8,128)(2,1)S(1)} %copy-done, f32[4,16]{1,0:T(4,128)} %param.11, f32[4,256]{1,0:T(4,128)} %param.12), kind=kOutput, calls=%fused_computation.13 | convolution fusion | flops 8437759 | bytes 626944 | tf_op jit(solution)/shard_map/iek,ikj->iej/dot_general | solution.py:139
  2.6 3.0 %collective-permute-start = (bf16[4,16,256]{2,1,0:T(8,128)(2,1)S(1)}, bf16[4,16,256]{2,1,0:T(8,128)(2,1)S(1)}, u32[]{:S(2)}, u32[]{:S(2)}) collective-permute-start(bf16[4,16,256]{2,1,0:T(8,128)(2,1)S(1)} %get-tuple-element.14), channel_id=1, source_target_pairs={{4,0},{0,4},{12,8},{8,12},{20,16},{16,20},{28,24},{24,28},{5,1},{1... | collective-permute-start | bytes 98312 | tf_op jit(solution)/shard_map/ppermute | solution.py:41
  5.6 1.9 %collective-permute-done = bf16[4,16,256]{2,1,0:T(8,128)(2,1)S(1)} collective-permute-done((bf16[4,16,256]{2,1,0:T(8,128)(2,1)S(1)}, bf16[4,16,256]{2,1,0:T(8,128)(2,1)S(1)}, u32[]{:S(2)}, u32[]{:S(2)}) %collective-permute-start) | collective-permute-done | bytes 32800 | tf_op jit(solution)/shard_map/ppermute | solution.py:41
  7.6 4.2 %collective-permute-start.3 = (bf16[8,16,256]{2,1,0:T(8,128)(2,1)S(1)}, bf16[8,16,256]{2,1,0:T(8,128)(2,1)S(1)}, u32[]{:S(2)}, u32[]{:S(2)}) collective-permute-start(bf16[8,16,256]{2,1,0:T(8,128)(2,1)S(1)} %pad_maximum_fusion), channel_id=1, source_target_pairs={{24,0},{28,4},{16,8},{20,12},{8,16},{12,20},{0,24},{4,28},{25,1},{... | collective-permute-start | bytes 196616 | tf_op jit(solution)/shard_map/ppermute | solution.py:41
  11.7 0.0 collective-permute-start.2
  11.7 0.6 %collective-permute-start.1 = (bf16[8,16,256]{2,1,0:T(8,128)(2,1)S(1)}, bf16[8,16,256]{2,1,0:T(8,128)(2,1)S(1)}, u32[]{:S(2)}, u32[]{:S(2)}) collective-permute-start(bf16[8,16,256]{2,1,0:T(8,128)(2,1)S(1)} %pad_maximum_fusion), channel_id=1, source_target_pairs={{8,0},{12,4},{0,8},{4,12},{24,16},{28,20},{16,24},{20,28},{9,1},{1... | collective-permute-start | bytes 196616 | tf_op jit(solution)/shard_map/ppermute | solution.py:41
  12.4 3.7 %collective-permute-done.1 = bf16[8,16,256]{2,1,0:T(8,128)(2,1)S(1)} collective-permute-done((bf16[8,16,256]{2,1,0:T(8,128)(2,1)S(1)}, bf16[8,16,256]{2,1,0:T(8,128)(2,1)S(1)}, u32[]{:S(2)}, u32[]{:S(2)}) %collective-permute-start.1) | collective-permute-done | bytes 65568 | tf_op jit(solution)/shard_map/ppermute | solution.py:41
  16.1 0.8 %collective-permute-done.2 = bf16[8,16,256]{2,1,0:T(8,128)(2,1)S(1)} collective-permute-done((bf16[8,16,256]{2,1,0:T(8,128)(2,1)S(1)}, bf16[8,16,256]{2,1,0:T(8,128)(2,1)S(1)}, u32[]{:S(2)}, u32[]{:S(2)}) %collective-permute-start.2) | collective-permute-done | bytes 65568 | tf_op jit(solution)/shard_map/ppermute | solution.py:41
  16.9 0.0 collective-permute-done.3
  16.9 0.0 copy-start.1
  16.9 5.8 %copy-done.1 = bf16[4,32,256,256]{3,2,1,0:T(8,128)(2,1)S(1)} copy-done((bf16[4,32,256,256]{3,2,1,0:T(8,128)(2,1)S(1)}, bf16[4,32,256,256]{3,2,1,0:T(8,128)(2,1)}, u32[]{:S(2)}) %copy-start.1) | copy-done | bytes 16777240
  22.7 0.0 copy-start.2
  22.7 0.9 %copy-done.2 = f32[4,32,256]{2,1,0:T(8,128)S(1)} copy-done((f32[4,32,256]{2,1,0:T(8,128)S(1)}, f32[4,32,256]{2,1,0:T(8,128)}, u32[]{:S(2)}) %copy-start.2) | copy-done | bytes 131096
  23.6 0.0 copy-start.3
  23.6 0.8 %copy-done.3 = f32[4,16,256]{2,1,0:T(8,128)S(1)} copy-done((f32[4,16,256]{2,1,0:T(8,128)S(1)}, f32[4,16,256]{2,1,0:T(8,128)}, u32[]{:S(2)}) %copy-start.3) | copy-done | bytes 65560
  24.5 0.0 copy-start.4
  24.5 0.7 %copy-done.4 = s32[32,32]{1,0:T(8,128)S(1)} copy-done((s32[32,32]{1,0:T(8,128)S(1)}, s32[32,32]{1,0:T(8,128)}, u32[]{:S(2)}) %copy-start.4) | copy-done | bytes 4120
  25.2 0.0 copy-start.5
  25.2 0.7 %copy-done.5 = f32[256]{0:T(256)S(1)} copy-done((f32[256]{0:T(256)S(1)}, f32[256]{0:T(256)}, u32[]{:S(2)}) %copy-start.5) | copy-done | bytes 1048
  25.9 0.0 copy-start.6
  25.9 0.7 %copy-done.6 = s32[32]{0:T(128)S(1)} copy-done((s32[32]{0:T(128)S(1)}, s32[32]{0:T(128)}, u32[]{:S(2)}) %copy-start.6) | copy-done | bytes 152
  26.5 8.7 %importers.1 = (bf16[4,16,256]{2,1,0:T(8,128)(2,1)}, f32[4,32,256]{2,1,0:T(8,128)S(1)}, bf16[32,16,256]{2,1,0:T(8,128)(2,1)S(1)}) custom-call(s32[1]{0:T(128)} %bitcast.me_ref, s32[32,32]{1,0:T(8,128)S(1)} %copy-done.4, s32[32]{0:T(128)S(1)} %copy-done.6, bf16[32,16,256]{2,1,0:T(8,128)(2,1)S(1)} %constant_dynamic-update-slice_fusion.costs_ref, ...), custom_call_target="tpu_custom_call" | custom-call | tf_op jit(solution)/shard_map/importers/pallas_call | solution.py:144
  35.3 0.6 %collective-permute-start.4 = (bf16[8,16,256]{2,1,0:T(8,128)(2,1)S(1)}, bf16[8,16,256]{2,1,0:T(8,128)(2,1)S(1)}, u32[]{:S(2)}, u32[]{:S(2)}) collective-permute-start(bf16[8,16,256]{2,1,0:T(8,128)(2,1)S(1)} %get-tuple-element.10), channel_id=1, source_target_pairs={{0,8},{4,12},{8,0},{12,4},{16,24},{20,28},{24,16},{28,20},{1,9},{5... | collective-permute-start | bytes 196616 | tf_op jit(solution)/shard_map/ppermute | solution.py:45
  35.9 2.9 %collective-permute-start.6 = (bf16[8,16,256]{2,1,0:T(8,128)(2,1)S(1)}, bf16[8,16,256]{2,1,0:T(8,128)(2,1)S(1)}, u32[]{:S(2)}, u32[]{:S(2)}) collective-permute-start(bf16[8,16,256]{2,1,0:T(8,128)(2,1)S(1)} %get-tuple-element.11), channel_id=1, source_target_pairs={{0,24},{4,28},{8,16},{12,20},{16,8},{20,12},{24,0},{28,4},{1,25},{... | collective-permute-start | bytes 196616 | tf_op jit(solution)/shard_map/ppermute | solution.py:45
  38.8 0.0 collective-permute-start.5
  38.8 0.0 collective-permute-start.8
  38.8 1.1 %collective-permute-done.4 = bf16[8,16,256]{2,1,0:T(8,128)(2,1)S(1)} collective-permute-done((bf16[8,16,256]{2,1,0:T(8,128)(2,1)S(1)}, bf16[8,16,256]{2,1,0:T(8,128)(2,1)S(1)}, u32[]{:S(2)}, u32[]{:S(2)}) %collective-permute-start.4) | collective-permute-done | bytes 65568 | tf_op jit(solution)/shard_map/ppermute | solution.py:45
  39.9 2.0 %collective-permute-done.6 = bf16[8,16,256]{2,1,0:T(8,128)(2,1)S(1)} collective-permute-done((bf16[8,16,256]{2,1,0:T(8,128)(2,1)S(1)}, bf16[8,16,256]{2,1,0:T(8,128)(2,1)S(1)}, u32[]{:S(2)}, u32[]{:S(2)}) %collective-permute-start.6) | collective-permute-done | bytes 65568 | tf_op jit(solution)/shard_map/ppermute | solution.py:45
  42.0 2.0 %collective-permute-done.5 = bf16[8,16,256]{2,1,0:T(8,128)(2,1)S(1)} collective-permute-done((bf16[8,16,256]{2,1,0:T(8,128)(2,1)S(1)}, bf16[8,16,256]{2,1,0:T(8,128)(2,1)S(1)}, u32[]{:S(2)}, u32[]{:S(2)}) %collective-permute-start.5) | collective-permute-done | bytes 65568 | tf_op jit(solution)/shard_map/ppermute | solution.py:45
  44.0 1.6 %collective-permute-start.7 = (bf16[4,16,256]{2,1,0:T(8,128)(2,1)S(1)}, bf16[4,16,256]{2,1,0:T(8,128)(2,1)S(1)}, u32[]{:S(2)}, u32[]{:S(2)}) collective-permute-start(bf16[4,16,256]{2,1,0:T(8,128)(2,1)S(1)} %split.35), channel_id=1, source_target_pairs={{0,4},{4,0},{8,12},{12,8},{16,20},{20,16},{24,28},{28,24},{1,5},{5... | collective-permute-start | bytes 98312 | tf_op jit(solution)/shard_map/ppermute | solution.py:45
  45.6 0.0 collective-permute-done.8
  45.6 1.6 %collective-permute-start.9 = (f32[4,32,256]{2,1,0:T(8,128)S(1)}, f32[4,32,256]{2,1,0:T(8,128)S(1)}, u32[]{:S(2)}, u32[]{:S(2)}) collective-permute-start(f32[4,32,256]{2,1,0:T(8,128)S(1)} %add.26), channel_id=1, source_target_pairs={{0,2},{1,3},{2,0},{3,1},{4,6},{5,7},{6,4},{7,5},{8,10},{9,11},{10,... | collective-permute-start | bytes 393224 | tf_op jit(solution)/shard_map/ppermute | solution.py:45
  47.2 0.8 %collective-permute-done.7 = bf16[4,16,256]{2,1,0:T(8,128)(2,1)S(1)} collective-permute-done((bf16[4,16,256]{2,1,0:T(8,128)(2,1)S(1)}, bf16[4,16,256]{2,1,0:T(8,128)(2,1)S(1)}, u32[]{:S(2)}, u32[]{:S(2)}) %collective-permute-start.7) | collective-permute-done | bytes 32800 | tf_op jit(solution)/shard_map/ppermute | solution.py:45
  48.0 0.9 %fusion.2 = f32[4,16,256]{2,1,0:T(8,128)} fusion(bf16[4,256,256]{2,1,0:T(8,128)(2,1)S(1)} %copy-done, bf16[4,16,256]{2,1,0:T(8,128)(2,1)S(1)} %collective-permute-done.7, f32[8,16,256]{2,1,0:T(8,128)S(1)} %convert_add_fusion), kind=kOutput, calls=%fused_computation.8 | convolution fusion | flops 8437760 | bytes 688128 | tf_op jit(solution)/shard_map/iej,ikj->iek/dot_general | solution.py:175
  48.9 0.0 copy-done.7
  48.9 0.7 %multiply_reduce_fusion = f32[4,16]{1,0:T(4,128)} fusion(bf16[4,16,256]{2,1,0:T(8,128)(2,1)S(1)} %collective-permute-done.7, f32[8,16,256]{2,1,0:T(8,128)S(1)} %convert_add_fusion, f32[4,256]{1,0:T(4,128)S(1)} %copy-done.7), kind=kLoop, calls=%fused_computation.6 | loop fusion | flops 65472 | bytes 102656 | tf_op jit(solution)/shard_map/reduce_sum | solution.py:178
  49.6 1.1 %collective-permute-done.9 = f32[4,32,256]{2,1,0:T(8,128)S(1)} collective-permute-done((f32[4,32,256]{2,1,0:T(8,128)S(1)}, f32[4,32,256]{2,1,0:T(8,128)S(1)}, u32[]{:S(2)}, u32[]{:S(2)}) %collective-permute-start.9) | collective-permute-done | bytes 131104 | tf_op jit(solution)/shard_map/ppermute | solution.py:45
  50.7 0.7 %add.27 = f32[4,32,256]{2,1,0:T(8,128)} add(f32[4,32,256]{2,1,0:T(8,128)S(1)} %add.26, f32[4,32,256]{2,1,0:T(8,128)S(1)} %collective-permute-done.9) | non-fusion elementwise | flops 32768 | bytes 393216 | tf_op jit(solution)/shard_map/add | solution.py:172
  (9 shorter events, 0.1 us)
Async XLA Ops:
  0.6 1.0 %copy-start = (bf16[4,256,256]{2,1,0:T(8,128)(2,1)S(1)}, bf16[4,256,256]{2,1,0:T(8,128)(2,1)}, u32[]{:S(2)}) copy-start(bf16[4,256,256]{2,1,0:T(8,128)(2,1)} %param.13) | copy-start | bytes 1572868
  0.6 48.3 %copy-start.7 = (f32[4,256]{1,0:T(4,128)S(1)}, f32[4,256]{1,0:T(4,128)}, u32[]{:S(2)}) copy-start(f32[4,256]{1,0:T(4,128)} %param.12) | copy-start | bytes 12292
  2.6 4.9 %collective-permute-start = (bf16[4,16,256]{2,1,0:T(8,128)(2,1)S(1)}, bf16[4,16,256]{2,1,0:T(8,128)(2,1)S(1)}, u32[]{:S(2)}, u32[]{:S(2)}) collective-permute-start(bf16[4,16,256]{2,1,0:T(8,128)(2,1)S(1)} %get-tuple-element.14), channel_id=1, source_target_pairs={{4,0},{0,4},{12,8},{8,12},{20,16},{16,20},{28,24},{24,28},{5,1},{1... | collective-permute-start | bytes 98312 | tf_op jit(solution)/shard_map/ppermute | solution.py:41
  7.6 9.4 %collective-permute-start.3 = (bf16[8,16,256]{2,1,0:T(8,128)(2,1)S(1)}, bf16[8,16,256]{2,1,0:T(8,128)(2,1)S(1)}, u32[]{:S(2)}, u32[]{:S(2)}) collective-permute-start(bf16[8,16,256]{2,1,0:T(8,128)(2,1)S(1)} %pad_maximum_fusion), channel_id=1, source_target_pairs={{24,0},{28,4},{16,8},{20,12},{8,16},{12,20},{0,24},{4,28},{25,1},{... | collective-permute-start | bytes 196616 | tf_op jit(solution)/shard_map/ppermute | solution.py:41
  11.7 5.2 %collective-permute-start.2 = (bf16[8,16,256]{2,1,0:T(8,128)(2,1)S(1)}, bf16[8,16,256]{2,1,0:T(8,128)(2,1)S(1)}, u32[]{:S(2)}, u32[]{:S(2)}) collective-permute-start(bf16[8,16,256]{2,1,0:T(8,128)(2,1)S(1)} %pad_maximum_fusion), channel_id=1, source_target_pairs={{16,0},{20,4},{24,8},{28,12},{0,16},{4,20},{8,24},{12,28},{17,1},{... | collective-permute-start | bytes 196616 | tf_op jit(solution)/shard_map/ppermute | solution.py:41
  11.7 4.4 %collective-permute-start.1 = (bf16[8,16,256]{2,1,0:T(8,128)(2,1)S(1)}, bf16[8,16,256]{2,1,0:T(8,128)(2,1)S(1)}, u32[]{:S(2)}, u32[]{:S(2)}) collective-permute-start(bf16[8,16,256]{2,1,0:T(8,128)(2,1)S(1)} %pad_maximum_fusion), channel_id=1, source_target_pairs={{8,0},{12,4},{0,8},{4,12},{24,16},{28,20},{16,24},{20,28},{9,1},{1... | collective-permute-start | bytes 196616 | tf_op jit(solution)/shard_map/ppermute | solution.py:41
  16.9 5.8 %copy-start.1 = (bf16[4,32,256,256]{3,2,1,0:T(8,128)(2,1)S(1)}, bf16[4,32,256,256]{3,2,1,0:T(8,128)(2,1)}, u32[]{:S(2)}) copy-start(bf16[4,32,256,256]{3,2,1,0:T(8,128)(2,1)} %blocks_ref.1) | copy-start | bytes 50331652
  22.7 0.9 %copy-start.2 = (f32[4,32,256]{2,1,0:T(8,128)S(1)}, f32[4,32,256]{2,1,0:T(8,128)}, u32[]{:S(2)}) copy-start(f32[4,32,256]{2,1,0:T(8,128)} %tau_ref.1) | copy-start | bytes 393220
  23.6 0.8 %copy-start.3 = (f32[4,16,256]{2,1,0:T(8,128)S(1)}, f32[4,16,256]{2,1,0:T(8,128)}, u32[]{:S(2)}) copy-start(f32[4,16,256]{2,1,0:T(8,128)} %cotangent_ref.1) | copy-start | bytes 196612
  24.5 0.7 %copy-start.4 = (s32[32,32]{1,0:T(8,128)S(1)}, s32[32,32]{1,0:T(8,128)}, u32[]{:S(2)}) copy-start(s32[32,32]{1,0:T(8,128)} %partners_ref.1) | copy-start | bytes 12292
  25.2 0.7 %copy-start.5 = (f32[256]{0:T(256)S(1)}, f32[256]{0:T(256)}, u32[]{:S(2)}) copy-start(f32[256]{0:T(256)} %param.16) | copy-start | bytes 3076
  25.9 0.7 %copy-start.6 = (s32[32]{0:T(128)S(1)}, s32[32]{0:T(128)}, u32[]{:S(2)}) copy-start(s32[32]{0:T(128)} %lengths_ref.1) | copy-start | bytes 388
  35.3 4.7 %collective-permute-start.4 = (bf16[8,16,256]{2,1,0:T(8,128)(2,1)S(1)}, bf16[8,16,256]{2,1,0:T(8,128)(2,1)S(1)}, u32[]{:S(2)}, u32[]{:S(2)}) collective-permute-start(bf16[8,16,256]{2,1,0:T(8,128)(2,1)S(1)} %get-tuple-element.10), channel_id=1, source_target_pairs={{0,8},{4,12},{8,0},{12,4},{16,24},{20,28},{24,16},{28,20},{1,9},{5... | collective-permute-start | bytes 196616 | tf_op jit(solution)/shard_map/ppermute | solution.py:45
  35.9 6.1 %collective-permute-start.6 = (bf16[8,16,256]{2,1,0:T(8,128)(2,1)S(1)}, bf16[8,16,256]{2,1,0:T(8,128)(2,1)S(1)}, u32[]{:S(2)}, u32[]{:S(2)}) collective-permute-start(bf16[8,16,256]{2,1,0:T(8,128)(2,1)S(1)} %get-tuple-element.11), channel_id=1, source_target_pairs={{0,24},{4,28},{8,16},{12,20},{16,8},{20,12},{24,0},{28,4},{1,25},{... | collective-permute-start | bytes 196616 | tf_op jit(solution)/shard_map/ppermute | solution.py:45
  38.8 5.2 %collective-permute-start.5 = (bf16[8,16,256]{2,1,0:T(8,128)(2,1)S(1)}, bf16[8,16,256]{2,1,0:T(8,128)(2,1)S(1)}, u32[]{:S(2)}, u32[]{:S(2)}) collective-permute-start(bf16[8,16,256]{2,1,0:T(8,128)(2,1)S(1)} %get-tuple-element.12), channel_id=1, source_target_pairs={{0,16},{4,20},{8,24},{12,28},{16,0},{20,4},{24,8},{28,12},{1,17},{... | collective-permute-start | bytes 196616 | tf_op jit(solution)/shard_map/ppermute | solution.py:45
  38.8 6.8 %collective-permute-start.8 = (f32[4,32,256]{2,1,0:T(8,128)S(1)}, f32[4,32,256]{2,1,0:T(8,128)S(1)}, u32[]{:S(2)}, u32[]{:S(2)}) collective-permute-start(f32[4,32,256]{2,1,0:T(8,128)S(1)} %get-tuple-element.9), channel_id=1, source_target_pairs={{0,1},{1,0},{2,3},{3,2},{4,5},{5,4},{6,7},{7,6},{8,9},{9,8},{10,11... | collective-permute-start | bytes 393224 | tf_op jit(solution)/shard_map/ppermute | solution.py:45
  44.0 4.0 %collective-permute-start.7 = (bf16[4,16,256]{2,1,0:T(8,128)(2,1)S(1)}, bf16[4,16,256]{2,1,0:T(8,128)(2,1)S(1)}, u32[]{:S(2)}, u32[]{:S(2)}) collective-permute-start(bf16[4,16,256]{2,1,0:T(8,128)(2,1)S(1)} %split.35), channel_id=1, source_target_pairs={{0,4},{4,0},{8,12},{12,8},{16,20},{20,16},{24,28},{28,24},{1,5},{5... | collective-permute-start | bytes 98312 | tf_op jit(solution)/shard_map/ppermute | solution.py:45
  45.6 5.0 %collective-permute-start.9 = (f32[4,32,256]{2,1,0:T(8,128)S(1)}, f32[4,32,256]{2,1,0:T(8,128)S(1)}, u32[]{:S(2)}, u32[]{:S(2)}) collective-permute-start(f32[4,32,256]{2,1,0:T(8,128)S(1)} %add.26), channel_id=1, source_target_pairs={{0,2},{1,3},{2,0},{3,1},{4,6},{5,7},{6,4},{7,5},{8,10},{9,11},{10,... | collective-permute-start | bytes 393224 | tf_op jit(solution)/shard_map/ppermute | solution.py:45

commit v2 on v1

v2 whole, which is shorter than its diff:
```python
import functools

import jax
import jax.numpy as jnp
from jax import lax
from jax.experimental import pallas as pl
from jax.experimental.pallas import tpu as pltpu
from jax.sharding import PartitionSpec as P

F32 = jnp.float32
BF16 = jnp.bfloat16
CONTRACT_LAST = (((1,), (1,)), ((), ()))
LOWEST = -1e30
VMEM = pl.BlockSpec(memory_space=pltpu.VMEM)
SMEM = pl.BlockSpec(memory_space=pltpu.SMEM)
HBM = pl.BlockSpec(memory_space=pltpu.HBM)


def is_power_of_two(n):
    return n & (n - 1) == 0


def peer(i, distance, n):
    return i ^ distance if is_power_of_two(n) else (i + distance) % n


def distance_of(owner, me, n):
    return owner ^ me if is_power_of_two(n) else lax.rem(owner - me + n, n)


def radices(n):
    stages = []
    if n.bit_length() % 2 == 0 and is_power_of_two(n):
        stages.append(2)
        n //= 2
    while n % 4 == 0:
        stages.append(4)
        n //= 4
    if n > 1 or not stages:
        stages.append(n)
    return stages


def from_peer(x, distance, axis, n):
    return lax.ppermute(x, axis, [(peer(i, distance, n), i) for i in range(n)])


def to_peer(x, distance, axis, n):
    return lax.ppermute(x, axis, [(i, peer(i, distance, n)) for i in range(n)])


def shape(dims, dtype):
    return jax.ShapeDtypeStruct(dims, dtype)


def params(mebibytes):
    return pltpu.CompilerParams(vmem_limit_bytes=mebibytes << 20)


def effort(size):
    return pl.CostEstimate(flops=0, bytes_accessed=size, transcendentals=0)


def in_hbm(x):
    return pltpu.with_memory_space_constraint(x, pltpu.HBM)


class Entries:
    def __init__(self, own, slots, reg_count):
        self.own, self.slots, self.reg_count = own, slots, reg_count
        self.capacity = -(-own * slots // reg_count)
        self.count = self.capacity * reg_count
        self.stride = self.count + 1

    def slot(self, table, entry):
        return table[entry]

    def importer(self, table, entry):
        return table[self.stride + entry]

    def place(self, table, entry):
        return table[2 * self.stride + entry]


def load_kernel(
    entries, me_ref, cost_ref, blocks, tau, cotangent, elasticity, partners, lengths,
    held_ref, tau_ref, cotangent_ref, elasticity_ref, cost_copy_ref, table_ref,
    partners_ref, lengths_ref, found_ref, sems,
):
    own, slots, n, capacity = entries.own, entries.slots, entries.reg_count, entries.capacity
    first = held_ref.shape[0] // 2
    copies = [
        pltpu.make_async_copy(source, target, sems.at[i])
        for i, (source, target) in enumerate(
            (
                (partners, partners_ref),
                (lengths, lengths_ref),
                (tau, tau_ref),
                (cotangent, cotangent_ref),
                (elasticity, elasticity_ref),
                (blocks.at[pl.ds(0, first)], held_ref.at[pl.ds(0, first)]),
            )
        )
    ]
    for copy in copies:
        copy.start()
    cost_copy_ref[...] = cost_ref[...]
    for entry in range(entries.stride):
        table_ref[entry] = 0
        table_ref[entries.stride + entry] = own
        table_ref[2 * entries.stride + entry] = 0
    for distance in range(n):
        found_ref[distance] = 0
    copies[0].wait()
    copies[1].wait()
    me = me_ref[0]
    for r in range(own):
        length = lengths_ref[me * own + r]
        for s in range(slots):
            partner = partners_ref[me * own + r, s]
            distance = distance_of(lax.div(partner, own), me, n)
            found = found_ref[distance]
            entry = jnp.where(s < length, distance * capacity + found, entries.count)
            entry = jnp.minimum(entry, entries.count)
            table_ref[entry] = r * slots + s
            table_ref[entries.stride + entry] = r
            table_ref[2 * entries.stride + entry] = lax.rem(partner, own)
            found_ref[distance] = found + (s < length).astype(jnp.int32)
    for copy in copies[2:]:
        copy.wait()


def score_entries(entries, first, table_ref, costs, held_ref, tau_ref, elasticity_ref, weights_ref, top_ref, norm_ref):
    own, capacity = entries.own, entries.capacity
    scale = -elasticity_ref[...]
    top_ref[...] = jnp.full(top_ref.shape, LOWEST, F32)
    norm_ref[...] = jnp.zeros(norm_ref.shape, F32)
    rows = [(ref, block) for ref in costs for block in range(ref.shape[0] // own)]
    for i in range(weights_ref.shape[0]):
        entry = first * capacity + i
        ref, block = rows[i // capacity]
        slot = entries.slot(table_ref, entry)
        importer = entries.importer(table_ref, entry)
        cost = ref[block * own + entries.place(table_ref, entry)]
        landed = jnp.dot(cost, held_ref[slot], preferred_element_type=F32) + tau_ref[pl.ds(slot, 1)]
        score = scale * landed
        weights_ref[i] = score
        top_ref[importer] = jnp.maximum(top_ref[importer], score)
    for i in range(weights_ref.shape[0]):
        importer = entries.importer(table_ref, first * capacity + i)
        weight = jnp.exp(weights_ref[i] - top_ref[importer])
        weights_ref[i] = weight
        norm_ref[importer] += weight


def near_kernel(entries, n_costs, *refs):
    table_ref, blocks, _, tau_ref, elasticity_ref = refs[:5]
    costs = refs[5 : 5 + n_costs]
    held_ref, weights_ref, top_ref, norm_ref, sem = refs[5 + n_costs :]
    first = held_ref.shape[0] // 2
    rest = held_ref.shape[0] - first
    copy = pltpu.make_async_copy(blocks.at[pl.ds(first, rest)], held_ref.at[pl.ds(first, rest)], sem)
    copy.start()
    copy.wait()
    score_entries(entries, 0, table_ref, costs, held_ref, tau_ref, elasticity_ref, weights_ref, top_ref, norm_ref)


def far_kernel(entries, first, table_ref, held_ref, tau_ref, elasticity_ref, cost_ref, weights_ref, top_ref, norm_ref):
    score_entries(entries, first, table_ref, [cost_ref], held_ref, tau_ref, elasticity_ref, weights_ref, top_ref, norm_ref)


def push_entries(entries, first, table_ref, adjoint_of, held_ref, total_ref):
    total_ref[...] = jnp.zeros(total_ref.shape, F32)
    own, capacity = entries.own, entries.capacity
    for i in range(total_ref.shape[0] // own * capacity):
        entry = first * capacity + i
        place = i // capacity * own + entries.place(table_ref, entry)
        total_ref[place] += lax.dot_general(
            adjoint_of(entry),
            held_ref[entries.slot(table_ref, entry)],
            CONTRACT_LAST,
            preferred_element_type=F32,
        )


def adjoint_kernel(entries, firsts, *refs):
    n = len(firsts)
    table_ref, held_ref, cotangent_ref = refs[:3]
    weights, tops, norms = refs[3 : 3 + n], refs[3 + n : 3 + 2 * n], refs[3 + 2 * n : 3 + 3 * n]
    adjoint_ref, tau_grad_ref, logsum_ref, partial_ref, factor_ref, total_ref = refs[3 + 3 * n :]
    own, capacity = entries.own, entries.capacity
    tau_grad_ref[...] = jnp.zeros(tau_grad_ref.shape, F32)
    for r in range(own):
        top = functools.reduce(jnp.maximum, [ref[r] for ref in tops])
        shrink = [jnp.exp(ref[r] - top) for ref in tops]
        norm = sum(ref[r] * factor for ref, factor in zip(norms, shrink))
        logsum_ref[r] = top + jnp.log(norm)
        scale = cotangent_ref[r] / norm
        for k in range(n):
            factor_ref[k, r] = scale * shrink[k]
    for k in range(n):
        factor_ref[k, own] = jnp.zeros(factor_ref.shape[2:], F32)

    def adjoint(k, i):
        entry = firsts[k] * capacity + i
        value = factor_ref[k, entries.importer(table_ref, entry)] * weights[k][i]
        tau_grad_ref[pl.ds(entries.slot(table_ref, entry), 1)] += jnp.sum(value, axis=0, keepdims=True)
        return value.astype(BF16)

    last = n - 1
    push_entries(
        entries, firsts[last], table_ref, lambda entry: adjoint(last, entry - firsts[last] * capacity), held_ref, total_ref
    )
    partial_ref[...] = total_ref[...].astype(BF16)
    for k in range(last):
        for i in range(weights[k].shape[0]):
            adjoint_ref[firsts[k] * capacity + i] = adjoint(k, i)


def push_kernel(entries, first, table_ref, held_ref, adjoint_ref, partial_ref, total_ref):
    push_entries(entries, first, table_ref, lambda entry: adjoint_ref[entry], held_ref, total_ref)
    partial_ref[...] = total_ref[...].astype(partial_ref.dtype)


def finish_kernel(
    own_sum_ref, received_ref, io_ref, share_ref, logsum_ref, elasticity_ref, prices_ref, price_grad_ref, wage_grad_ref
):
    for r in range(own_sum_ref.shape[0]):
        cost_adjoint = own_sum_ref[r] + received_ref[r].astype(F32)
        price_grad_ref[r] = lax.dot_general(
            cost_adjoint.astype(BF16), io_ref[r], CONTRACT_LAST, preferred_element_type=F32
        )
        wage_grad_ref[r] = jnp.sum(cost_adjoint * share_ref[pl.ds(r, 1)], axis=1)
        prices_ref[r] = (-logsum_ref[r] / elasticity_ref[...]).astype(BF16)


def shards(
    log_prices,
    log_wages,
    labor_share,
    io_coeffs,
    pair_blocks,
    log_tau,
    elasticity,
    partners,
    list_lengths,
    price_cotangent,
):
    own, episodes, sectors = log_prices.shape
    slots = pair_blocks.shape[1]
    reg_count = lax.axis_size("reg")
    ep_count = lax.axis_size("ep")
    entries = Entries(own, slots, reg_count)
    blocks = pair_blocks.reshape(own * slots, sectors, sectors)
    row = (episodes, sectors)
    stages = radices(reg_count)
    last_radix = stages[-1]
    last_stride = reg_count // last_radix
    capacity = entries.capacity

    unit_cost = (
        labor_share[:, None, :] * log_wages[:, :, None]
        + jnp.einsum("iek,ikj->iej", log_prices, io_coeffs, preferred_element_type=F32)
    ).astype(BF16)

    held, tau, cotangent, elastic, cost_copy, table = pl.pallas_call(
        functools.partial(load_kernel, entries),
        out_shape=(
            shape(blocks.shape, BF16),
            shape((own * slots, sectors), F32),
            shape(price_cotangent.shape, F32),
            shape((1, sectors), F32),
            shape(unit_cost.shape, BF16),
            pltpu.SMEM((3 * entries.stride,), jnp.int32),
        ),
        in_specs=[SMEM, VMEM] + [HBM] * 6,
        out_specs=(VMEM,) * 5 + (SMEM,),
        scratch_shapes=[
            pltpu.SMEM(partners.shape, jnp.int32),
            pltpu.SMEM(list_lengths.shape, jnp.int32),
            pltpu.SMEM((reg_count,), jnp.int32),
            pltpu.SemaphoreType.DMA((6,)),
        ],
        compiler_params=params(1),
        cost_estimate=effort(blocks.size),
        name="load",
    )(
        lax.axis_index("reg").reshape(1),
        unit_cost,
        in_hbm(blocks),
        in_hbm(log_tau.reshape(own * slots, sectors)),
        in_hbm(price_cotangent),
        in_hbm(elasticity.reshape(1, sectors)),
        in_hbm(partners),
        in_hbm(list_lengths),
    )

    near = [unit_cost]
    stride = 1
    for radix in stages[:-1]:
        if stride > 1:
            near[0] = cost_copy
        whole = jnp.concatenate(near, axis=0)
        near += [from_peer(whole, j * stride, "reg", reg_count) for j in range(1, radix)]
        stride *= radix
    near[0] = cost_copy
    whole = jnp.concatenate(near, axis=0)
    far = [from_peer(whole, j * stride, "reg", reg_count) for j in range(1, last_radix)]

    def scored(count):
        return (
            shape((count,) + row, F32),
            shape((own + 1,) + row, F32),
            shape((own + 1,) + row, F32),
        )

    piece = last_stride * capacity
    held, *near_scores = pl.pallas_call(
        functools.partial(near_kernel, entries, len(near)),
        out_shape=(shape(blocks.shape, BF16),) + scored(piece),
        in_specs=[SMEM, HBM] + [VMEM] * (3 + len(near)),
        out_specs=(VMEM,) * 4,
        scratch_shapes=[pltpu.SemaphoreType.DMA],
        input_output_aliases={2: 0},
        compiler_params=params(2),
        cost_estimate=effort(blocks.size),
        name="near",
    )(table, in_hbm(blocks), held, tau, elastic, *near)
    scores = [near_scores]
    for j, cost in enumerate(far, 1):
        scores.append(
            pl.pallas_call(
                functools.partial(far_kernel, entries, j * last_stride),
                out_shape=scored(piece),
                in_specs=[SMEM] + [VMEM] * 4,
                out_specs=(VMEM,) * 3,
                compiler_params=params(2),
                cost_estimate=effort(blocks.size // last_radix * 2),
                name="far",
            )(table, held, tau, elastic, cost)
        )
    firsts = [j * last_stride for j in range(last_radix)]
    partial_dims = (last_stride * own,) + row
    adjoint, tau_grad, logsum, partial = pl.pallas_call(
        functools.partial(adjoint_kernel, entries, firsts),
        out_shape=(
            shape((max(entries.count - piece, 1),) + row, BF16),
            shape((own * slots, sectors), F32),
            shape((own,) + row, F32),
            shape(partial_dims, BF16),
        ),
        in_specs=[SMEM] + [VMEM] * (2 + 3 * last_radix),
        out_specs=(VMEM,) * 4,
        scratch_shapes=[
            pltpu.VMEM((last_radix, own + 1) + row, F32),
            pltpu.VMEM(partial_dims, F32),
        ],
        compiler_params=params(8),
        cost_estimate=effort(blocks.size // last_radix * 2),
        name="adjoint",
    )(table, held, cotangent, *[s[0] for s in scores], *[s[1] for s in scores], *[s[2] for s in scores])

    def push(j, dtype):
        return pl.pallas_call(
            functools.partial(push_kernel, entries, firsts[j]),
            out_shape=shape(partial_dims, dtype),
            in_specs=[SMEM, VMEM, VMEM],
            out_specs=VMEM,
            scratch_shapes=[pltpu.VMEM(partial_dims, F32)],
            compiler_params=params(8),
            cost_estimate=effort(blocks.size // last_radix * 2),
            name="push",
        )(table, held, adjoint)

    received = [to_peer(partial, firsts[-1], "reg", reg_count)]
    for j in range(last_radix - 2, 0, -1):
        received.append(to_peer(push(j, BF16), firsts[j], "reg", reg_count))
    summed = push(0, F32)
    for block in received:
        summed = summed + block.astype(F32)
    stride = last_stride
    arrived = jnp.zeros((own,) + row, BF16)
    for radix in reversed(stages[:-1]):
        stride //= radix
        parts = jnp.split(summed, radix, axis=0)
        received = [to_peer(parts[j].astype(BF16), j * stride, "reg", reg_count) for j in range(1, radix)]
        summed = parts[0]
        if stride == 1:
            arrived = received.pop()
        for block in received:
            summed = summed + block.astype(F32)

    if is_power_of_two(ep_count):
        distance = 1
        while distance < ep_count:
            tau_grad = tau_grad + to_peer(tau_grad, distance, "ep", ep_count)
            distance *= 2
    else:
        tau_grad = lax.psum(tau_grad, "ep")

    new_prices, price_grad, wage_grad = pl.pallas_call(
        finish_kernel,
        out_shape=(shape((own,) + row, BF16), shape((own,) + row, F32), shape((own, episodes), F32)),
        in_specs=[VMEM] * 6,
        out_specs=(VMEM,) * 3,
        compiler_params=params(4),
        name="finish",
    )(summed, arrived, io_coeffs, labor_share, logsum, elastic)
    return new_prices, price_grad, wage_grad, tau_grad.reshape(own, slots, sectors)


def solution(mesh):
    return jax.shard_map(
        shards,
        mesh=mesh,
        in_specs=(
            P("reg", "ep", None),
            P("reg", "ep"),
            P("reg", None),
            P("reg", None, None),
            P("reg", None, None, None),
            P("reg", None, None),
            P(),
            P(),
            P(),
            P("reg", "ep", None),
        ),
        out_specs=(
            P("reg", "ep", None),
            P("reg", "ep", None),
            P("reg", "ep"),
            P("reg", None, None),
        ),
        check_vma=False,
    )
```

time: 51.7 us -> 40.8 us (0.79)
  local copies, waits for them, and re-layouts: 10.6 us -> 0.79 us
  Pallas kernels: 8.73 us -> 16.5 us
  waiting for transfers between devices: 13.5 us -> 6.48 us
  other arithmetic: 1.41 us -> 0.72 us
  matrix products: 1.84 us -> 1.24 us
    unnamed x19 -> x7, local copies, waits for them, and re-layouts: 10.6 us -> 0.77 us
    pallas_call x1 -> x10, Pallas kernels: 8.73 us -> 16.5 us  [the longest x1 4.28 us: shards(): pl.pallas_call(functools.partial(near_kernel, entries, len(near)), out_sh...]
    ppermute x4, waiting for transfers between devices: 6.43 us -> 0.01 us  [from_peer(): return lax.ppermute(x, axis, [(peer(i, distance, n), i) for i in range(n)])]
    dot_general x1 -> x0, matrix products: 0.88 us -> none  [shards(): jnp.einsum('iej,ikj->iek', cost_adjoint.astype(BF16), io_coeffs, preferre...]
    reduce_sum x1 -> x0, other arithmetic: 0.67 us -> none  [shards(): wage_grad = jnp.sum(cost_adjoint * labor_share[:, None, :], axis=2)]
    ppermute x6, waiting for transfers between devices: 7.08 us -> 6.47 us  [to_peer(): return lax.ppermute(x, axis, [(i, peer(i, distance, n)) for i in range(n)])]
  transfers between devices with their start and end apart: 10 -> 10, of which waited for: 8 -> 2; matrix products, arithmetic and copies ran while one was open for 3% -> 0% of each run, Pallas kernels for 0% -> 35%
where the time goes in v2:
time: 40.8 us; the launch traced here: 40.6 us
  Pallas kernels  16.5 us (40%)
  starting transfers between devices  14.1 us (35%)
  waiting for transfers between devices  6.48 us (16%)
  matrix products  1.24 us (3%)
  local copies, waits for them, and re-layouts  0.79 us (2%)
  between operations  0.78 us (2%)
  other arithmetic  0.72 us (2%)
    ppermute x4, starting transfers between devices, from_peer(): return lax.ppermute(x, axis, [(peer(i, distance, n), i) for i in range(n)])  7.47 us
    ppermute x6, starting transfers between devices, to_peer(): return lax.ppermute(x, axis, [(i, peer(i, distance, n)) for i in range(n)])  6.62 us
    ppermute x6, waiting for transfers between devices, to_peer(): return lax.ppermute(x, axis, [(i, peer(i, distance, n)) for i in range(n)])  6.47 us
    pallas_call x1, Pallas kernels, shards(): pl.pallas_call(functools.partial(near_kernel, entries, len(near)), out_sh...  4.28 us
    pallas_call x3, Pallas kernels, push(): pl.pallas_call(functools.partial(push_kernel, entries, firsts[j]), out_sh...  3.67 us
    pallas_call x1, Pallas kernels, shards(): pl.pallas_call(functools.partial(load_kernel, entries), out_shape=(shape(...  3.57 us
    pallas_call x3, Pallas kernels, shards(): pl.pallas_call(functools.partial(far_kernel, entries, j * last_stride), o...  2.7 us
    pallas_call x1, Pallas kernels, shards(): pl.pallas_call(functools.partial(adjoint_kernel, entries, firsts), out_sh...  1.36 us
  transfers between devices with their start and end apart: 10, of which 2 were waited for; matrix products, arithmetic and copies ran while one was open for 0% of the time, Pallas kernels for 35%

profile of v2, /device:TPU:0, one launch (start us, length us, event | category | flops | bytes accessed | tf_op | source)
XLA Modules:
  0.0 40.6 jit_solution(2167337421700477149)
XLA Ops:
  0.6 0.0 copy-start
  0.6 0.7 %copy-done = bf16[4,16,256]{2,1,0:T(8,128)(2,1)S(1)} copy-done((bf16[4,16,256]{2,1,0:T(8,128)(2,1)S(1)}, bf16[4,16,256]{2,1,0:T(8,128)(2,1)}, u32[]{:S(2)}) %copy-start) | copy-done | bytes 32792
  1.4 1.2 %fusion.cost_ref = bf16[4,16,256]{2,1,0:T(8,128)(2,1)S(1)} fusion(bf16[4,16,256]{2,1,0:T(8,128)(2,1)S(1)} %copy-done, bf16[4,256,256]{2,1,0:T(8,128)(2,1)} %io_ref.1, f32[4,16]{1,0:T(4,128)} %param.11, f32[4,256]{1,0:T(4,128)} %share_ref.1), kind=kOutput, calls=%fused_computation.1 | convolution fusion | flops 8437760 | bytes 594176 | tf_op jit(solution)/shard_map/iek,ikj->iej/dot_general | solution.py:263
  2.6 3.0 %collective-permute-start = (bf16[4,16,256]{2,1,0:T(8,128)(2,1)S(1)}, bf16[4,16,256]{2,1,0:T(8,128)(2,1)S(1)}, u32[]{:S(2)}, u32[]{:S(2)}) collective-permute-start(bf16[4,16,256]{2,1,0:T(8,128)(2,1)S(1)} %fusion.cost_ref), channel_id=1, source_target_pairs={{4,0},{0,4},{12,8},{8,12},{20,16},{16,20},{28,24},{24,28},{5,1},{1... | collective-permute-start | bytes 98312 | tf_op jit(solution)/shard_map/ppermute | solution.py:45
  5.6 3.6 %load.1 = (bf16[128,256,256]{2,1,0:T(8,128)(2,1)S(1)}, f32[128,256]{1,0:T(8,128)S(1)}, f32[4,16,256]{2,1,0:T(8,128)S(1)}, f32[1,256]{1,0:T(1,128)S(1)}, bf16[4,16,256]{2,1,0:T(8,128)(2,1)S(1)}, /*index=5*/s32[387]{0:T(512)S(4)}) custom-call(s32[1]{0:T(128)} %bitcast.me_ref, bf16[4,16,256]{2,1,0:T(8,128)(2,1)S(1)} %fusion.cost_ref, ...), custom_call_target="tpu_custom_call" | custom-call | bytes 8388608 | tf_op jit(solution)/shard_map/load/pallas_call | solution.py:266
  9.2 0.0 collective-permute-done.refs_6_
  9.3 3.7 %collective-permute-start.3 = (bf16[8,16,256]{2,1,0:T(8,128)(2,1)S(1)}, bf16[8,16,256]{2,1,0:T(8,128)(2,1)S(1)}, u32[]{:S(2)}, u32[]{:S(2)}) collective-permute-start(bf16[8,16,256]{2,1,0:T(8,128)(2,1)S(1)} %constant_dynamic-update-slice_fusion), channel_id=1, source_target_pairs={{24,0},{28,4},{16,8},{20,12},{8,16},{12,20},{0,24},{4,28},{25,1},{... | collective-permute-start | bytes 196616 | tf_op jit(solution)/shard_map/ppermute | solution.py:45
  12.9 0.0 collective-permute-start.2
  12.9 0.8 %collective-permute-start.1 = (bf16[8,16,256]{2,1,0:T(8,128)(2,1)S(1)}, bf16[8,16,256]{2,1,0:T(8,128)(2,1)S(1)}, u32[]{:S(2)}, u32[]{:S(2)}) collective-permute-start(bf16[8,16,256]{2,1,0:T(8,128)(2,1)S(1)} %constant_dynamic-update-slice_fusion), channel_id=1, source_target_pairs={{8,0},{12,4},{0,8},{4,12},{24,16},{28,20},{16,24},{20,28},{9,1},{1... | collective-permute-start | bytes 196616 | tf_op jit(solution)/shard_map/ppermute | solution.py:45
  13.7 4.3 %near.1 = (bf16[128,256,256]{2,1,0:T(8,128)(2,1)S(1)}, f32[32,16,256]{2,1,0:T(8,128)S(1)}, f32[5,16,256]{2,1,0:T(8,128)S(1)}, f32[5,16,256]{2,1,0:T(8,128)S(1)}) custom-call(s32[387]{0:T(512)S(4)} %get-tuple-element.30.refs_0_.table_ref, bf16[128,256,256]{2,1,0:T(8,128)(2,1)} %bitcast.8, ...), custom_call_target="tpu_custom_call", output_to_operand_aliasing={{0}: (2, {})} | custom-call | bytes 8388608 | tf_op jit(solution)/shard_map/near/pallas_call | solution.py:318
  18.0 0.0 collective-permute-done.3.cost_ref
  18.0 0.9 %far.5 = (f32[32,16,256]{2,1,0:T(8,128)S(1)}, f32[5,16,256]{2,1,0:T(8,128)S(1)}, f32[5,16,256]{2,1,0:T(8,128)S(1)}) custom-call(s32[387]{0:T(512)S(4)} %get-tuple-element.30.refs_0_.table_ref, bf16[128,256,256]{2,1,0:T(8,128)(2,1)S(1)} %get-tuple-element.35.held_ref.refs_1_, f32[128,256]{1,0:T(8,128)S(1)} %get-tuple-element.32.refs_3_.tau_ref, ...), custom_call_target="tpu_custom_call" | custom-call | bytes 4194304 | tf_op jit(solution)/shard_map/far/pallas_call | solution.py:332
  18.9 0.0 collective-permute-done.2.cost_ref
  18.9 0.9 %far.4 = (f32[32,16,256]{2,1,0:T(8,128)S(1)}, f32[5,16,256]{2,1,0:T(8,128)S(1)}, f32[5,16,256]{2,1,0:T(8,128)S(1)}) custom-call(s32[387]{0:T(512)S(4)} %get-tuple-element.30.refs_0_.table_ref, bf16[128,256,256]{2,1,0:T(8,128)(2,1)S(1)} %get-tuple-element.35.held_ref.refs_1_, f32[128,256]{1,0:T(8,128)S(1)} %get-tuple-element.32.refs_3_.tau_ref, ...), custom_call_target="tpu_custom_call" | custom-call | bytes 4194304 | tf_op jit(solution)/shard_map/far/pallas_call | solution.py:332
  19.8 0.0 collective-permute-done.1.cost_ref
  19.8 0.9 %far.3 = (f32[32,16,256]{2,1,0:T(8,128)S(1)}, f32[5,16,256]{2,1,0:T(8,128)S(1)}, f32[5,16,256]{2,1,0:T(8,128)S(1)}) custom-call(s32[387]{0:T(512)S(4)} %get-tuple-element.30.refs_0_.table_ref, bf16[128,256,256]{2,1,0:T(8,128)(2,1)S(1)} %get-tuple-element.35.held_ref.refs_1_, f32[128,256]{1,0:T(8,128)S(1)} %get-tuple-element.32.refs_3_.tau_ref, ...), custom_call_target="tpu_custom_call" | custom-call | bytes 4194304 | tf_op jit(solution)/shard_map/far/pallas_call | solution.py:332
  20.7 1.4 %adjoint.1 = (bf16[96,16,256]{2,1,0:T(8,128)(2,1)S(1)}, f32[128,256]{1,0:T(8,128)S(1)}, f32[4,16,256]{2,1,0:T(8,128)S(1)}, bf16[8,16,256]{2,1,0:T(8,128)(2,1)S(1)}) custom-call(s32[387]{0:T(512)S(4)} %get-tuple-element.30.refs_0_.table_ref, bf16[128,256,256]{2,1,0:T(8,128)(2,1)S(1)} %get-tuple-element.35.held_ref.refs_1_, ...), custom_call_target="tpu_custom_call" | custom-call | bytes 4194304 | tf_op jit(solution)/shard_map/adjoint/pallas_call | solution.py:344
  22.1 0.1 collective-permute-start.8
  22.2 1.2 %push.4 = bf16[8,16,256]{2,1,0:T(8,128)(2,1)S(1)} custom-call(s32[387]{0:T(512)S(4)} %get-tuple-element.30.refs_0_.table_ref, bf16[128,256,256]{2,1,0:T(8,128)(2,1)S(1)} %get-tuple-element.35.held_ref.refs_1_, bf16[96,16,256]{2,1,0:T(8,128)(2,1)S(1)} %get-tuple-element.49.adjoint_ref), custom_call_target="tpu_custom_call" | custom-call | bytes 4194304 | tf_op jit(solution)/shard_map/push/pallas_call | solution.py:364
  23.4 0.0 copy-start.1
  23.4 0.0 copy-start.2
  23.4 1.2 %push.5 = bf16[8,16,256]{2,1,0:T(8,128)(2,1)S(1)} custom-call(s32[387]{0:T(512)S(4)} %get-tuple-element.30.refs_0_.table_ref, bf16[128,256,256]{2,1,0:T(8,128)(2,1)S(1)} %get-tuple-element.35.held_ref.refs_1_, bf16[96,16,256]{2,1,0:T(8,128)(2,1)S(1)} %get-tuple-element.49.adjoint_ref), custom_call_target="tpu_custom_call" | custom-call | bytes 4194304 | tf_op jit(solution)/shard_map/push/pallas_call | solution.py:364
  24.7 2.3 %collective-permute-start.5 = (bf16[8,16,256]{2,1,0:T(8,128)(2,1)S(1)}, bf16[8,16,256]{2,1,0:T(8,128)(2,1)S(1)}, u32[]{:S(2)}, u32[]{:S(2)}) collective-permute-start(bf16[8,16,256]{2,1,0:T(8,128)(2,1)S(1)} %push.4), channel_id=1, source_target_pairs={{0,16},{4,20},{8,24},{12,28},{16,0},{20,4},{24,8},{28,12},{1,17},{... | collective-permute-start | bytes 196616 | tf_op jit(solution)/shard_map/ppermute | solution.py:49
  26.9 2.0 %collective-permute-start.6 = (bf16[8,16,256]{2,1,0:T(8,128)(2,1)S(1)}, bf16[8,16,256]{2,1,0:T(8,128)(2,1)S(1)}, u32[]{:S(2)}, u32[]{:S(2)}) collective-permute-start(bf16[8,16,256]{2,1,0:T(8,128)(2,1)S(1)} %push.5), channel_id=1, source_target_pairs={{0,8},{4,12},{8,0},{12,4},{16,24},{20,28},{24,16},{28,20},{1,9},{5... | collective-permute-start | bytes 196616 | tf_op jit(solution)/shard_map/ppermute | solution.py:49
  28.9 0.2 collective-permute-start.4
  29.1 1.2 %push.3 = f32[8,16,256]{2,1,0:T(8,128)S(1)} custom-call(s32[387]{0:T(512)S(4)} %get-tuple-element.30.refs_0_.table_ref, bf16[128,256,256]{2,1,0:T(8,128)(2,1)S(1)} %get-tuple-element.35.held_ref.refs_1_, bf16[96,16,256]{2,1,0:T(8,128)(2,1)S(1)} %get-tuple-element.49.adjoint_ref), custom_call_target="tpu_custom_call" | custom-call | bytes 4194304 | tf_op jit(solution)/shard_map/push/pallas_call | solution.py:364
  30.3 0.0 collective-permute-done.8
  30.4 1.6 %collective-permute-start.9 = (f32[128,256]{1,0:T(8,128)S(1)}, f32[128,256]{1,0:T(8,128)S(1)}, u32[]{:S(2)}, u32[]{:S(2)}) collective-permute-start(f32[128,256]{1,0:T(8,128)S(1)} %add.22), channel_id=1, source_target_pairs={{0,2},{1,3},{2,0},{3,1},{4,6},{5,7},{6,4},{7,5},{8,10},{9,11},{10,... | collective-permute-start | bytes 393224 | tf_op jit(solution)/shard_map/ppermute | solution.py:49
  31.9 0.0 collective-permute-done.5
  31.9 0.0 collective-permute-done.6
  31.9 3.0 %collective-permute-done.4 = bf16[8,16,256]{2,1,0:T(8,128)(2,1)S(1)} collective-permute-done((bf16[8,16,256]{2,1,0:T(8,128)(2,1)S(1)}, bf16[8,16,256]{2,1,0:T(8,128)(2,1)S(1)}, u32[]{:S(2)}, u32[]{:S(2)}) %collective-permute-start.4) | collective-permute-done | bytes 65568 | tf_op jit(solution)/shard_map/ppermute | solution.py:49
  35.0 0.5 %collective-permute-start.7 = (bf16[4,16,256]{2,1,0:T(8,128)(2,1)S(1)}, bf16[4,16,256]{2,1,0:T(8,128)(2,1)S(1)}, u32[]{:S(2)}, u32[]{:S(2)}) collective-permute-start(bf16[4,16,256]{2,1,0:T(8,128)(2,1)S(1)} %split.12), channel_id=1, source_target_pairs={{0,4},{4,0},{8,12},{12,8},{16,20},{20,16},{24,28},{28,24},{1,5},{5... | collective-permute-start | bytes 98312 | tf_op jit(solution)/shard_map/ppermute | solution.py:49
  35.6 3.4 %collective-permute-done.7.received_ref = bf16[4,16,256]{2,1,0:T(8,128)(2,1)S(1)} collective-permute-done((bf16[4,16,256]{2,1,0:T(8,128)(2,1)S(1)}, bf16[4,16,256]{2,1,0:T(8,128)(2,1)S(1)}, u32[]{:S(2)}, u32[]{:S(2)}) %collective-permute-start.7) | collective-permute-done | bytes 32800 | tf_op jit(solution)/shard_map/ppermute | solution.py:49
  39.0 0.0 copy-done.1
  39.0 0.0 copy-done.2
  39.0 0.9 %finish.1 = (bf16[4,16,256]{2,1,0:T(8,128)(2,1)}, f32[4,16,256]{2,1,0:T(8,128)}, f32[4,16]{1,0:T(4,128)}) custom-call(f32[4,16,256]{2,1,0:T(8,128)S(1)} %split.9.own_sum_ref, bf16[4,16,256]{2,1,0:T(8,128)(2,1)S(1)} %collective-permute-done.7.received_ref, bf16[4,256,256]{2,1,0:T(8,128)(2,1)S(1)} %copy-done.1, f32[4,256]{1,0:T(4,128)S(1)} %copy-done.2, ...), custom_call_target="tpu_custom_call" | custom-call | tf_op jit(solution)/shard_map/finish/pallas_call | solution.py:401
  39.9 0.0 collective-permute-done.9
  39.9 0.7 %add.23 = f32[128,256]{1,0:T(8,128)} add(f32[128,256]{1,0:T(8,128)S(1)} %add.22, f32[128,256]{1,0:T(8,128)S(1)} %collective-permute-done.9) | non-fusion elementwise | flops 32768 | bytes 393216 | tf_op jit(solution)/shard_map/add | solution.py:396
  (6 shorter events, 0.1 us)
Async XLA Ops:
  0.6 0.8 %copy-start = (bf16[4,16,256]{2,1,0:T(8,128)(2,1)S(1)}, bf16[4,16,256]{2,1,0:T(8,128)(2,1)}, u32[]{:S(2)}) copy-start(bf16[4,16,256]{2,1,0:T(8,128)(2,1)} %param.10) | copy-start | bytes 98308
  2.6 6.6 %collective-permute-start = (bf16[4,16,256]{2,1,0:T(8,128)(2,1)S(1)}, bf16[4,16,256]{2,1,0:T(8,128)(2,1)S(1)}, u32[]{:S(2)}, u32[]{:S(2)}) collective-permute-start(bf16[4,16,256]{2,1,0:T(8,128)(2,1)S(1)} %fusion.cost_ref), channel_id=1, source_target_pairs={{4,0},{0,4},{12,8},{8,12},{20,16},{16,20},{28,24},{24,28},{5,1},{1... | collective-permute-start | bytes 98312 | tf_op jit(solution)/shard_map/ppermute | solution.py:45
  9.3 8.7 %collective-permute-start.3 = (bf16[8,16,256]{2,1,0:T(8,128)(2,1)S(1)}, bf16[8,16,256]{2,1,0:T(8,128)(2,1)S(1)}, u32[]{:S(2)}, u32[]{:S(2)}) collective-permute-start(bf16[8,16,256]{2,1,0:T(8,128)(2,1)S(1)} %constant_dynamic-update-slice_fusion), channel_id=1, source_target_pairs={{24,0},{28,4},{16,8},{20,12},{8,16},{12,20},{0,24},{4,28},{25,1},{... | collective-permute-start | bytes 196616 | tf_op jit(solution)/shard_map/ppermute | solution.py:45
  12.9 6.0 %collective-permute-start.2 = (bf16[8,16,256]{2,1,0:T(8,128)(2,1)S(1)}, bf16[8,16,256]{2,1,0:T(8,128)(2,1)S(1)}, u32[]{:S(2)}, u32[]{:S(2)}) collective-permute-start(bf16[8,16,256]{2,1,0:T(8,128)(2,1)S(1)} %constant_dynamic-update-slice_fusion), channel_id=1, source_target_pairs={{16,0},{20,4},{24,8},{28,12},{0,16},{4,20},{8,24},{12,28},{17,1},{... | collective-permute-start | bytes 196616 | tf_op jit(solution)/shard_map/ppermute | solution.py:45
  12.9 6.9 %collective-permute-start.1 = (bf16[8,16,256]{2,1,0:T(8,128)(2,1)S(1)}, bf16[8,16,256]{2,1,0:T(8,128)(2,1)S(1)}, u32[]{:S(2)}, u32[]{:S(2)}) collective-permute-start(bf16[8,16,256]{2,1,0:T(8,128)(2,1)S(1)} %constant_dynamic-update-slice_fusion), channel_id=1, source_target_pairs={{8,0},{12,4},{0,8},{4,12},{24,16},{28,20},{16,24},{20,28},{9,1},{1... | collective-permute-start | bytes 196616 | tf_op jit(solution)/shard_map/ppermute | solution.py:45
  22.1 8.3 %collective-permute-start.8 = (f32[128,256]{1,0:T(8,128)S(1)}, f32[128,256]{1,0:T(8,128)S(1)}, u32[]{:S(2)}, u32[]{:S(2)}) collective-permute-start(f32[128,256]{1,0:T(8,128)S(1)} %get-tuple-element.55), channel_id=1, source_target_pairs={{0,1},{1,0},{2,3},{3,2},{4,5},{5,4},{6,7},{7,6},{8,9},{9,8},{10,11... | collective-permute-start | bytes 393224 | tf_op jit(solution)/shard_map/ppermute | solution.py:49
  23.4 15.6 %copy-start.1 = (bf16[4,256,256]{2,1,0:T(8,128)(2,1)S(1)}, bf16[4,256,256]{2,1,0:T(8,128)(2,1)}, u32[]{:S(2)}) copy-start(bf16[4,256,256]{2,1,0:T(8,128)(2,1)} %io_ref.1) | copy-start | bytes 1572868
  23.4 15.6 %copy-start.2 = (f32[4,256]{1,0:T(4,128)S(1)}, f32[4,256]{1,0:T(4,128)}, u32[]{:S(2)}) copy-start(f32[4,256]{1,0:T(4,128)} %share_ref.1) | copy-start | bytes 12292
  24.7 7.3 %collective-permute-start.5 = (bf16[8,16,256]{2,1,0:T(8,128)(2,1)S(1)}, bf16[8,16,256]{2,1,0:T(8,128)(2,1)S(1)}, u32[]{:S(2)}, u32[]{:S(2)}) collective-permute-start(bf16[8,16,256]{2,1,0:T(8,128)(2,1)S(1)} %push.4), channel_id=1, source_target_pairs={{0,16},{4,20},{8,24},{12,28},{16,0},{20,4},{24,8},{28,12},{1,17},{... | collective-permute-start | bytes 196616 | tf_op jit(solution)/shard_map/ppermute | solution.py:49
  26.9 5.0 %collective-permute-start.6 = (bf16[8,16,256]{2,1,0:T(8,128)(2,1)S(1)}, bf16[8,16,256]{2,1,0:T(8,128)(2,1)S(1)}, u32[]{:S(2)}, u32[]{:S(2)}) collective-permute-start(bf16[8,16,256]{2,1,0:T(8,128)(2,1)S(1)} %push.5), channel_id=1, source_target_pairs={{0,8},{4,12},{8,0},{12,4},{16,24},{20,28},{24,16},{28,20},{1,9},{5... | collective-permute-start | bytes 196616 | tf_op jit(solution)/shard_map/ppermute | solution.py:49
  28.9 6.1 %collective-permute-start.4 = (bf16[8,16,256]{2,1,0:T(8,128)(2,1)S(1)}, bf16[8,16,256]{2,1,0:T(8,128)(2,1)S(1)}, u32[]{:S(2)}, u32[]{:S(2)}) collective-permute-start(bf16[8,16,256]{2,1,0:T(8,128)(2,1)S(1)} %get-tuple-element.50), channel_id=1, source_target_pairs={{0,24},{4,28},{8,16},{12,20},{16,8},{20,12},{24,0},{28,4},{1,25},{... | collective-permute-start | bytes 196616 | tf_op jit(solution)/shard_map/ppermute | solution.py:49
  30.4 9.5 %collective-permute-start.9 = (f32[128,256]{1,0:T(8,128)S(1)}, f32[128,256]{1,0:T(8,128)S(1)}, u32[]{:S(2)}, u32[]{:S(2)}) collective-permute-start(f32[128,256]{1,0:T(8,128)S(1)} %add.22), channel_id=1, source_target_pairs={{0,2},{1,3},{2,0},{3,1},{4,6},{5,7},{6,4},{7,5},{8,10},{9,11},{10,... | collective-permute-start | bytes 393224 | tf_op jit(solution)/shard_map/ppermute | solution.py:49
  35.0 4.0 %collective-permute-start.7 = (bf16[4,16,256]{2,1,0:T(8,128)(2,1)S(1)}, bf16[4,16,256]{2,1,0:T(8,128)(2,1)S(1)}, u32[]{:S(2)}, u32[]{:S(2)}) collective-permute-start(bf16[4,16,256]{2,1,0:T(8,128)(2,1)S(1)} %split.12), channel_id=1, source_target_pairs={{0,4},{4,0},{8,12},{12,8},{16,20},{20,16},{24,28},{28,24},{1,5},{5... | collective-permute-start | bytes 98312 | tf_op jit(solution)/shard_map/ppermute | solution.py:49

commit v3 on v2

--- a/solution.py
+++ b/solution.py
@@ -169,26 +169,24 @@
     score_entries(entries, first, table_ref, [cost_ref], held_ref, tau_ref, elasticity_ref, weights_ref, top_ref, norm_ref)
 
 
-def push_entries(entries, first, table_ref, adjoint_of, held_ref, total_ref):
+def push_entries(entries, distances, table_ref, adjoint_of, held_ref, total_ref):
     total_ref[...] = jnp.zeros(total_ref.shape, F32)
-    own, capacity = entries.own, entries.capacity
-    for i in range(total_ref.shape[0] // own * capacity):
-        entry = first * capacity + i
-        place = i // capacity * own + entries.place(table_ref, entry)
-        total_ref[place] += lax.dot_general(
-            adjoint_of(entry),
-            held_ref[entries.slot(table_ref, entry)],
-            CONTRACT_LAST,
-            preferred_element_type=F32,
-        )
-
-
-def adjoint_kernel(entries, firsts, *refs):
-    n = len(firsts)
+    for block, distance in enumerate(distances):
+        for entry in range(distance * entries.capacity, (distance + 1) * entries.capacity):
+            total_ref[block * entries.own + entries.place(table_ref, entry)] += lax.dot_general(
+                adjoint_of(entry),
+                held_ref[entries.slot(table_ref, entry)],
+                CONTRACT_LAST,
+                preferred_element_type=F32,
+            )
+
+
+def adjoint_kernel(entries, n, distances, *refs):
     table_ref, held_ref, cotangent_ref = refs[:3]
     weights, tops, norms = refs[3 : 3 + n], refs[3 + n : 3 + 2 * n], refs[3 + 2 * n : 3 + 3 * n]
     adjoint_ref, tau_grad_ref, logsum_ref, partial_ref, factor_ref, total_ref = refs[3 + 3 * n :]
     own, capacity = entries.own, entries.capacity
+    piece = weights[0].shape[0]
     tau_grad_ref[...] = jnp.zeros(tau_grad_ref.shape, F32)
     for r in range(own):
         top = functools.reduce(jnp.maximum, [ref[r] for ref in tops])
@@ -201,37 +199,38 @@
     for k in range(n):
         factor_ref[k, own] = jnp.zeros(factor_ref.shape[2:], F32)
 
-    def adjoint(k, i):
-        entry = firsts[k] * capacity + i
+    def adjoint(entry):
+        k, i = divmod(entry, piece)
         value = factor_ref[k, entries.importer(table_ref, entry)] * weights[k][i]
         tau_grad_ref[pl.ds(entries.slot(table_ref, entry), 1)] += jnp.sum(value, axis=0, keepdims=True)
         return value.astype(BF16)
 
-    last = n - 1
-    push_entries(
-        entries, firsts[last], table_ref, lambda entry: adjoint(last, entry - firsts[last] * capacity), held_ref, total_ref
-    )
+    push_entries(entries, distances, table_ref, adjoint, held_ref, total_ref)
     partial_ref[...] = total_ref[...].astype(BF16)
-    for k in range(last):
-        for i in range(weights[k].shape[0]):
-            adjoint_ref[firsts[k] * capacity + i] = adjoint(k, i)
-
-
-def push_kernel(entries, first, table_ref, held_ref, adjoint_ref, partial_ref, total_ref):
-    push_entries(entries, first, table_ref, lambda entry: adjoint_ref[entry], held_ref, total_ref)
+    for entry in range(entries.count):
+        if entry // capacity not in distances:
+            adjoint_ref[entry] = adjoint(entry)
+
+
+def push_kernel(entries, distances, table_ref, held_ref, adjoint_ref, partial_ref, total_ref):
+    push_entries(entries, distances, table_ref, lambda entry: adjoint_ref[entry], held_ref, total_ref)
     partial_ref[...] = total_ref[...].astype(partial_ref.dtype)
 
 
-def finish_kernel(
-    own_sum_ref, received_ref, io_ref, share_ref, logsum_ref, elasticity_ref, prices_ref, price_grad_ref, wage_grad_ref
-):
+def finish_kernel(n, *refs):
+    own_sum_ref, received = refs[0], refs[1 : 1 + n]
+    io_ref, share_ref, logsum_ref, elasticity_ref, tau_ref, tau_received_ref = refs[1 + n : 7 + n]
+    prices_ref, price_grad_ref, wage_grad_ref, tau_grad_ref = refs[7 + n :]
+    tau_grad_ref[...] = tau_ref[...] + tau_received_ref[...]
     for r in range(own_sum_ref.shape[0]):
-        cost_adjoint = own_sum_ref[r] + received_ref[r].astype(F32)
+        prices_ref[r] = (-logsum_ref[r] / elasticity_ref[...]).astype(BF16)
+        cost_adjoint = own_sum_ref[r]
+        for ref in received:
+            cost_adjoint = cost_adjoint + ref[r].astype(F32)
         price_grad_ref[r] = lax.dot_general(
             cost_adjoint.astype(BF16), io_ref[r], CONTRACT_LAST, preferred_element_type=F32
         )
         wage_grad_ref[r] = jnp.sum(cost_adjoint * share_ref[pl.ds(r, 1)], axis=1)
-        prices_ref[r] = (-logsum_ref[r] / elasticity_ref[...]).astype(BF16)
 
 
 def shards(
@@ -339,12 +338,13 @@
                 name="far",
             )(table, held, tau, elastic, cost)
         )
-    firsts = [j * last_stride for j in range(last_radix)]
-    partial_dims = (last_stride * own,) + row
+    radix = stages[0]
+    groups = [range(j, reg_count, radix) for j in range(radix)]
+    partial_dims = (reg_count // radix * own,) + row
     adjoint, tau_grad, logsum, partial = pl.pallas_call(
-        functools.partial(adjoint_kernel, entries, firsts),
+        functools.partial(adjoint_kernel, entries, last_radix, groups[-1]),
         out_shape=(
-            shape((max(entries.count - piece, 1),) + row, BF16),
+            shape((entries.count,) + row, BF16),
             shape((own * slots, sectors), F32),
             shape((own,) + row, F32),
             shape(partial_dims, BF16),
@@ -356,56 +356,63 @@
             pltpu.VMEM(partial_dims, F32),
         ],
         compiler_params=params(8),
-        cost_estimate=effort(blocks.size // last_radix * 2),
+        cost_estimate=effort(blocks.size),
         name="adjoint",
     )(table, held, cotangent, *[s[0] for s in scores], *[s[1] for s in scores], *[s[2] for s in scores])
 
     def push(j, dtype):
         return pl.pallas_call(
-            functools.partial(push_kernel, entries, firsts[j]),
+            functools.partial(push_kernel, entries, groups[j]),
             out_shape=shape(partial_dims, dtype),
             in_specs=[SMEM, VMEM, VMEM],
             out_specs=VMEM,
             scratch_shapes=[pltpu.VMEM(partial_dims, F32)],
             compiler_params=params(8),
-            cost_estimate=effort(blocks.size // last_radix * 2),
+            cost_estimate=effort(blocks.size),
             name="push",
         )(table, held, adjoint)
 
-    received = [to_peer(partial, firsts[-1], "reg", reg_count)]
-    for j in range(last_radix - 2, 0, -1):
-        received.append(to_peer(push(j, BF16), firsts[j], "reg", reg_count))
-    summed = push(0, F32)
-    for block in received:
-        summed = summed + block.astype(F32)
-    stride = last_stride
-    arrived = jnp.zeros((own,) + row, BF16)
-    for radix in reversed(stages[:-1]):
-        stride //= radix
-        parts = jnp.split(summed, radix, axis=0)
-        received = [to_peer(parts[j].astype(BF16), j * stride, "reg", reg_count) for j in range(1, radix)]
-        summed = parts[0]
-        if stride == 1:
-            arrived = received.pop()
+    received = [to_peer(partial, radix - 1, "reg", reg_count)] if radix > 1 else []
+    for j in range(radix - 2, 0, -1):
+        received.append(to_peer(push(j, BF16), j, "reg", reg_count))
+    summed = push(0, F32) if radix > 1 else partial.astype(F32)
+    stride = 1
+    for following in stages[1:]:
         for block in received:
             summed = summed + block.astype(F32)
+        stride *= radix
+        radix = following
+        parts = summed.reshape((-1, radix, own) + row)
+        received = [
+            to_peer(parts[:, j].reshape((-1,) + row).astype(BF16), j * stride, "reg", reg_count)
+            for j in range(radix - 1, 0, -1)
+        ]
+        summed = parts[:, 0].reshape((-1,) + row)
 
     if is_power_of_two(ep_count):
+        tau_received = jnp.zeros_like(tau_grad)
         distance = 1
         while distance < ep_count:
-            tau_grad = tau_grad + to_peer(tau_grad, distance, "ep", ep_count)
+            tau_grad = tau_grad + tau_received if distance > 1 else tau_grad
+            tau_received = to_peer(tau_grad, distance, "ep", ep_count)
             distance *= 2
     else:
         tau_grad = lax.psum(tau_grad, "ep")
-
-    new_prices, price_grad, wage_grad = pl.pallas_call(
-        finish_kernel,
-        out_shape=(shape((own,) + row, BF16), shape((own,) + row, F32), shape((own, episodes), F32)),
-        in_specs=[VMEM] * 6,
-        out_specs=(VMEM,) * 3,
+        tau_received = jnp.zeros_like(tau_grad)
+
+    new_prices, price_grad, wage_grad, tau_grad = pl.pallas_call(
+        functools.partial(finish_kernel, len(received)),
+        out_shape=(
+            shape((own,) + row, BF16),
+            shape((own,) + row, F32),
+            shape((own, episodes), F32),
+            shape(tau_grad.shape, F32),
+        ),
+        in_specs=[VMEM] * (7 + len(received)),
+        out_specs=(VMEM,) * 4,
         compiler_params=params(4),
         name="finish",
-    )(summed, arrived, io_coeffs, labor_share, logsum, elastic)
+    )(summed, *received, io_coeffs, labor_share, logsum, elastic, tau_grad, tau_received)
     return new_prices, price_grad, wage_grad, tau_grad.reshape(own, slots, sectors)
 
 

time: 40.8 us -> 39 us (0.956)
  waiting for transfers between devices: 6.48 us -> 5.48 us
  other arithmetic: 0.72 us -> 0.07 us
    ppermute x6, waiting for transfers between devices: 6.47 us -> 5.47 us  [to_peer(): return lax.ppermute(x, axis, [(i, peer(i, distance, n)) for i in range(n)])]
    add x2 -> x1, other arithmetic: 0.69 us -> 0.02 us  [shards(): tau_grad = tau_grad + tau_received if distance > 1 else tau_grad]
    pallas_call x5 -> x3, Pallas kernels: 5.92 us -> 5.7 us  [the longest x1 2.49 us: shards(): pl.pallas_call(functools.partial(adjoint_kernel, entries, last_radix, gro...]
  transfers between devices with their start and end apart: 10 -> 10, of which waited for: 2 -> 3; matrix products, arithmetic and copies ran while one was open for 0% -> 0% of each run, Pallas kernels for 35% -> 31%
where the time goes in v3:
time: 39 us; the launch traced here: 38.7 us
  Pallas kernels  16.3 us (42%)
  starting transfers between devices  14.1 us (36%)
  waiting for transfers between devices  5.48 us (14%)
  matrix products  1.24 us (3%)
  local copies, waits for them, and re-layouts  0.79 us (2%)
  between operations  0.78 us (2%)
    ppermute x4, starting transfers between devices, from_peer(): return lax.ppermute(x, axis, [(peer(i, distance, n), i) for i in range(n)])  7.47 us
    ppermute x6, starting transfers between devices, to_peer(): return lax.ppermute(x, axis, [(i, peer(i, distance, n)) for i in range(n)])  6.63 us
    ppermute x6, waiting for transfers between devices, to_peer(): return lax.ppermute(x, axis, [(i, peer(i, distance, n)) for i in range(n)])  5.47 us
    pallas_call x1, Pallas kernels, shards(): pl.pallas_call(functools.partial(near_kernel, entries, len(near)), out_sh...  4.28 us
    pallas_call x1, Pallas kernels, shards(): pl.pallas_call(functools.partial(load_kernel, entries), out_shape=(shape(...  3.57 us
    pallas_call x3, Pallas kernels, shards(): pl.pallas_call(functools.partial(far_kernel, entries, j * last_stride), o...  2.71 us
    pallas_call x1, Pallas kernels, shards(): pl.pallas_call(functools.partial(adjoint_kernel, entries, last_radix, gro...  2.49 us
    pallas_call x1, Pallas kernels, push(): pl.pallas_call(functools.partial(push_kernel, entries, groups[j]), out_sh...  2.33 us
  transfers between devices with their start and end apart: 10, of which 3 were waited for; matrix products, arithmetic and copies ran while one was open for 0% of the time, Pallas kernels for 31%

profile of v3, /device:TPU:0, one launch (start us, length us, event | category | flops | bytes accessed | tf_op | source)
XLA Modules:
  0.0 38.7 jit_solution(1786221813400763652)
XLA Ops:
  0.6 0.0 copy-start
  0.6 0.7 %copy-done = bf16[4,16,256]{2,1,0:T(8,128)(2,1)S(1)} copy-done((bf16[4,16,256]{2,1,0:T(8,128)(2,1)S(1)}, bf16[4,16,256]{2,1,0:T(8,128)(2,1)}, u32[]{:S(2)}) %copy-start) | copy-done | bytes 32792
  1.4 1.2 %fusion.cost_ref = bf16[4,16,256]{2,1,0:T(8,128)(2,1)S(1)} fusion(bf16[4,16,256]{2,1,0:T(8,128)(2,1)S(1)} %copy-done, bf16[4,256,256]{2,1,0:T(8,128)(2,1)} %refs_4_.1, f32[4,16]{1,0:T(4,128)} %param.11, f32[4,256]{1,0:T(4,128)} %refs_5_.1), kind=kOutput, calls=%fused_computation.1 | convolution fusion | flops 8437760 | bytes 594176 | tf_op jit(solution)/shard_map/iek,ikj->iej/dot_general | solution.py:262
  2.6 3.0 %collective-permute-start = (bf16[4,16,256]{2,1,0:T(8,128)(2,1)S(1)}, bf16[4,16,256]{2,1,0:T(8,128)(2,1)S(1)}, u32[]{:S(2)}, u32[]{:S(2)}) collective-permute-start(bf16[4,16,256]{2,1,0:T(8,128)(2,1)S(1)} %fusion.cost_ref), channel_id=1, source_target_pairs={{4,0},{0,4},{12,8},{8,12},{20,16},{16,20},{28,24},{24,28},{5,1},{1... | collective-permute-start | bytes 98312 | tf_op jit(solution)/shard_map/ppermute | solution.py:45
  5.6 3.6 %load.1 = (bf16[128,256,256]{2,1,0:T(8,128)(2,1)S(1)}, f32[128,256]{1,0:T(8,128)S(1)}, f32[4,16,256]{2,1,0:T(8,128)S(1)}, f32[1,256]{1,0:T(1,128)S(1)}, bf16[4,16,256]{2,1,0:T(8,128)(2,1)S(1)}, /*index=5*/s32[387]{0:T(512)S(4)}) custom-call(s32[1]{0:T(128)} %bitcast.me_ref, bf16[4,16,256]{2,1,0:T(8,128)(2,1)S(1)} %fusion.cost_ref, ...), custom_call_target="tpu_custom_call" | custom-call | bytes 8388608 | tf_op jit(solution)/shard_map/load/pallas_call | solution.py:265
  9.2 0.0 collective-permute-done.refs_6_
  9.3 3.7 %collective-permute-start.3 = (bf16[8,16,256]{2,1,0:T(8,128)(2,1)S(1)}, bf16[8,16,256]{2,1,0:T(8,128)(2,1)S(1)}, u32[]{:S(2)}, u32[]{:S(2)}) collective-permute-start(bf16[8,16,256]{2,1,0:T(8,128)(2,1)S(1)} %constant_dynamic-update-slice_fusion), channel_id=1, source_target_pairs={{24,0},{28,4},{16,8},{20,12},{8,16},{12,20},{0,24},{4,28},{25,1},{... | collective-permute-start | bytes 196616 | tf_op jit(solution)/shard_map/ppermute | solution.py:45
  12.9 0.0 collective-permute-start.2
  12.9 0.8 %collective-permute-start.1 = (bf16[8,16,256]{2,1,0:T(8,128)(2,1)S(1)}, bf16[8,16,256]{2,1,0:T(8,128)(2,1)S(1)}, u32[]{:S(2)}, u32[]{:S(2)}) collective-permute-start(bf16[8,16,256]{2,1,0:T(8,128)(2,1)S(1)} %constant_dynamic-update-slice_fusion), channel_id=1, source_target_pairs={{8,0},{12,4},{0,8},{4,12},{24,16},{28,20},{16,24},{20,28},{9,1},{1... | collective-permute-start | bytes 196616 | tf_op jit(solution)/shard_map/ppermute | solution.py:45
  13.7 4.3 %near.1 = (bf16[128,256,256]{2,1,0:T(8,128)(2,1)S(1)}, f32[32,16,256]{2,1,0:T(8,128)S(1)}, f32[5,16,256]{2,1,0:T(8,128)S(1)}, f32[5,16,256]{2,1,0:T(8,128)S(1)}) custom-call(s32[387]{0:T(512)S(4)} %get-tuple-element.31.refs_0_.table_ref, bf16[128,256,256]{2,1,0:T(8,128)(2,1)} %bitcast.17, ...), custom_call_target="tpu_custom_call", output_to_operand_aliasing={{0}: (2, {})} | custom-call | bytes 8388608 | tf_op jit(solution)/shard_map/near/pallas_call | solution.py:317
  18.0 0.0 collective-permute-done.3.cost_ref
  18.0 0.9 %far.5 = (f32[32,16,256]{2,1,0:T(8,128)S(1)}, f32[5,16,256]{2,1,0:T(8,128)S(1)}, f32[5,16,256]{2,1,0:T(8,128)S(1)}) custom-call(s32[387]{0:T(512)S(4)} %get-tuple-element.31.refs_0_.table_ref, bf16[128,256,256]{2,1,0:T(8,128)(2,1)S(1)} %get-tuple-element.36.held_ref.refs_1_, f32[128,256]{1,0:T(8,128)S(1)} %get-tuple-element.33.refs_3_.tau_ref, ...), custom_call_target="tpu_custom_call" | custom-call | bytes 4194304 | tf_op jit(solution)/shard_map/far/pallas_call | solution.py:331
  18.9 0.0 collective-permute-done.2.cost_ref
  18.9 0.9 %far.4 = (f32[32,16,256]{2,1,0:T(8,128)S(1)}, f32[5,16,256]{2,1,0:T(8,128)S(1)}, f32[5,16,256]{2,1,0:T(8,128)S(1)}) custom-call(s32[387]{0:T(512)S(4)} %get-tuple-element.31.refs_0_.table_ref, bf16[128,256,256]{2,1,0:T(8,128)(2,1)S(1)} %get-tuple-element.36.held_ref.refs_1_, f32[128,256]{1,0:T(8,128)S(1)} %get-tuple-element.33.refs_3_.tau_ref, ...), custom_call_target="tpu_custom_call" | custom-call | bytes 4194304 | tf_op jit(solution)/shard_map/far/pallas_call | solution.py:331
  19.8 0.0 collective-permute-done.1.cost_ref
  19.8 0.9 %far.3 = (f32[32,16,256]{2,1,0:T(8,128)S(1)}, f32[5,16,256]{2,1,0:T(8,128)S(1)}, f32[5,16,256]{2,1,0:T(8,128)S(1)}) custom-call(s32[387]{0:T(512)S(4)} %get-tuple-element.31.refs_0_.table_ref, bf16[128,256,256]{2,1,0:T(8,128)(2,1)S(1)} %get-tuple-element.36.held_ref.refs_1_, f32[128,256]{1,0:T(8,128)S(1)} %get-tuple-element.33.refs_3_.tau_ref, ...), custom_call_target="tpu_custom_call" | custom-call | bytes 4194304 | tf_op jit(solution)/shard_map/far/pallas_call | solution.py:331
  20.7 0.0 copy-start.1
  20.7 0.0 copy-start.2
  20.8 2.5 %adjoint.1 = (bf16[128,16,256]{2,1,0:T(8,128)(2,1)S(1)}, f32[128,256]{1,0:T(8,128)S(1)}, f32[4,16,256]{2,1,0:T(8,128)S(1)}, bf16[16,16,256]{2,1,0:T(8,128)(2,1)S(1)}) custom-call(s32[387]{0:T(512)S(4)} %get-tuple-element.31.refs_0_.table_ref, bf16[128,256,256]{2,1,0:T(8,128)(2,1)S(1)} %get-tuple-element.36.held_ref.refs_1_, ...), custom_call_target="tpu_custom_call" | custom-call | bytes 8388608 | tf_op jit(solution)/shard_map/adjoint/pallas_call | solution.py:344
  23.3 0.1 collective-permute-start.8
  23.3 0.4 %collective-permute-start.4 = (bf16[16,16,256]{2,1,0:T(8,128)(2,1)S(1)}, bf16[16,16,256]{2,1,0:T(8,128)(2,1)S(1)}, u32[]{:S(2)}, u32[]{:S(2)}) collective-permute-start(bf16[16,16,256]{2,1,0:T(8,128)(2,1)S(1)} %get-tuple-element.51), channel_id=1, source_target_pairs={{0,4},{4,0},{8,12},{12,8},{16,20},{20,16},{24,28},{28,24},{1,5},{5... | collective-permute-start | bytes 393224 | tf_op jit(solution)/shard_map/ppermute | solution.py:49
  23.7 2.3 %push.1 = f32[16,16,256]{2,1,0:T(8,128)S(1)} custom-call(s32[387]{0:T(512)S(4)} %get-tuple-element.31.refs_0_.table_ref, bf16[128,256,256]{2,1,0:T(8,128)(2,1)S(1)} %get-tuple-element.36.held_ref.refs_1_, bf16[128,16,256]{2,1,0:T(8,128)(2,1)S(1)} %get-tuple-element.50.adjoint_ref), custom_call_target="tpu_custom_call" | custom-call | bytes 8388608 | tf_op jit(solution)/shard_map/push/pallas_call | solution.py:364
  26.1 0.0 collective-permute-done.8
  26.1 1.7 %collective-permute-start.9 = (f32[128,256]{1,0:T(8,128)S(1)}, f32[128,256]{1,0:T(8,128)S(1)}, u32[]{:S(2)}, u32[]{:S(2)}) collective-permute-start(f32[128,256]{1,0:T(8,128)S(1)} %add.11.refs_8_), channel_id=1, source_target_pairs={{0,2},{1,3},{2,0},{3,1},{4,6},{5,7},{6,4},{7,5},{8,10},{9,11},{10,... | collective-permute-start | bytes 393224 | tf_op jit(solution)/shard_map/ppermute | solution.py:49
  27.8 1.4 %collective-permute-done.4 = bf16[16,16,256]{2,1,0:T(8,128)(2,1)S(1)} collective-permute-done((bf16[16,16,256]{2,1,0:T(8,128)(2,1)S(1)}, bf16[16,16,256]{2,1,0:T(8,128)(2,1)S(1)}, u32[]{:S(2)}, u32[]{:S(2)}) %collective-permute-start.4) | collective-permute-done | bytes 131104 | tf_op jit(solution)/shard_map/ppermute | solution.py:49
  29.3 3.7 %collective-permute-start.5 = (bf16[4,16,256]{2,1,0:T(8,128)(2,1)S(1)}, bf16[4,16,256]{2,1,0:T(8,128)(2,1)S(1)}, u32[]{:S(2)}, u32[]{:S(2)}) collective-permute-start(bf16[4,16,256]{2,1,0:T(8,128)(2,1)S(1)} %get-tuple-element.60), channel_id=1, source_target_pairs={{0,24},{4,28},{8,16},{12,20},{16,8},{20,12},{24,0},{28,4},{1,25},{... | collective-permute-start | bytes 98312 | tf_op jit(solution)/shard_map/ppermute | solution.py:49
  33.0 0.0 collective-permute-start.6
  33.0 0.8 %collective-permute-start.7 = (bf16[4,16,256]{2,1,0:T(8,128)(2,1)S(1)}, bf16[4,16,256]{2,1,0:T(8,128)(2,1)S(1)}, u32[]{:S(2)}, u32[]{:S(2)}) collective-permute-start(bf16[4,16,256]{2,1,0:T(8,128)(2,1)S(1)} %get-tuple-element.58), channel_id=1, source_target_pairs={{0,8},{4,12},{8,0},{12,4},{16,24},{20,28},{24,16},{28,20},{1,9},{5... | collective-permute-start | bytes 98312 | tf_op jit(solution)/shard_map/ppermute | solution.py:49
  33.8 1.3 %collective-permute-done.5.refs_1_ = bf16[4,16,256]{2,1,0:T(8,128)(2,1)S(1)} collective-permute-done((bf16[4,16,256]{2,1,0:T(8,128)(2,1)S(1)}, bf16[4,16,256]{2,1,0:T(8,128)(2,1)S(1)}, u32[]{:S(2)}, u32[]{:S(2)}) %collective-permute-start.5) | collective-permute-done | bytes 32800 | tf_op jit(solution)/shard_map/ppermute | solution.py:49
  35.1 2.7 %collective-permute-done.6.refs_2_ = bf16[4,16,256]{2,1,0:T(8,128)(2,1)S(1)} collective-permute-done((bf16[4,16,256]{2,1,0:T(8,128)(2,1)S(1)}, bf16[4,16,256]{2,1,0:T(8,128)(2,1)S(1)}, u32[]{:S(2)}, u32[]{:S(2)}) %collective-permute-start.6) | collective-permute-done | bytes 32800 | tf_op jit(solution)/shard_map/ppermute | solution.py:49
  37.8 0.0 collective-permute-done.7.refs_3_
  37.8 0.0 collective-permute-done.9.refs_9_
  37.8 0.0 copy-done.1
  37.8 0.0 copy-done.2
  37.8 0.9 %finish.1 = (bf16[4,16,256]{2,1,0:T(8,128)(2,1)}, f32[4,16,256]{2,1,0:T(8,128)}, f32[4,16]{1,0:T(4,128)}, f32[128,256]{1,0:T(8,128)}) custom-call(f32[4,16,256]{2,1,0:T(8,128)S(1)} %slice_bitcast_fusion.refs_0_, bf16[4,16,256]{2,1,0:T(8,128)(2,1)S(1)} %collective-permute-done.5.refs_1_, bf16[4,16,256]{2,1,0:T(8,128)(2,1)S(1)} %collective-permute-done.6.refs_2_, ...), custom_call_target="tpu_custom_call" | custom-call | tf_op jit(solution)/shard_map/finish/pallas_call | solution.py:403
  (7 shorter events, 0.1 us)
Async XLA Ops:
  0.6 0.8 %copy-start = (bf16[4,16,256]{2,1,0:T(8,128)(2,1)S(1)}, bf16[4,16,256]{2,1,0:T(8,128)(2,1)}, u32[]{:S(2)}) copy-start(bf16[4,16,256]{2,1,0:T(8,128)(2,1)} %param.10) | copy-start | bytes 98308
  2.6 6.6 %collective-permute-start = (bf16[4,16,256]{2,1,0:T(8,128)(2,1)S(1)}, bf16[4,16,256]{2,1,0:T(8,128)(2,1)S(1)}, u32[]{:S(2)}, u32[]{:S(2)}) collective-permute-start(bf16[4,16,256]{2,1,0:T(8,128)(2,1)S(1)} %fusion.cost_ref), channel_id=1, source_target_pairs={{4,0},{0,4},{12,8},{8,12},{20,16},{16,20},{28,24},{24,28},{5,1},{1... | collective-permute-start | bytes 98312 | tf_op jit(solution)/shard_map/ppermute | solution.py:45
  9.3 8.7 %collective-permute-start.3 = (bf16[8,16,256]{2,1,0:T(8,128)(2,1)S(1)}, bf16[8,16,256]{2,1,0:T(8,128)(2,1)S(1)}, u32[]{:S(2)}, u32[]{:S(2)}) collective-permute-start(bf16[8,16,256]{2,1,0:T(8,128)(2,1)S(1)} %constant_dynamic-update-slice_fusion), channel_id=1, source_target_pairs={{24,0},{28,4},{16,8},{20,12},{8,16},{12,20},{0,24},{4,28},{25,1},{... | collective-permute-start | bytes 196616 | tf_op jit(solution)/shard_map/ppermute | solution.py:45
  12.9 6.0 %collective-permute-start.2 = (bf16[8,16,256]{2,1,0:T(8,128)(2,1)S(1)}, bf16[8,16,256]{2,1,0:T(8,128)(2,1)S(1)}, u32[]{:S(2)}, u32[]{:S(2)}) collective-permute-start(bf16[8,16,256]{2,1,0:T(8,128)(2,1)S(1)} %constant_dynamic-update-slice_fusion), channel_id=1, source_target_pairs={{16,0},{20,4},{24,8},{28,12},{0,16},{4,20},{8,24},{12,28},{17,1},{... | collective-permute-start | bytes 196616 | tf_op jit(solution)/shard_map/ppermute | solution.py:45
  12.9 6.9 %collective-permute-start.1 = (bf16[8,16,256]{2,1,0:T(8,128)(2,1)S(1)}, bf16[8,16,256]{2,1,0:T(8,128)(2,1)S(1)}, u32[]{:S(2)}, u32[]{:S(2)}) collective-permute-start(bf16[8,16,256]{2,1,0:T(8,128)(2,1)S(1)} %constant_dynamic-update-slice_fusion), channel_id=1, source_target_pairs={{8,0},{12,4},{0,8},{4,12},{24,16},{28,20},{16,24},{20,28},{9,1},{1... | collective-permute-start | bytes 196616 | tf_op jit(solution)/shard_map/ppermute | solution.py:45
  20.7 17.1 %copy-start.1 = (bf16[4,256,256]{2,1,0:T(8,128)(2,1)S(1)}, bf16[4,256,256]{2,1,0:T(8,128)(2,1)}, u32[]{:S(2)}) copy-start(bf16[4,256,256]{2,1,0:T(8,128)(2,1)} %refs_4_.1) | copy-start | bytes 1572868
  20.7 17.1 %copy-start.2 = (f32[4,256]{1,0:T(4,128)S(1)}, f32[4,256]{1,0:T(4,128)}, u32[]{:S(2)}) copy-start(f32[4,256]{1,0:T(4,128)} %refs_5_.1) | copy-start | bytes 12292
  23.3 2.8 %collective-permute-start.8 = (f32[128,256]{1,0:T(8,128)S(1)}, f32[128,256]{1,0:T(8,128)S(1)}, u32[]{:S(2)}, u32[]{:S(2)}) collective-permute-start(f32[128,256]{1,0:T(8,128)S(1)} %get-tuple-element.53), channel_id=1, source_target_pairs={{0,1},{1,0},{2,3},{3,2},{4,5},{5,4},{6,7},{7,6},{8,9},{9,8},{10,11... | collective-permute-start | bytes 393224 | tf_op jit(solution)/shard_map/ppermute | solution.py:49
  23.3 5.9 %collective-permute-start.4 = (bf16[16,16,256]{2,1,0:T(8,128)(2,1)S(1)}, bf16[16,16,256]{2,1,0:T(8,128)(2,1)S(1)}, u32[]{:S(2)}, u32[]{:S(2)}) collective-permute-start(bf16[16,16,256]{2,1,0:T(8,128)(2,1)S(1)} %get-tuple-element.51), channel_id=1, source_target_pairs={{0,4},{4,0},{8,12},{12,8},{16,20},{20,16},{24,28},{28,24},{1,5},{5... | collective-permute-start | bytes 393224 | tf_op jit(solution)/shard_map/ppermute | solution.py:49
  26.1 11.7 %collective-permute-start.9 = (f32[128,256]{1,0:T(8,128)S(1)}, f32[128,256]{1,0:T(8,128)S(1)}, u32[]{:S(2)}, u32[]{:S(2)}) collective-permute-start(f32[128,256]{1,0:T(8,128)S(1)} %add.11.refs_8_), channel_id=1, source_target_pairs={{0,2},{1,3},{2,0},{3,1},{4,6},{5,7},{6,4},{7,5},{8,10},{9,11},{10,... | collective-permute-start | bytes 393224 | tf_op jit(solution)/shard_map/ppermute | solution.py:49
  29.3 5.8 %collective-permute-start.5 = (bf16[4,16,256]{2,1,0:T(8,128)(2,1)S(1)}, bf16[4,16,256]{2,1,0:T(8,128)(2,1)S(1)}, u32[]{:S(2)}, u32[]{:S(2)}) collective-permute-start(bf16[4,16,256]{2,1,0:T(8,128)(2,1)S(1)} %get-tuple-element.60), channel_id=1, source_target_pairs={{0,24},{4,28},{8,16},{12,20},{16,8},{20,12},{24,0},{28,4},{1,25},{... | collective-permute-start | bytes 98312 | tf_op jit(solution)/shard_map/ppermute | solution.py:49
  33.0 4.8 %collective-permute-start.6 = (bf16[4,16,256]{2,1,0:T(8,128)(2,1)S(1)}, bf16[4,16,256]{2,1,0:T(8,128)(2,1)S(1)}, u32[]{:S(2)}, u32[]{:S(2)}) collective-permute-start(bf16[4,16,256]{2,1,0:T(8,128)(2,1)S(1)} %get-tuple-element.59), channel_id=1, source_target_pairs={{0,16},{4,20},{8,24},{12,28},{16,0},{20,4},{24,8},{28,12},{1,17},{... | collective-permute-start | bytes 98312 | tf_op jit(solution)/shard_map/ppermute | solution.py:49
  33.0 4.8 %collective-permute-start.7 = (bf16[4,16,256]{2,1,0:T(8,128)(2,1)S(1)}, bf16[4,16,256]{2,1,0:T(8,128)(2,1)S(1)}, u32[]{:S(2)}, u32[]{:S(2)}) collective-permute-start(bf16[4,16,256]{2,1,0:T(8,128)(2,1)S(1)} %get-tuple-element.58), channel_id=1, source_target_pairs={{0,8},{4,12},{8,0},{12,4},{16,24},{20,28},{24,16},{28,20},{1,9},{5... | collective-permute-start | bytes 98312 | tf_op jit(solution)/shard_map/ppermute | solution.py:49

commit v4 on v3

--- a/solution.py
+++ b/solution.py
@@ -68,18 +68,53 @@
 class Entries:
     def __init__(self, own, slots, reg_count):
         self.own, self.slots, self.reg_count = own, slots, reg_count
-        self.capacity = -(-own * slots // reg_count)
+        self.slot_count = own * slots
+        self.dense = reg_count * own <= slots
+        self.capacity = own * own if self.dense else -(-own * slots // reg_count)
         self.count = self.capacity * reg_count
         self.stride = self.count + 1
+        self.columns = 2 if self.dense else 4
 
     def slot(self, table, entry):
         return table[entry]
 
+    def row(self, table, entry):
+        return table[self.stride + entry]
+
+    def live(self, table, entry):
+        return self.row(table, entry) < self.slot_count
+
     def importer(self, table, entry):
-        return table[self.stride + entry]
+        return entry % self.capacity // self.own if self.dense else table[2 * self.stride + entry]
 
     def place(self, table, entry):
-        return table[2 * self.stride + entry]
+        return entry % self.own if self.dense else table[3 * self.stride + entry]
+
+    def fill(self, table, found, partners, lengths, me):
+        own = self.own
+        for entry in range(self.stride):
+            for column, value in enumerate((0, self.slot_count, own, 0)[: self.columns]):
+                table[column * self.stride + entry] = value
+        if not self.dense:
+            for distance in range(self.reg_count):
+                found[distance] = 0
+        for r in range(own):
+            length = lengths[me * own + r]
+            for s in range(self.slots):
+                partner = partners[me * own + r, s]
+                distance = distance_of(lax.div(partner, own), me, self.reg_count)
+                place = lax.rem(partner, own)
+                slot = r * self.slots + s
+                if self.dense:
+                    entry = distance * self.capacity + r * own + place
+                    columns = (slot, slot)
+                else:
+                    entry = distance * self.capacity + found[distance]
+                    columns = (slot, slot, r, place)
+                    found[distance] += (s < length).astype(jnp.int32)
+                entry = jnp.minimum(jnp.where(s < length, entry, self.count), self.count)
+                for column, value in enumerate(columns):
+                    table[column * self.stride + entry] = value
 
 
 def load_kernel(
@@ -87,8 +122,6 @@
     held_ref, tau_ref, cotangent_ref, elasticity_ref, cost_copy_ref, table_ref,
     partners_ref, lengths_ref, found_ref, sems,
 ):
-    own, slots, n, capacity = entries.own, entries.slots, entries.reg_count, entries.capacity
-    first = held_ref.shape[0] // 2
     copies = [
         pltpu.make_async_copy(source, target, sems.at[i])
         for i, (source, target) in enumerate(
@@ -98,55 +131,61 @@
                 (tau, tau_ref),
                 (cotangent, cotangent_ref),
                 (elasticity, elasticity_ref),
-                (blocks.at[pl.ds(0, first)], held_ref.at[pl.ds(0, first)]),
+                (blocks.at[pl.ds(0, entries.slots)], held_ref.at[pl.ds(0, entries.slots)]),
             )
         )
     ]
     for copy in copies:
         copy.start()
     cost_copy_ref[...] = cost_ref[...]
-    for entry in range(entries.stride):
-        table_ref[entry] = 0
-        table_ref[entries.stride + entry] = own
-        table_ref[2 * entries.stride + entry] = 0
-    for distance in range(n):
-        found_ref[distance] = 0
     copies[0].wait()
     copies[1].wait()
-    me = me_ref[0]
-    for r in range(own):
-        length = lengths_ref[me * own + r]
-        for s in range(slots):
-            partner = partners_ref[me * own + r, s]
-            distance = distance_of(lax.div(partner, own), me, n)
-            found = found_ref[distance]
-            entry = jnp.where(s < length, distance * capacity + found, entries.count)
-            entry = jnp.minimum(entry, entries.count)
-            table_ref[entry] = r * slots + s
-            table_ref[entries.stride + entry] = r
-            table_ref[2 * entries.stride + entry] = lax.rem(partner, own)
-            found_ref[distance] = found + (s < length).astype(jnp.int32)
+    entries.fill(table_ref, found_ref, partners_ref, lengths_ref, me_ref[0])
     for copy in copies[2:]:
         copy.wait()
 
 
-def score_entries(entries, first, table_ref, costs, held_ref, tau_ref, elasticity_ref, weights_ref, top_ref, norm_ref):
+def score_entries(
+    entries, first, table_ref, costs, held_ref, tau_ref, elasticity_ref, weights_ref, top_ref, norm_ref, arrive=lambda r: None
+):
     own, capacity = entries.own, entries.capacity
+    count = weights_ref.shape[0]
     scale = -elasticity_ref[...]
-    top_ref[...] = jnp.full(top_ref.shape, LOWEST, F32)
-    norm_ref[...] = jnp.zeros(norm_ref.shape, F32)
+    lowest = jnp.full(top_ref.shape[1:], LOWEST, F32)
+    zero = jnp.zeros(top_ref.shape[1:], F32)
     rows = [(ref, block) for ref in costs for block in range(ref.shape[0] // own)]
-    for i in range(weights_ref.shape[0]):
+
+    def score(i):
         entry = first * capacity + i
         ref, block = rows[i // capacity]
         slot = entries.slot(table_ref, entry)
-        importer = entries.importer(table_ref, entry)
         cost = ref[block * own + entries.place(table_ref, entry)]
         landed = jnp.dot(cost, held_ref[slot], preferred_element_type=F32) + tau_ref[pl.ds(slot, 1)]
-        score = scale * landed
-        weights_ref[i] = score
-        top_ref[importer] = jnp.maximum(top_ref[importer], score)
-    for i in range(weights_ref.shape[0]):
+        return scale * landed
+
+    if entries.dense:
+        for r in range(own):
+            arrive(r)
+            members = [i for i in range(count) if entries.importer(table_ref, i) == r]
+            scores = [jnp.where(entries.live(table_ref, first * capacity + i), score(i), -jnp.inf) for i in members]
+            top = functools.reduce(jnp.maximum, scores, lowest)
+            norm = zero
+            for i, value in zip(members, scores):
+                weight = jnp.exp(value - top)
+                weights_ref[i] = weight
+                norm = norm + weight
+            top_ref[r] = top
+            norm_ref[r] = norm
+        return
+    arrive(None)
+    top_ref[...] = jnp.full(top_ref.shape, LOWEST, F32)
+    norm_ref[...] = jnp.zeros(norm_ref.shape, F32)
+    for i in range(count):
+        importer = entries.importer(table_ref, first * capacity + i)
+        value = score(i)
+        weights_ref[i] = value
+        top_ref[importer] = jnp.maximum(top_ref[importer], value)
+    for i in range(count):
         importer = entries.importer(table_ref, first * capacity + i)
         weight = jnp.exp(weights_ref[i] - top_ref[importer])
         weights_ref[i] = weight
@@ -156,13 +195,22 @@
 def near_kernel(entries, n_costs, *refs):
     table_ref, blocks, _, tau_ref, elasticity_ref = refs[:5]
     costs = refs[5 : 5 + n_costs]
-    held_ref, weights_ref, top_ref, norm_ref, sem = refs[5 + n_costs :]
-    first = held_ref.shape[0] // 2
-    rest = held_ref.shape[0] - first
-    copy = pltpu.make_async_copy(blocks.at[pl.ds(first, rest)], held_ref.at[pl.ds(first, rest)], sem)
-    copy.start()
-    copy.wait()
-    score_entries(entries, 0, table_ref, costs, held_ref, tau_ref, elasticity_ref, weights_ref, top_ref, norm_ref)
+    held_ref, weights_ref, top_ref, norm_ref, sems = refs[5 + n_costs :]
+    own, slots = entries.own, entries.slots
+    copies = [
+        pltpu.make_async_copy(blocks.at[pl.ds(r * slots, slots)], held_ref.at[pl.ds(r * slots, slots)], sems.at[r])
+        for r in range(1, own)
+    ]
+    for copy in copies:
+        copy.start()
+
+    def arrive(r):
+        for copy in copies if r is None else copies[r - 1 : r] if r else []:
+            copy.wait()
+
+    score_entries(
+        entries, 0, table_ref, costs, held_ref, tau_ref, elasticity_ref, weights_ref, top_ref, norm_ref, arrive
+    )
 
 
 def far_kernel(entries, first, table_ref, held_ref, tau_ref, elasticity_ref, cost_ref, weights_ref, top_ref, norm_ref):
@@ -170,24 +218,36 @@
 
 
 def push_entries(entries, distances, table_ref, adjoint_of, held_ref, total_ref):
-    total_ref[...] = jnp.zeros(total_ref.shape, F32)
+    own, capacity = entries.own, entries.capacity
+
+    def pushed(entry):
+        return lax.dot_general(
+            adjoint_of(entry),
+            held_ref[entries.slot(table_ref, entry)],
+            CONTRACT_LAST,
+            preferred_element_type=F32,
+        )
+
+    if entries.dense:
+        for block, distance in enumerate(distances):
+            for place in range(own):
+                terms = [pushed(distance * capacity + r * own + place) for r in range(own)]
+                total_ref[block * own + place] = sum(terms[1:], terms[0]).astype(total_ref.dtype)
+        return
+    total_ref[...] = jnp.zeros(total_ref.shape, total_ref.dtype)
     for block, distance in enumerate(distances):
-        for entry in range(distance * entries.capacity, (distance + 1) * entries.capacity):
-            total_ref[block * entries.own + entries.place(table_ref, entry)] += lax.dot_general(
-                adjoint_of(entry),
-                held_ref[entries.slot(table_ref, entry)],
-                CONTRACT_LAST,
-                preferred_element_type=F32,
-            )
-
-
-def adjoint_kernel(entries, n, distances, *refs):
+        for entry in range(distance * capacity, (distance + 1) * capacity):
+            total_ref[block * own + entries.place(table_ref, entry)] += pushed(entry)
+
+
+def adjoint_kernel(entries, order, distances, *refs):
+    n = len(order)
     table_ref, held_ref, cotangent_ref = refs[:3]
-    weights, tops, norms = refs[3 : 3 + n], refs[3 + n : 3 + 2 * n], refs[3 + 2 * n : 3 + 3 * n]
-    adjoint_ref, tau_grad_ref, logsum_ref, partial_ref, factor_ref, total_ref = refs[3 + 3 * n :]
+    weights, tops, norms = ([refs[3 + c * n + order.index(k)] for k in range(n)] for c in range(3))
+    adjoint_ref, tau_grad_ref, logsum_ref, partial_ref, factor_ref, tau_rows_ref, total_ref = refs[3 + 3 * n :]
     own, capacity = entries.own, entries.capacity
     piece = weights[0].shape[0]
-    tau_grad_ref[...] = jnp.zeros(tau_grad_ref.shape, F32)
+    tau_rows_ref[...] = jnp.zeros(tau_rows_ref.shape, F32)
     for r in range(own):
         top = functools.reduce(jnp.maximum, [ref[r] for ref in tops])
         shrink = [jnp.exp(ref[r] - top) for ref in tops]
@@ -202,7 +262,7 @@
     def adjoint(entry):
         k, i = divmod(entry, piece)
         value = factor_ref[k, entries.importer(table_ref, entry)] * weights[k][i]
-        tau_grad_ref[pl.ds(entries.slot(table_ref, entry), 1)] += jnp.sum(value, axis=0, keepdims=True)
+        tau_rows_ref[pl.ds(entries.row(table_ref, entry), 1)] = jnp.sum(value, axis=0, keepdims=True)
         return value.astype(BF16)
 
     push_entries(entries, distances, table_ref, adjoint, held_ref, total_ref)
@@ -210,6 +270,7 @@
     for entry in range(entries.count):
         if entry // capacity not in distances:
             adjoint_ref[entry] = adjoint(entry)
+    tau_grad_ref[...] = tau_rows_ref[pl.ds(0, entries.slot_count)]
 
 
 def push_kernel(entries, distances, table_ref, held_ref, adjoint_ref, partial_ref, total_ref):
@@ -270,7 +331,7 @@
             shape(price_cotangent.shape, F32),
             shape((1, sectors), F32),
             shape(unit_cost.shape, BF16),
-            pltpu.SMEM((3 * entries.stride,), jnp.int32),
+            pltpu.SMEM((entries.columns * entries.stride,), jnp.int32),
         ),
         in_specs=[SMEM, VMEM] + [HBM] * 6,
         out_specs=(VMEM,) * 5 + (SMEM,),
@@ -319,7 +380,7 @@
         out_shape=(shape(blocks.shape, BF16),) + scored(piece),
         in_specs=[SMEM, HBM] + [VMEM] * (3 + len(near)),
         out_specs=(VMEM,) * 4,
-        scratch_shapes=[pltpu.SemaphoreType.DMA],
+        scratch_shapes=[pltpu.SemaphoreType.DMA((own,))],
         input_output_aliases={2: 0},
         compiler_params=params(2),
         cost_estimate=effort(blocks.size),
@@ -338,11 +399,12 @@
                 name="far",
             )(table, held, tau, elastic, cost)
         )
+    order = [0, *range(2, last_radix), 1]
     radix = stages[0]
     groups = [range(j, reg_count, radix) for j in range(radix)]
     partial_dims = (reg_count // radix * own,) + row
     adjoint, tau_grad, logsum, partial = pl.pallas_call(
-        functools.partial(adjoint_kernel, entries, last_radix, groups[-1]),
+        functools.partial(adjoint_kernel, entries, order, groups[-1]),
         out_shape=(
             shape((entries.count,) + row, BF16),
             shape((own * slots, sectors), F32),
@@ -353,12 +415,13 @@
         out_specs=(VMEM,) * 4,
         scratch_shapes=[
             pltpu.VMEM((last_radix, own + 1) + row, F32),
+            pltpu.VMEM((own * slots + 8, sectors), F32),
             pltpu.VMEM(partial_dims, F32),
         ],
         compiler_params=params(8),
         cost_estimate=effort(blocks.size),
         name="adjoint",
-    )(table, held, cotangent, *[s[0] for s in scores], *[s[1] for s in scores], *[s[2] for s in scores])
+    )(table, held, cotangent, *[scores[k][c] for c in range(3) for k in order])
 
     def push(j, dtype):
         return pl.pallas_call(

time: 39 us -> 37.4 us (0.959)
  waiting for transfers between devices: 5.48 us -> 4.21 us
  Pallas kernels: 16.3 us -> 15.3 us
  starting transfers between devices: 14.1 us -> 14.8 us
    ppermute x6, waiting for transfers between devices: 5.47 us -> 4.2 us  [to_peer(): return lax.ppermute(x, axis, [(i, peer(i, distance, n)) for i in range(n)])]
    pallas_call x1, Pallas kernels: 3.57 us -> 2.37 us  [shards(): pl.pallas_call(functools.partial(load_kernel, entries), out_shape=(shape(...]
    ppermute x6, starting transfers between devices: 6.63 us -> 7.51 us  [to_peer(): return lax.ppermute(x, axis, [(i, peer(i, distance, n)) for i in range(n)])]
    pallas_call x1, Pallas kernels: 4.28 us -> 4.98 us  [shards(): pl.pallas_call(functools.partial(near_kernel, entries, len(near)), out_sh...]
    pallas_call x3, Pallas kernels: 2.71 us -> 2.11 us  [shards(): pl.pallas_call(functools.partial(far_kernel, entries, j * last_stride), o...]
  transfers between devices with their start and end apart: 10 -> 10, of which waited for: 3 -> 3; matrix products, arithmetic and copies ran while one was open for 0% -> 0% of each run, Pallas kernels for 31% -> 30%
where the time goes in v4:
time: 37.4 us; the launch traced here: 37.1 us
  Pallas kernels  15.3 us (41%)
  starting transfers between devices  14.8 us (40%)
  waiting for transfers between devices  4.21 us (11%)
  matrix products  1.24 us (3%)
  local copies, waits for them, and re-layouts  0.79 us (2%)
  between operations  0.79 us (2%)
    ppermute x6, starting transfers between devices, to_peer(): return lax.ppermute(x, axis, [(i, peer(i, distance, n)) for i in range(n)])  7.51 us
    ppermute x4, starting transfers between devices, from_peer(): return lax.ppermute(x, axis, [(peer(i, distance, n), i) for i in range(n)])  7.25 us
    pallas_call x1, Pallas kernels, shards(): pl.pallas_call(functools.partial(near_kernel, entries, len(near)), out_sh...  4.98 us
    ppermute x6, waiting for transfers between devices, to_peer(): return lax.ppermute(x, axis, [(i, peer(i, distance, n)) for i in range(n)])  4.2 us
    pallas_call x1, Pallas kernels, shards(): pl.pallas_call(functools.partial(adjoint_kernel, entries, order, groups[-...  2.65 us
    pallas_call x1, Pallas kernels, shards(): pl.pallas_call(functools.partial(load_kernel, entries), out_shape=(shape(...  2.37 us
    pallas_call x1, Pallas kernels, push(): pl.pallas_call(functools.partial(push_kernel, entries, groups[j]), out_sh...  2.26 us
    pallas_call x3, Pallas kernels, shards(): pl.pallas_call(functools.partial(far_kernel, entries, j * last_stride), o...  2.11 us
  transfers between devices with their start and end apart: 10, of which 3 were waited for; matrix products, arithmetic and copies ran while one was open for 0% of the time, Pallas kernels for 30%

profile of v4, /device:TPU:0, one launch (start us, length us, event | category | flops | bytes accessed | tf_op | source)
XLA Modules:
  0.0 37.1 jit_solution(5304899583183178253)
XLA Ops:
  0.6 0.0 copy-start
  0.6 0.7 %copy-done = bf16[4,16,256]{2,1,0:T(8,128)(2,1)S(1)} copy-done((bf16[4,16,256]{2,1,0:T(8,128)(2,1)S(1)}, bf16[4,16,256]{2,1,0:T(8,128)(2,1)}, u32[]{:S(2)}) %copy-start) | copy-done | bytes 32792
  1.4 1.2 %fusion.cost_ref = bf16[4,16,256]{2,1,0:T(8,128)(2,1)S(1)} fusion(bf16[4,16,256]{2,1,0:T(8,128)(2,1)S(1)} %copy-done, bf16[4,256,256]{2,1,0:T(8,128)(2,1)} %refs_4_.1, f32[4,16]{1,0:T(4,128)} %param.11, f32[4,256]{1,0:T(4,128)} %refs_5_.1), kind=kOutput, calls=%fused_computation.1 | convolution fusion | flops 8437760 | bytes 594176 | tf_op jit(solution)/shard_map/iek,ikj->iej/dot_general | solution.py:323
  2.6 3.0 %collective-permute-start = (bf16[4,16,256]{2,1,0:T(8,128)(2,1)S(1)}, bf16[4,16,256]{2,1,0:T(8,128)(2,1)S(1)}, u32[]{:S(2)}, u32[]{:S(2)}) collective-permute-start(bf16[4,16,256]{2,1,0:T(8,128)(2,1)S(1)} %fusion.cost_ref), channel_id=1, source_target_pairs={{4,0},{0,4},{12,8},{8,12},{20,16},{16,20},{28,24},{24,28},{5,1},{1... | collective-permute-start | bytes 98312 | tf_op jit(solution)/shard_map/ppermute | solution.py:45
  5.6 2.4 %load.1 = (bf16[128,256,256]{2,1,0:T(8,128)(2,1)S(1)}, f32[128,256]{1,0:T(8,128)S(1)}, f32[4,16,256]{2,1,0:T(8,128)S(1)}, f32[1,256]{1,0:T(1,128)S(1)}, bf16[4,16,256]{2,1,0:T(8,128)(2,1)S(1)}, /*index=5*/s32[258]{0:T(512)S(4)}) custom-call(s32[1]{0:T(128)} %bitcast.me_ref, bf16[4,16,256]{2,1,0:T(8,128)(2,1)S(1)} %fusion.cost_ref, ...), custom_call_target="tpu_custom_call" | custom-call | bytes 8388608 | tf_op jit(solution)/shard_map/load/pallas_call | solution.py:326
  8.0 0.0 collective-permute-done.refs_6_
  8.1 1.6 %collective-permute-start.3 = (bf16[8,16,256]{2,1,0:T(8,128)(2,1)S(1)}, bf16[8,16,256]{2,1,0:T(8,128)(2,1)S(1)}, u32[]{:S(2)}, u32[]{:S(2)}) collective-permute-start(bf16[8,16,256]{2,1,0:T(8,128)(2,1)S(1)} %constant_dynamic-update-slice_fusion), channel_id=1, source_target_pairs={{8,0},{12,4},{0,8},{4,12},{24,16},{28,20},{16,24},{20,28},{9,1},{1... | collective-permute-start | bytes 196616 | tf_op jit(solution)/shard_map/ppermute | solution.py:45
  9.7 2.5 %collective-permute-start.2 = (bf16[8,16,256]{2,1,0:T(8,128)(2,1)S(1)}, bf16[8,16,256]{2,1,0:T(8,128)(2,1)S(1)}, u32[]{:S(2)}, u32[]{:S(2)}) collective-permute-start(bf16[8,16,256]{2,1,0:T(8,128)(2,1)S(1)} %constant_dynamic-update-slice_fusion), channel_id=1, source_target_pairs={{24,0},{28,4},{16,8},{20,12},{8,16},{12,20},{0,24},{4,28},{25,1},{... | collective-permute-start | bytes 196616 | tf_op jit(solution)/shard_map/ppermute | solution.py:45
  12.2 0.1 collective-permute-start.1
  12.3 5.0 %near.1 = (bf16[128,256,256]{2,1,0:T(8,128)(2,1)S(1)}, f32[32,16,256]{2,1,0:T(8,128)S(1)}, f32[5,16,256]{2,1,0:T(8,128)S(1)}, f32[5,16,256]{2,1,0:T(8,128)S(1)}) custom-call(s32[258]{0:T(512)S(4)} %get-tuple-element.31.refs_0_.table_ref, bf16[128,256,256]{2,1,0:T(8,128)(2,1)} %bitcast.17, ...), custom_call_target="tpu_custom_call", output_to_operand_aliasing={{0}: (2, {})} | custom-call | bytes 8388608 | tf_op jit(solution)/shard_map/near/pallas_call | solution.py:378
  17.3 0.0 collective-permute-done.3.cost_ref
  17.3 0.7 %far.5 = (f32[32,16,256]{2,1,0:T(8,128)S(1)}, f32[5,16,256]{2,1,0:T(8,128)S(1)}, f32[5,16,256]{2,1,0:T(8,128)S(1)}) custom-call(s32[258]{0:T(512)S(4)} %get-tuple-element.31.refs_0_.table_ref, bf16[128,256,256]{2,1,0:T(8,128)(2,1)S(1)} %get-tuple-element.36.held_ref.refs_1_, f32[128,256]{1,0:T(8,128)S(1)} %get-tuple-element.33.refs_3_.tau_ref, ...), custom_call_target="tpu_custom_call" | custom-call | bytes 4194304 | tf_op jit(solution)/shard_map/far/pallas_call | solution.py:392
  18.0 0.0 collective-permute-done.2.cost_ref
  18.0 0.7 %far.4 = (f32[32,16,256]{2,1,0:T(8,128)S(1)}, f32[5,16,256]{2,1,0:T(8,128)S(1)}, f32[5,16,256]{2,1,0:T(8,128)S(1)}) custom-call(s32[258]{0:T(512)S(4)} %get-tuple-element.31.refs_0_.table_ref, bf16[128,256,256]{2,1,0:T(8,128)(2,1)S(1)} %get-tuple-element.36.held_ref.refs_1_, f32[128,256]{1,0:T(8,128)S(1)} %get-tuple-element.33.refs_3_.tau_ref, ...), custom_call_target="tpu_custom_call" | custom-call | bytes 4194304 | tf_op jit(solution)/shard_map/far/pallas_call | solution.py:392
  18.7 0.0 collective-permute-done.1.cost_ref
  18.7 0.7 %far.3 = (f32[32,16,256]{2,1,0:T(8,128)S(1)}, f32[5,16,256]{2,1,0:T(8,128)S(1)}, f32[5,16,256]{2,1,0:T(8,128)S(1)}) custom-call(s32[258]{0:T(512)S(4)} %get-tuple-element.31.refs_0_.table_ref, bf16[128,256,256]{2,1,0:T(8,128)(2,1)S(1)} %get-tuple-element.36.held_ref.refs_1_, f32[128,256]{1,0:T(8,128)S(1)} %get-tuple-element.33.refs_3_.tau_ref, ...), custom_call_target="tpu_custom_call" | custom-call | bytes 4194304 | tf_op jit(solution)/shard_map/far/pallas_call | solution.py:392
  19.4 0.0 copy-start.1
  19.5 0.0 copy-start.2
  19.5 2.7 %adjoint.1 = (bf16[128,16,256]{2,1,0:T(8,128)(2,1)S(1)}, f32[128,256]{1,0:T(8,128)S(1)}, f32[4,16,256]{2,1,0:T(8,128)S(1)}, bf16[16,16,256]{2,1,0:T(8,128)(2,1)S(1)}) custom-call(s32[258]{0:T(512)S(4)} %get-tuple-element.31.refs_0_.table_ref, bf16[128,256,256]{2,1,0:T(8,128)(2,1)S(1)} %get-tuple-element.36.held_ref.refs_1_, ...), custom_call_target="tpu_custom_call" | custom-call | bytes 8388608 | tf_op jit(solution)/shard_map/adjoint/pallas_call | solution.py:406
  22.1 0.0 collective-permute-start.8
  22.1 1.5 %collective-permute-start.4 = (bf16[16,16,256]{2,1,0:T(8,128)(2,1)S(1)}, bf16[16,16,256]{2,1,0:T(8,128)(2,1)S(1)}, u32[]{:S(2)}, u32[]{:S(2)}) collective-permute-start(bf16[16,16,256]{2,1,0:T(8,128)(2,1)S(1)} %get-tuple-element.51), channel_id=1, source_target_pairs={{0,4},{4,0},{8,12},{12,8},{16,20},{20,16},{24,28},{28,24},{1,5},{5... | collective-permute-start | bytes 393224 | tf_op jit(solution)/shard_map/ppermute | solution.py:49
  23.6 2.3 %push.1 = f32[16,16,256]{2,1,0:T(8,128)S(1)} custom-call(s32[258]{0:T(512)S(4)} %get-tuple-element.31.refs_0_.table_ref, bf16[128,256,256]{2,1,0:T(8,128)(2,1)S(1)} %get-tuple-element.36.held_ref.refs_1_, bf16[128,16,256]{2,1,0:T(8,128)(2,1)S(1)} %get-tuple-element.50.adjoint_ref), custom_call_target="tpu_custom_call" | custom-call | bytes 8388608 | tf_op jit(solution)/shard_map/push/pallas_call | solution.py:427
  25.9 0.0 collective-permute-done.8
  25.9 1.6 %collective-permute-start.9 = (f32[128,256]{1,0:T(8,128)S(1)}, f32[128,256]{1,0:T(8,128)S(1)}, u32[]{:S(2)}, u32[]{:S(2)}) collective-permute-start(f32[128,256]{1,0:T(8,128)S(1)} %add.11.refs_8_), channel_id=1, source_target_pairs={{0,2},{1,3},{2,0},{3,1},{4,6},{5,7},{6,4},{7,5},{8,10},{9,11},{10,... | collective-permute-start | bytes 393224 | tf_op jit(solution)/shard_map/ppermute | solution.py:49
  27.5 0.6 %collective-permute-done.4 = bf16[16,16,256]{2,1,0:T(8,128)(2,1)S(1)} collective-permute-done((bf16[16,16,256]{2,1,0:T(8,128)(2,1)S(1)}, bf16[16,16,256]{2,1,0:T(8,128)(2,1)S(1)}, u32[]{:S(2)}, u32[]{:S(2)}) %collective-permute-start.4) | collective-permute-done | bytes 131104 | tf_op jit(solution)/shard_map/ppermute | solution.py:49
  28.1 3.0 %collective-permute-start.5 = (bf16[4,16,256]{2,1,0:T(8,128)(2,1)S(1)}, bf16[4,16,256]{2,1,0:T(8,128)(2,1)S(1)}, u32[]{:S(2)}, u32[]{:S(2)}) collective-permute-start(bf16[4,16,256]{2,1,0:T(8,128)(2,1)S(1)} %get-tuple-element.60), channel_id=1, source_target_pairs={{0,24},{4,28},{8,16},{12,20},{16,8},{20,12},{24,0},{28,4},{1,25},{... | collective-permute-start | bytes 98312 | tf_op jit(solution)/shard_map/ppermute | solution.py:49
  31.1 0.3 collective-permute-start.6
  31.5 1.1 %collective-permute-start.7 = (bf16[4,16,256]{2,1,0:T(8,128)(2,1)S(1)}, bf16[4,16,256]{2,1,0:T(8,128)(2,1)S(1)}, u32[]{:S(2)}, u32[]{:S(2)}) collective-permute-start(bf16[4,16,256]{2,1,0:T(8,128)(2,1)S(1)} %get-tuple-element.58), channel_id=1, source_target_pairs={{0,8},{4,12},{8,0},{12,4},{16,24},{20,28},{24,16},{28,20},{1,9},{5... | collective-permute-start | bytes 98312 | tf_op jit(solution)/shard_map/ppermute | solution.py:49
  32.6 1.3 %collective-permute-done.5.refs_1_ = bf16[4,16,256]{2,1,0:T(8,128)(2,1)S(1)} collective-permute-done((bf16[4,16,256]{2,1,0:T(8,128)(2,1)S(1)}, bf16[4,16,256]{2,1,0:T(8,128)(2,1)S(1)}, u32[]{:S(2)}, u32[]{:S(2)}) %collective-permute-start.5) | collective-permute-done | bytes 32800 | tf_op jit(solution)/shard_map/ppermute | solution.py:49
  33.9 2.3 %collective-permute-done.6.refs_2_ = bf16[4,16,256]{2,1,0:T(8,128)(2,1)S(1)} collective-permute-done((bf16[4,16,256]{2,1,0:T(8,128)(2,1)S(1)}, bf16[4,16,256]{2,1,0:T(8,128)(2,1)S(1)}, u32[]{:S(2)}, u32[]{:S(2)}) %collective-permute-start.6) | collective-permute-done | bytes 32800 | tf_op jit(solution)/shard_map/ppermute | solution.py:49
  36.2 0.0 collective-permute-done.7.refs_3_
  36.2 0.0 collective-permute-done.9.refs_9_
  36.2 0.0 copy-done.1
  36.2 0.0 copy-done.2
  36.2 0.9 %finish.1 = (bf16[4,16,256]{2,1,0:T(8,128)(2,1)}, f32[4,16,256]{2,1,0:T(8,128)}, f32[4,16]{1,0:T(4,128)}, f32[128,256]{1,0:T(8,128)}) custom-call(f32[4,16,256]{2,1,0:T(8,128)S(1)} %slice_bitcast_fusion.refs_0_, bf16[4,16,256]{2,1,0:T(8,128)(2,1)S(1)} %collective-permute-done.5.refs_1_, bf16[4,16,256]{2,1,0:T(8,128)(2,1)S(1)} %collective-permute-done.6.refs_2_, ...), custom_call_target="tpu_custom_call" | custom-call | tf_op jit(solution)/shard_map/finish/pallas_call | solution.py:466
  (7 shorter events, 0.1 us)
Async XLA Ops:
  0.6 0.8 %copy-start = (bf16[4,16,256]{2,1,0:T(8,128)(2,1)S(1)}, bf16[4,16,256]{2,1,0:T(8,128)(2,1)}, u32[]{:S(2)}) copy-start(bf16[4,16,256]{2,1,0:T(8,128)(2,1)} %param.10) | copy-start | bytes 98308
  2.6 5.4 %collective-permute-start = (bf16[4,16,256]{2,1,0:T(8,128)(2,1)S(1)}, bf16[4,16,256]{2,1,0:T(8,128)(2,1)S(1)}, u32[]{:S(2)}, u32[]{:S(2)}) collective-permute-start(bf16[4,16,256]{2,1,0:T(8,128)(2,1)S(1)} %fusion.cost_ref), channel_id=1, source_target_pairs={{4,0},{0,4},{12,8},{8,12},{20,16},{16,20},{28,24},{24,28},{5,1},{1... | collective-permute-start | bytes 98312 | tf_op jit(solution)/shard_map/ppermute | solution.py:45
  8.1 9.2 %collective-permute-start.3 = (bf16[8,16,256]{2,1,0:T(8,128)(2,1)S(1)}, bf16[8,16,256]{2,1,0:T(8,128)(2,1)S(1)}, u32[]{:S(2)}, u32[]{:S(2)}) collective-permute-start(bf16[8,16,256]{2,1,0:T(8,128)(2,1)S(1)} %constant_dynamic-update-slice_fusion), channel_id=1, source_target_pairs={{8,0},{12,4},{0,8},{4,12},{24,16},{28,20},{16,24},{20,28},{9,1},{1... | collective-permute-start | bytes 196616 | tf_op jit(solution)/shard_map/ppermute | solution.py:45
  9.7 8.3 %collective-permute-start.2 = (bf16[8,16,256]{2,1,0:T(8,128)(2,1)S(1)}, bf16[8,16,256]{2,1,0:T(8,128)(2,1)S(1)}, u32[]{:S(2)}, u32[]{:S(2)}) collective-permute-start(bf16[8,16,256]{2,1,0:T(8,128)(2,1)S(1)} %constant_dynamic-update-slice_fusion), channel_id=1, source_target_pairs={{24,0},{28,4},{16,8},{20,12},{8,16},{12,20},{0,24},{4,28},{25,1},{... | collective-permute-start | bytes 196616 | tf_op jit(solution)/shard_map/ppermute | solution.py:45
  12.2 6.5 %collective-permute-start.1 = (bf16[8,16,256]{2,1,0:T(8,128)(2,1)S(1)}, bf16[8,16,256]{2,1,0:T(8,128)(2,1)S(1)}, u32[]{:S(2)}, u32[]{:S(2)}) collective-permute-start(bf16[8,16,256]{2,1,0:T(8,128)(2,1)S(1)} %constant_dynamic-update-slice_fusion), channel_id=1, source_target_pairs={{16,0},{20,4},{24,8},{28,12},{0,16},{4,20},{8,24},{12,28},{17,1},{... | collective-permute-start | bytes 196616 | tf_op jit(solution)/shard_map/ppermute | solution.py:45
  19.4 16.8 %copy-start.1 = (bf16[4,256,256]{2,1,0:T(8,128)(2,1)S(1)}, bf16[4,256,256]{2,1,0:T(8,128)(2,1)}, u32[]{:S(2)}) copy-start(bf16[4,256,256]{2,1,0:T(8,128)(2,1)} %refs_4_.1) | copy-start | bytes 1572868
  19.5 16.8 %copy-start.2 = (f32[4,256]{1,0:T(4,128)S(1)}, f32[4,256]{1,0:T(4,128)}, u32[]{:S(2)}) copy-start(f32[4,256]{1,0:T(4,128)} %refs_5_.1) | copy-start | bytes 12292
  22.1 3.8 %collective-permute-start.8 = (f32[128,256]{1,0:T(8,128)S(1)}, f32[128,256]{1,0:T(8,128)S(1)}, u32[]{:S(2)}, u32[]{:S(2)}) collective-permute-start(f32[128,256]{1,0:T(8,128)S(1)} %get-tuple-element.53), channel_id=1, source_target_pairs={{0,1},{1,0},{2,3},{3,2},{4,5},{5,4},{6,7},{7,6},{8,9},{9,8},{10,11... | collective-permute-start | bytes 393224 | tf_op jit(solution)/shard_map/ppermute | solution.py:49
  22.1 5.9 %collective-permute-start.4 = (bf16[16,16,256]{2,1,0:T(8,128)(2,1)S(1)}, bf16[16,16,256]{2,1,0:T(8,128)(2,1)S(1)}, u32[]{:S(2)}, u32[]{:S(2)}) collective-permute-start(bf16[16,16,256]{2,1,0:T(8,128)(2,1)S(1)} %get-tuple-element.51), channel_id=1, source_target_pairs={{0,4},{4,0},{8,12},{12,8},{16,20},{20,16},{24,28},{28,24},{1,5},{5... | collective-permute-start | bytes 393224 | tf_op jit(solution)/shard_map/ppermute | solution.py:49
  25.9 10.3 %collective-permute-start.9 = (f32[128,256]{1,0:T(8,128)S(1)}, f32[128,256]{1,0:T(8,128)S(1)}, u32[]{:S(2)}, u32[]{:S(2)}) collective-permute-start(f32[128,256]{1,0:T(8,128)S(1)} %add.11.refs_8_), channel_id=1, source_target_pairs={{0,2},{1,3},{2,0},{3,1},{4,6},{5,7},{6,4},{7,5},{8,10},{9,11},{10,... | collective-permute-start | bytes 393224 | tf_op jit(solution)/shard_map/ppermute | solution.py:49
  28.1 5.8 %collective-permute-start.5 = (bf16[4,16,256]{2,1,0:T(8,128)(2,1)S(1)}, bf16[4,16,256]{2,1,0:T(8,128)(2,1)S(1)}, u32[]{:S(2)}, u32[]{:S(2)}) collective-permute-start(bf16[4,16,256]{2,1,0:T(8,128)(2,1)S(1)} %get-tuple-element.60), channel_id=1, source_target_pairs={{0,24},{4,28},{8,16},{12,20},{16,8},{20,12},{24,0},{28,4},{1,25},{... | collective-permute-start | bytes 98312 | tf_op jit(solution)/shard_map/ppermute | solution.py:49
  31.1 5.1 %collective-permute-start.6 = (bf16[4,16,256]{2,1,0:T(8,128)(2,1)S(1)}, bf16[4,16,256]{2,1,0:T(8,128)(2,1)S(1)}, u32[]{:S(2)}, u32[]{:S(2)}) collective-permute-start(bf16[4,16,256]{2,1,0:T(8,128)(2,1)S(1)} %get-tuple-element.59), channel_id=1, source_target_pairs={{0,16},{4,20},{8,24},{12,28},{16,0},{20,4},{24,8},{28,12},{1,17},{... | collective-permute-start | bytes 98312 | tf_op jit(solution)/shard_map/ppermute | solution.py:49
  31.5 4.8 %collective-permute-start.7 = (bf16[4,16,256]{2,1,0:T(8,128)(2,1)S(1)}, bf16[4,16,256]{2,1,0:T(8,128)(2,1)S(1)}, u32[]{:S(2)}, u32[]{:S(2)}) collective-permute-start(bf16[4,16,256]{2,1,0:T(8,128)(2,1)S(1)} %get-tuple-element.58), channel_id=1, source_target_pairs={{0,8},{4,12},{8,0},{12,4},{16,24},{20,28},{24,16},{28,20},{1,9},{5... | collective-permute-start | bytes 98312 | tf_op jit(solution)/shard_map/ppermute | solution.py:49

commit v5 on v4

--- a/solution.py
+++ b/solution.py
@@ -69,11 +69,20 @@
     def __init__(self, own, slots, reg_count):
         self.own, self.slots, self.reg_count = own, slots, reg_count
         self.slot_count = own * slots
+        self.loaded_first = 3 * own * slots // 8
         self.dense = reg_count * own <= slots
         self.capacity = own * own if self.dense else -(-own * slots // reg_count)
         self.count = self.capacity * reg_count
         self.stride = self.count + 1
         self.columns = 2 if self.dense else 4
+
+    def numbers(self, distances):
+        return [distance * self.capacity + i for distance in distances for i in range(self.capacity)]
+
+    def turned(self, distances):
+        if not self.dense:
+            return []
+        return self.numbers(distances)
 
     def slot(self, table, entry):
         return table[entry]
@@ -131,7 +140,7 @@
                 (tau, tau_ref),
                 (cotangent, cotangent_ref),
                 (elasticity, elasticity_ref),
-                (blocks.at[pl.ds(0, entries.slots)], held_ref.at[pl.ds(0, entries.slots)]),
+                (blocks.at[pl.ds(0, entries.loaded_first)], held_ref.at[pl.ds(0, entries.loaded_first)]),
             )
         )
     ]
@@ -146,17 +155,19 @@
 
 
 def score_entries(
-    entries, first, table_ref, costs, held_ref, tau_ref, elasticity_ref, weights_ref, top_ref, norm_ref, arrive=lambda r: None
+    entries, distances, table_ref, costs, held_ref, tau_ref, elasticity_ref, weights_ref, top_ref, norm_ref,
+    arrive=lambda r: None,
 ):
     own, capacity = entries.own, entries.capacity
-    count = weights_ref.shape[0]
+    numbers = entries.numbers(distances)
+    count = len(numbers)
     scale = -elasticity_ref[...]
     lowest = jnp.full(top_ref.shape[1:], LOWEST, F32)
     zero = jnp.zeros(top_ref.shape[1:], F32)
     rows = [(ref, block) for ref in costs for block in range(ref.shape[0] // own)]
 
     def score(i):
-        entry = first * capacity + i
+        entry = numbers[i]
         ref, block = rows[i // capacity]
         slot = entries.slot(table_ref, entry)
         cost = ref[block * own + entries.place(table_ref, entry)]
@@ -166,8 +177,8 @@
     if entries.dense:
         for r in range(own):
             arrive(r)
-            members = [i for i in range(count) if entries.importer(table_ref, i) == r]
-            scores = [jnp.where(entries.live(table_ref, first * capacity + i), score(i), -jnp.inf) for i in members]
+            members = [i for i in range(count) if entries.importer(table_ref, numbers[i]) == r]
+            scores = [jnp.where(entries.live(table_ref, numbers[i]), score(i), -jnp.inf) for i in members]
             top = functools.reduce(jnp.maximum, scores, lowest)
             norm = zero
             for i, value in zip(members, scores):
@@ -181,46 +192,55 @@
     top_ref[...] = jnp.full(top_ref.shape, LOWEST, F32)
     norm_ref[...] = jnp.zeros(norm_ref.shape, F32)
     for i in range(count):
-        importer = entries.importer(table_ref, first * capacity + i)
+        importer = entries.importer(table_ref, numbers[i])
         value = score(i)
         weights_ref[i] = value
         top_ref[importer] = jnp.maximum(top_ref[importer], value)
     for i in range(count):
-        importer = entries.importer(table_ref, first * capacity + i)
+        importer = entries.importer(table_ref, numbers[i])
         weight = jnp.exp(weights_ref[i] - top_ref[importer])
         weights_ref[i] = weight
         norm_ref[importer] += weight
 
 
-def near_kernel(entries, n_costs, *refs):
+def near_kernel(entries, distances, turned, n_costs, *refs):
     table_ref, blocks, _, tau_ref, elasticity_ref = refs[:5]
     costs = refs[5 : 5 + n_costs]
-    held_ref, weights_ref, top_ref, norm_ref, sems = refs[5 + n_costs :]
-    own, slots = entries.own, entries.slots
-    copies = [
-        pltpu.make_async_copy(blocks.at[pl.ds(r * slots, slots)], held_ref.at[pl.ds(r * slots, slots)], sems.at[r])
-        for r in range(1, own)
-    ]
+    held_ref, weights_ref, top_ref, norm_ref, turned_ref, sems = refs[5 + n_costs :]
+    copies = []
+    for r in range(entries.own):
+        start, stop = max(r * entries.slots, entries.loaded_first), (r + 1) * entries.slots
+        if start < stop:
+            part = pl.ds(start, stop - start)
+            copies.append(pltpu.make_async_copy(blocks.at[part], held_ref.at[part], sems.at[r]))
     for copy in copies:
         copy.start()
+    skipped = entries.own - len(copies)
 
     def arrive(r):
-        for copy in copies if r is None else copies[r - 1 : r] if r else []:
+        for copy in copies if r is None else copies[r - skipped : r - skipped + 1] if r >= skipped else []:
             copy.wait()
+        for i, entry in enumerate(turned):
+            if r is None or entries.importer(table_ref, entry) == r:
+                turned_ref[i] = held_ref[entries.slot(table_ref, entry)].T
 
     score_entries(
-        entries, 0, table_ref, costs, held_ref, tau_ref, elasticity_ref, weights_ref, top_ref, norm_ref, arrive
+        entries, distances, table_ref, costs, held_ref, tau_ref, elasticity_ref, weights_ref, top_ref, norm_ref, arrive
     )
 
 
-def far_kernel(entries, first, table_ref, held_ref, tau_ref, elasticity_ref, cost_ref, weights_ref, top_ref, norm_ref):
-    score_entries(entries, first, table_ref, [cost_ref], held_ref, tau_ref, elasticity_ref, weights_ref, top_ref, norm_ref)
-
-
-def push_entries(entries, distances, table_ref, adjoint_of, held_ref, total_ref):
+def far_kernel(entries, distances, table_ref, held_ref, tau_ref, elasticity_ref, cost_ref, weights_ref, top_ref, norm_ref):
+    score_entries(
+        entries, distances, table_ref, [cost_ref], held_ref, tau_ref, elasticity_ref, weights_ref, top_ref, norm_ref
+    )
+
+
+def push_entries(entries, distances, table_ref, adjoint_of, held_ref, total_ref, turned=(), turned_ref=None):
     own, capacity = entries.own, entries.capacity
 
     def pushed(entry):
+        if entry in turned:
+            return jnp.dot(adjoint_of(entry), turned_ref[turned.index(entry)], preferred_element_type=F32)
         return lax.dot_general(
             adjoint_of(entry),
             held_ref[entries.slot(table_ref, entry)],
@@ -240,13 +260,13 @@
             total_ref[block * own + entries.place(table_ref, entry)] += pushed(entry)
 
 
-def adjoint_kernel(entries, order, distances, *refs):
-    n = len(order)
-    table_ref, held_ref, cotangent_ref = refs[:3]
-    weights, tops, norms = ([refs[3 + c * n + order.index(k)] for k in range(n)] for c in range(3))
-    adjoint_ref, tau_grad_ref, logsum_ref, partial_ref, factor_ref, tau_rows_ref, total_ref = refs[3 + 3 * n :]
+def adjoint_kernel(entries, pieces, distances, turned, *refs):
+    n = len(pieces)
+    piece_of = {entry: (k, i) for k, piece in enumerate(pieces) for i, entry in enumerate(entries.numbers(piece))}
+    table_ref, held_ref, turned_ref, cotangent_ref = refs[:4]
+    weights, tops, norms = refs[4 : 4 + n], refs[4 + n : 4 + 2 * n], refs[4 + 2 * n : 4 + 3 * n]
+    adjoint_ref, tau_grad_ref, logsum_ref, partial_ref, factor_ref, tau_rows_ref, total_ref = refs[4 + 3 * n :]
     own, capacity = entries.own, entries.capacity
-    piece = weights[0].shape[0]
     tau_rows_ref[...] = jnp.zeros(tau_rows_ref.shape, F32)
     for r in range(own):
         top = functools.reduce(jnp.maximum, [ref[r] for ref in tops])
@@ -260,12 +280,12 @@
         factor_ref[k, own] = jnp.zeros(factor_ref.shape[2:], F32)
 
     def adjoint(entry):
-        k, i = divmod(entry, piece)
+        k, i = piece_of[entry]
         value = factor_ref[k, entries.importer(table_ref, entry)] * weights[k][i]
         tau_rows_ref[pl.ds(entries.row(table_ref, entry), 1)] = jnp.sum(value, axis=0, keepdims=True)
         return value.astype(BF16)
 
-    push_entries(entries, distances, table_ref, adjoint, held_ref, total_ref)
+    push_entries(entries, distances, table_ref, adjoint, held_ref, total_ref, turned, turned_ref)
     partial_ref[...] = total_ref[...].astype(BF16)
     for entry in range(entries.count):
         if entry // capacity not in distances:
@@ -314,9 +334,6 @@
     blocks = pair_blocks.reshape(own * slots, sectors, sectors)
     row = (episodes, sectors)
     stages = radices(reg_count)
-    last_radix = stages[-1]
-    last_stride = reg_count // last_radix
-    capacity = entries.capacity
 
     unit_cost = (
         labor_share[:, None, :] * log_wages[:, :, None]
@@ -355,31 +372,37 @@
         in_hbm(list_lengths),
     )
 
-    near = [unit_cost]
-    stride = 1
-    for radix in stages[:-1]:
+    near, near_distances = [unit_cost], [0]
+    stride = reg_count
+    for radix in reversed(stages):
+        stride //= radix
+        whole, distances = jnp.concatenate(near, axis=0), near_distances
+        order = [*range(2, radix), 1]
+        received = [from_peer(whole, j * stride, "reg", reg_count) for j in order]
+        reached = [[d + j * stride for d in distances] for j in order]
+        near[0] = cost_copy
         if stride > 1:
-            near[0] = cost_copy
-        whole = jnp.concatenate(near, axis=0)
-        near += [from_peer(whole, j * stride, "reg", reg_count) for j in range(1, radix)]
-        stride *= radix
-    near[0] = cost_copy
-    whole = jnp.concatenate(near, axis=0)
-    far = [from_peer(whole, j * stride, "reg", reg_count) for j in range(1, last_radix)]
-
-    def scored(count):
+            near = near + received
+            near_distances = sum(reached, distances)
+    pieces = [near_distances] + reached
+
+    def scored(distances):
         return (
-            shape((count,) + row, F32),
+            shape((len(distances) * entries.capacity,) + row, F32),
             shape((own + 1,) + row, F32),
             shape((own + 1,) + row, F32),
         )
 
-    piece = last_stride * capacity
-    held, *near_scores = pl.pallas_call(
-        functools.partial(near_kernel, entries, len(near)),
-        out_shape=(shape(blocks.shape, BF16),) + scored(piece),
+    radix = stages[0]
+    groups = [range(j, reg_count, radix) for j in range(radix)]
+    turned = entries.turned(groups[-1])
+    held, *near_scores, turned_blocks = pl.pallas_call(
+        functools.partial(near_kernel, entries, near_distances, turned, len(near)),
+        out_shape=(shape(blocks.shape, BF16),)
+        + scored(near_distances)
+        + (shape((max(len(turned), 1), sectors, sectors), BF16),),
         in_specs=[SMEM, HBM] + [VMEM] * (3 + len(near)),
-        out_specs=(VMEM,) * 4,
+        out_specs=(VMEM,) * 5,
         scratch_shapes=[pltpu.SemaphoreType.DMA((own,))],
         input_output_aliases={2: 0},
         compiler_params=params(2),
@@ -387,41 +410,38 @@
         name="near",
     )(table, in_hbm(blocks), held, tau, elastic, *near)
     scores = [near_scores]
-    for j, cost in enumerate(far, 1):
+    for cost, distances in zip(received, reached):
         scores.append(
             pl.pallas_call(
-                functools.partial(far_kernel, entries, j * last_stride),
-                out_shape=scored(piece),
+                functools.partial(far_kernel, entries, distances),
+                out_shape=scored(distances),
                 in_specs=[SMEM] + [VMEM] * 4,
                 out_specs=(VMEM,) * 3,
                 compiler_params=params(2),
-                cost_estimate=effort(blocks.size // last_radix * 2),
+                cost_estimate=effort(blocks.size // len(pieces) * 2),
                 name="far",
             )(table, held, tau, elastic, cost)
         )
-    order = [0, *range(2, last_radix), 1]
-    radix = stages[0]
-    groups = [range(j, reg_count, radix) for j in range(radix)]
     partial_dims = (reg_count // radix * own,) + row
     adjoint, tau_grad, logsum, partial = pl.pallas_call(
-        functools.partial(adjoint_kernel, entries, order, groups[-1]),
+        functools.partial(adjoint_kernel, entries, pieces, groups[-1], turned),
         out_shape=(
             shape((entries.count,) + row, BF16),
             shape((own * slots, sectors), F32),
             shape((own,) + row, F32),
             shape(partial_dims, BF16),
         ),
-        in_specs=[SMEM] + [VMEM] * (2 + 3 * last_radix),
+        in_specs=[SMEM] + [VMEM] * (3 + 3 * len(pieces)),
         out_specs=(VMEM,) * 4,
         scratch_shapes=[
-            pltpu.VMEM((last_radix, own + 1) + row, F32),
+            pltpu.VMEM((len(pieces), own + 1) + row, F32),
             pltpu.VMEM((own * slots + 8, sectors), F32),
             pltpu.VMEM(partial_dims, F32),
         ],
         compiler_params=params(8),
         cost_estimate=effort(blocks.size),
         name="adjoint",
-    )(table, held, cotangent, *[scores[k][c] for c in range(3) for k in order])
+    )(table, held, turned_blocks, cotangent, *[score[c] for c in range(3) for score in scores])
 
     def push(j, dtype):
         return pl.pallas_call(

time: 37.4 us -> 36 us (0.963)
  Pallas kernels: 15.3 us -> 13.7 us
  waiting for transfers between devices: 4.21 us -> 5.26 us
  starting transfers between devices: 14.8 us -> 13.9 us
    pallas_call x5 -> x3, Pallas kernels: 9.74 us -> 7.56 us  [the longest x1 4.68 us: shards(): pl.pallas_call(functools.partial(near_kernel, entries, near_distances, tu...]
    ppermute x4, waiting for transfers between devices: 0.01 us -> 1.15 us  [from_peer(): return lax.ppermute(x, axis, [(peer(i, distance, n), i) for i in range(n)])]
    ppermute x6, starting transfers between devices: 7.51 us -> 6.65 us  [to_peer(): return lax.ppermute(x, axis, [(i, peer(i, distance, n)) for i in range(n)])]
    pallas_call x1, Pallas kernels: 2.37 us -> 2.97 us  [shards(): pl.pallas_call(functools.partial(load_kernel, entries), out_shape=(shape(...]
    unnamed x7 -> x6, local copies, waits for them, and re-layouts: 0.77 us -> 0.77 us
  transfers between devices with their start and end apart: 10 -> 10, of which waited for: 3 -> 4; matrix products, arithmetic and copies ran while one was open for 0% -> 0% of each run, Pallas kernels for 30% -> 28%
where the time goes in v5:
time: 36 us; the launch traced here: 35.7 us
  starting transfers between devices  13.9 us (39%)
  Pallas kernels  13.7 us (38%)
  waiting for transfers between devices  5.26 us (15%)
  matrix products  1.24 us (3%)
  local copies, waits for them, and re-layouts  0.78 us (2%)
  between operations  0.75 us (2%)
    ppermute x4, starting transfers between devices, from_peer(): return lax.ppermute(x, axis, [(peer(i, distance, n), i) for i in range(n)])  7.25 us
    ppermute x6, starting transfers between devices, to_peer(): return lax.ppermute(x, axis, [(i, peer(i, distance, n)) for i in range(n)])  6.65 us
    pallas_call x1, Pallas kernels, shards(): pl.pallas_call(functools.partial(near_kernel, entries, near_distances, tu...  4.68 us
    ppermute x6, waiting for transfers between devices, to_peer(): return lax.ppermute(x, axis, [(i, peer(i, distance, n)) for i in range(n)])  4.11 us
    pallas_call x1, Pallas kernels, shards(): pl.pallas_call(functools.partial(load_kernel, entries), out_shape=(shape(...  2.97 us
    pallas_call x1, Pallas kernels, push(): pl.pallas_call(functools.partial(push_kernel, entries, groups[j]), out_sh...  2.26 us
    pallas_call x1, Pallas kernels, shards(): pl.pallas_call(functools.partial(adjoint_kernel, entries, pieces, groups[...  1.61 us
    pallas_call x1, Pallas kernels, shards(): pl.pallas_call(functools.partial(far_kernel, entries, distances), out_sha...  1.27 us
  transfers between devices with their start and end apart: 10, of which 4 were waited for; matrix products, arithmetic and copies ran while one was open for 0% of the time, Pallas kernels for 28%

profile of v5, /device:TPU:0, one launch (start us, length us, event | category | flops | bytes accessed | tf_op | source)
XLA Modules:
  0.0 35.7 jit_solution(13047313977556933516)
XLA Ops:
  0.6 0.0 copy-start
  0.6 0.7 %copy-done = bf16[4,16,256]{2,1,0:T(8,128)(2,1)S(1)} copy-done((bf16[4,16,256]{2,1,0:T(8,128)(2,1)S(1)}, bf16[4,16,256]{2,1,0:T(8,128)(2,1)}, u32[]{:S(2)}) %copy-start) | copy-done | bytes 32792
  1.4 1.2 %fusion.cost_ref = bf16[4,16,256]{2,1,0:T(8,128)(2,1)S(1)} fusion(bf16[4,16,256]{2,1,0:T(8,128)(2,1)S(1)} %copy-done, bf16[4,256,256]{2,1,0:T(8,128)(2,1)} %refs_4_.1, f32[4,16]{1,0:T(4,128)} %param.11, f32[4,256]{1,0:T(4,128)} %refs_5_.1), kind=kOutput, calls=%fused_computation.1 | convolution fusion | flops 8437760 | bytes 594176 | tf_op jit(solution)/shard_map/iek,ikj->iej/dot_general | solution.py:340
  2.6 4.1 %collective-permute-start = (bf16[4,16,256]{2,1,0:T(8,128)(2,1)S(1)}, bf16[4,16,256]{2,1,0:T(8,128)(2,1)S(1)}, u32[]{:S(2)}, u32[]{:S(2)}) collective-permute-start(bf16[4,16,256]{2,1,0:T(8,128)(2,1)S(1)} %fusion.cost_ref), channel_id=1, source_target_pairs={{16,0},{20,4},{24,8},{28,12},{0,16},{4,20},{8,24},{12,28},{17,1},{... | collective-permute-start | bytes 98312 | tf_op jit(solution)/shard_map/ppermute | solution.py:45
  6.7 1.3 %collective-permute-start.1 = (bf16[4,16,256]{2,1,0:T(8,128)(2,1)S(1)}, bf16[4,16,256]{2,1,0:T(8,128)(2,1)S(1)}, u32[]{:S(2)}, u32[]{:S(2)}) collective-permute-start(bf16[4,16,256]{2,1,0:T(8,128)(2,1)S(1)} %fusion.cost_ref), channel_id=1, source_target_pairs={{24,0},{28,4},{16,8},{20,12},{8,16},{12,20},{0,24},{4,28},{25,1},{... | collective-permute-start | bytes 98312 | tf_op jit(solution)/shard_map/ppermute | solution.py:45
  8.1 0.2 collective-permute-start.2
  8.3 3.0 %load.1 = (bf16[128,256,256]{2,1,0:T(8,128)(2,1)S(1)}, f32[128,256]{1,0:T(8,128)S(1)}, f32[4,16,256]{2,1,0:T(8,128)S(1)}, f32[1,256]{1,0:T(1,128)S(1)}, bf16[4,16,256]{2,1,0:T(8,128)(2,1)S(1)}, /*index=5*/s32[258]{0:T(512)S(4)}) custom-call(s32[1]{0:T(128)} %bitcast.me_ref, bf16[4,16,256]{2,1,0:T(8,128)(2,1)S(1)} %fusion.cost_ref, ...), custom_call_target="tpu_custom_call" | custom-call | bytes 8388608 | tf_op jit(solution)/shard_map/load/pallas_call | solution.py:343
  11.3 0.0 collective-permute-done.refs_6_
  11.3 1.1 %collective-permute-done.1.refs_7_ = bf16[4,16,256]{2,1,0:T(8,128)(2,1)S(1)} collective-permute-done((bf16[4,16,256]{2,1,0:T(8,128)(2,1)S(1)}, bf16[4,16,256]{2,1,0:T(8,128)(2,1)S(1)}, u32[]{:S(2)}, u32[]{:S(2)}) %collective-permute-start.1) | collective-permute-done | bytes 32800 | tf_op jit(solution)/shard_map/ppermute | solution.py:45
  12.4 0.0 collective-permute-done.2.refs_8_
  12.5 1.6 %collective-permute-start.3 = (bf16[16,16,256]{2,1,0:T(8,128)(2,1)S(1)}, bf16[16,16,256]{2,1,0:T(8,128)(2,1)S(1)}, u32[]{:S(2)}, u32[]{:S(2)}) collective-permute-start(bf16[16,16,256]{2,1,0:T(8,128)(2,1)S(1)} %pad_maximum_fusion), channel_id=1, source_target_pairs={{4,0},{0,4},{12,8},{8,12},{20,16},{16,20},{28,24},{24,28},{5,1},{1... | collective-permute-start | bytes 393224 | tf_op jit(solution)/shard_map/ppermute | solution.py:45
  14.0 4.7 %near.1 = (bf16[128,256,256]{2,1,0:T(8,128)(2,1)S(1)}, f32[64,16,256]{2,1,0:T(8,128)S(1)}, f32[5,16,256]{2,1,0:T(8,128)S(1)}, f32[5,16,256]{2,1,0:T(8,128)S(1)}, bf16[64,256,256]{2,1,0:T(8,128)(2,1)S(1)}) custom-call(s32[258]{0:T(512)S(4)} %get-tuple-element.26.refs_0_.table_ref, bf16[128,256,256]{2,1,0:T(8,128)(2,1)} %bitcast.17, ...), custom_call_target="tpu_custom_call", output_to_operand_aliasing={{0}: (2, {})} | custom-call | bytes 8388608 | tf_op jit(solution)/shard_map/near/pallas_call | solution.py:399
  18.7 0.0 collective-permute-done.3.cost_ref
  18.7 1.3 %far.1 = (f32[64,16,256]{2,1,0:T(8,128)S(1)}, f32[5,16,256]{2,1,0:T(8,128)S(1)}, f32[5,16,256]{2,1,0:T(8,128)S(1)}) custom-call(s32[258]{0:T(512)S(4)} %get-tuple-element.26.refs_0_.table_ref, bf16[128,256,256]{2,1,0:T(8,128)(2,1)S(1)} %get-tuple-element.31.held_ref.refs_1_, f32[128,256]{1,0:T(8,128)S(1)} %get-tuple-element.28.refs_3_.tau_ref, ...), custom_call_target="tpu_custom_call" | custom-call | bytes 8388608 | tf_op jit(solution)/shard_map/far/pallas_call | solution.py:415
  20.0 1.6 %adjoint.1 = (bf16[128,16,256]{2,1,0:T(8,128)(2,1)S(1)}, f32[128,256]{1,0:T(8,128)S(1)}, f32[4,16,256]{2,1,0:T(8,128)S(1)}, bf16[16,16,256]{2,1,0:T(8,128)(2,1)S(1)}) custom-call(s32[258]{0:T(512)S(4)} %get-tuple-element.26.refs_0_.table_ref, bf16[128,256,256]{2,1,0:T(8,128)(2,1)S(1)} %get-tuple-element.31.held_ref.refs_1_, ...), custom_call_target="tpu_custom_call" | custom-call | bytes 8388608 | tf_op jit(solution)/shard_map/adjoint/pallas_call | solution.py:426
  21.6 0.0 copy-start.1
  21.6 0.0 copy-start.2
  21.6 0.1 collective-permute-start.8
  21.7 0.6 %collective-permute-start.4 = (bf16[16,16,256]{2,1,0:T(8,128)(2,1)S(1)}, bf16[16,16,256]{2,1,0:T(8,128)(2,1)S(1)}, u32[]{:S(2)}, u32[]{:S(2)}) collective-permute-start(bf16[16,16,256]{2,1,0:T(8,128)(2,1)S(1)} %get-tuple-element.41), channel_id=1, source_target_pairs={{0,4},{4,0},{8,12},{12,8},{16,20},{20,16},{24,28},{28,24},{1,5},{5... | collective-permute-start | bytes 393224 | tf_op jit(solution)/shard_map/ppermute | solution.py:49
  22.3 2.3 %push.1 = f32[16,16,256]{2,1,0:T(8,128)S(1)} custom-call(s32[258]{0:T(512)S(4)} %get-tuple-element.26.refs_0_.table_ref, bf16[128,256,256]{2,1,0:T(8,128)(2,1)S(1)} %get-tuple-element.31.held_ref.refs_1_, bf16[128,16,256]{2,1,0:T(8,128)(2,1)S(1)} %get-tuple-element.40.adjoint_ref), custom_call_target="tpu_custom_call" | custom-call | bytes 8388608 | tf_op jit(solution)/shard_map/push/pallas_call | solution.py:447
  24.6 0.0 collective-permute-done.8
  24.6 1.6 %collective-permute-start.9 = (f32[128,256]{1,0:T(8,128)S(1)}, f32[128,256]{1,0:T(8,128)S(1)}, u32[]{:S(2)}, u32[]{:S(2)}) collective-permute-start(f32[128,256]{1,0:T(8,128)S(1)} %add.11.refs_8_), channel_id=1, source_target_pairs={{0,2},{1,3},{2,0},{3,1},{4,6},{5,7},{6,4},{7,5},{8,10},{9,11},{10,... | collective-permute-start | bytes 393224 | tf_op jit(solution)/shard_map/ppermute | solution.py:49
  26.2 1.5 %collective-permute-done.4 = bf16[16,16,256]{2,1,0:T(8,128)(2,1)S(1)} collective-permute-done((bf16[16,16,256]{2,1,0:T(8,128)(2,1)S(1)}, bf16[16,16,256]{2,1,0:T(8,128)(2,1)S(1)}, u32[]{:S(2)}, u32[]{:S(2)}) %collective-permute-start.4) | collective-permute-done | bytes 131104 | tf_op jit(solution)/shard_map/ppermute | solution.py:49
  27.7 2.1 %collective-permute-start.5 = (bf16[4,16,256]{2,1,0:T(8,128)(2,1)S(1)}, bf16[4,16,256]{2,1,0:T(8,128)(2,1)S(1)}, u32[]{:S(2)}, u32[]{:S(2)}) collective-permute-start(bf16[4,16,256]{2,1,0:T(8,128)(2,1)S(1)} %get-tuple-element.50), channel_id=1, source_target_pairs={{0,24},{4,28},{8,16},{12,20},{16,8},{20,12},{24,0},{28,4},{1,25},{... | collective-permute-start | bytes 98312 | tf_op jit(solution)/shard_map/ppermute | solution.py:49
  29.8 0.1 collective-permute-start.6
  29.9 2.2 %collective-permute-start.7 = (bf16[4,16,256]{2,1,0:T(8,128)(2,1)S(1)}, bf16[4,16,256]{2,1,0:T(8,128)(2,1)S(1)}, u32[]{:S(2)}, u32[]{:S(2)}) collective-permute-start(bf16[4,16,256]{2,1,0:T(8,128)(2,1)S(1)} %get-tuple-element.48), channel_id=1, source_target_pairs={{0,8},{4,12},{8,0},{12,4},{16,24},{20,28},{24,16},{28,20},{1,9},{5... | collective-permute-start | bytes 98312 | tf_op jit(solution)/shard_map/ppermute | solution.py:49
  32.2 1.3 %collective-permute-done.5.refs_1_ = bf16[4,16,256]{2,1,0:T(8,128)(2,1)S(1)} collective-permute-done((bf16[4,16,256]{2,1,0:T(8,128)(2,1)S(1)}, bf16[4,16,256]{2,1,0:T(8,128)(2,1)S(1)}, u32[]{:S(2)}, u32[]{:S(2)}) %collective-permute-start.5) | collective-permute-done | bytes 32800 | tf_op jit(solution)/shard_map/ppermute | solution.py:49
  33.5 1.3 %collective-permute-done.6.refs_2_ = bf16[4,16,256]{2,1,0:T(8,128)(2,1)S(1)} collective-permute-done((bf16[4,16,256]{2,1,0:T(8,128)(2,1)S(1)}, bf16[4,16,256]{2,1,0:T(8,128)(2,1)S(1)}, u32[]{:S(2)}, u32[]{:S(2)}) %collective-permute-start.6) | collective-permute-done | bytes 32800 | tf_op jit(solution)/shard_map/ppermute | solution.py:49
  34.8 0.0 collective-permute-done.7.refs_3_
  34.8 0.0 collective-permute-done.9.refs_9_
  34.8 0.0 copy-done.1
  34.8 0.0 copy-done.2
  34.8 0.9 %finish.1 = (bf16[4,16,256]{2,1,0:T(8,128)(2,1)}, f32[4,16,256]{2,1,0:T(8,128)}, f32[4,16]{1,0:T(4,128)}, f32[128,256]{1,0:T(8,128)}) custom-call(f32[4,16,256]{2,1,0:T(8,128)S(1)} %slice_bitcast_fusion.refs_0_, bf16[4,16,256]{2,1,0:T(8,128)(2,1)S(1)} %collective-permute-done.5.refs_1_, bf16[4,16,256]{2,1,0:T(8,128)(2,1)S(1)} %collective-permute-done.6.refs_2_, ...), custom_call_target="tpu_custom_call" | custom-call | tf_op jit(solution)/shard_map/finish/pallas_call | solution.py:486
  (6 shorter events, 0.1 us)
Async XLA Ops:
  0.6 0.8 %copy-start = (bf16[4,16,256]{2,1,0:T(8,128)(2,1)S(1)}, bf16[4,16,256]{2,1,0:T(8,128)(2,1)}, u32[]{:S(2)}) copy-start(bf16[4,16,256]{2,1,0:T(8,128)(2,1)} %param.10) | copy-start | bytes 98308
  2.6 8.6 %collective-permute-start = (bf16[4,16,256]{2,1,0:T(8,128)(2,1)S(1)}, bf16[4,16,256]{2,1,0:T(8,128)(2,1)S(1)}, u32[]{:S(2)}, u32[]{:S(2)}) collective-permute-start(bf16[4,16,256]{2,1,0:T(8,128)(2,1)S(1)} %fusion.cost_ref), channel_id=1, source_target_pairs={{16,0},{20,4},{24,8},{28,12},{0,16},{4,20},{8,24},{12,28},{17,1},{... | collective-permute-start | bytes 98312 | tf_op jit(solution)/shard_map/ppermute | solution.py:45
  6.7 5.7 %collective-permute-start.1 = (bf16[4,16,256]{2,1,0:T(8,128)(2,1)S(1)}, bf16[4,16,256]{2,1,0:T(8,128)(2,1)S(1)}, u32[]{:S(2)}, u32[]{:S(2)}) collective-permute-start(bf16[4,16,256]{2,1,0:T(8,128)(2,1)S(1)} %fusion.cost_ref), channel_id=1, source_target_pairs={{24,0},{28,4},{16,8},{20,12},{8,16},{12,20},{0,24},{4,28},{25,1},{... | collective-permute-start | bytes 98312 | tf_op jit(solution)/shard_map/ppermute | solution.py:45
  8.1 4.4 %collective-permute-start.2 = (bf16[4,16,256]{2,1,0:T(8,128)(2,1)S(1)}, bf16[4,16,256]{2,1,0:T(8,128)(2,1)S(1)}, u32[]{:S(2)}, u32[]{:S(2)}) collective-permute-start(bf16[4,16,256]{2,1,0:T(8,128)(2,1)S(1)} %fusion.cost_ref), channel_id=1, source_target_pairs={{8,0},{12,4},{0,8},{4,12},{24,16},{28,20},{16,24},{20,28},{9,1},{1... | collective-permute-start | bytes 98312 | tf_op jit(solution)/shard_map/ppermute | solution.py:45
  12.5 6.3 %collective-permute-start.3 = (bf16[16,16,256]{2,1,0:T(8,128)(2,1)S(1)}, bf16[16,16,256]{2,1,0:T(8,128)(2,1)S(1)}, u32[]{:S(2)}, u32[]{:S(2)}) collective-permute-start(bf16[16,16,256]{2,1,0:T(8,128)(2,1)S(1)} %pad_maximum_fusion), channel_id=1, source_target_pairs={{4,0},{0,4},{12,8},{8,12},{20,16},{16,20},{28,24},{24,28},{5,1},{1... | collective-permute-start | bytes 393224 | tf_op jit(solution)/shard_map/ppermute | solution.py:45
  21.6 13.2 %copy-start.1 = (bf16[4,256,256]{2,1,0:T(8,128)(2,1)S(1)}, bf16[4,256,256]{2,1,0:T(8,128)(2,1)}, u32[]{:S(2)}) copy-start(bf16[4,256,256]{2,1,0:T(8,128)(2,1)} %refs_4_.1) | copy-start | bytes 1572868
  21.6 13.2 %copy-start.2 = (f32[4,256]{1,0:T(4,128)S(1)}, f32[4,256]{1,0:T(4,128)}, u32[]{:S(2)}) copy-start(f32[4,256]{1,0:T(4,128)} %refs_5_.1) | copy-start | bytes 12292
  21.6 2.9 %collective-permute-start.8 = (f32[128,256]{1,0:T(8,128)S(1)}, f32[128,256]{1,0:T(8,128)S(1)}, u32[]{:S(2)}, u32[]{:S(2)}) collective-permute-start(f32[128,256]{1,0:T(8,128)S(1)} %get-tuple-element.43), channel_id=1, source_target_pairs={{0,1},{1,0},{2,3},{3,2},{4,5},{5,4},{6,7},{7,6},{8,9},{9,8},{10,11... | collective-permute-start | bytes 393224 | tf_op jit(solution)/shard_map/ppermute | solution.py:49
  21.7 5.9 %collective-permute-start.4 = (bf16[16,16,256]{2,1,0:T(8,128)(2,1)S(1)}, bf16[16,16,256]{2,1,0:T(8,128)(2,1)S(1)}, u32[]{:S(2)}, u32[]{:S(2)}) collective-permute-start(bf16[16,16,256]{2,1,0:T(8,128)(2,1)S(1)} %get-tuple-element.41), channel_id=1, source_target_pairs={{0,4},{4,0},{8,12},{12,8},{16,20},{20,16},{24,28},{28,24},{1,5},{5... | collective-permute-start | bytes 393224 | tf_op jit(solution)/shard_map/ppermute | solution.py:49
  24.6 10.2 %collective-permute-start.9 = (f32[128,256]{1,0:T(8,128)S(1)}, f32[128,256]{1,0:T(8,128)S(1)}, u32[]{:S(2)}, u32[]{:S(2)}) collective-permute-start(f32[128,256]{1,0:T(8,128)S(1)} %add.11.refs_8_), channel_id=1, source_target_pairs={{0,2},{1,3},{2,0},{3,1},{4,6},{5,7},{6,4},{7,5},{8,10},{9,11},{10,... | collective-permute-start | bytes 393224 | tf_op jit(solution)/shard_map/ppermute | solution.py:49
  27.7 5.8 %collective-permute-start.5 = (bf16[4,16,256]{2,1,0:T(8,128)(2,1)S(1)}, bf16[4,16,256]{2,1,0:T(8,128)(2,1)S(1)}, u32[]{:S(2)}, u32[]{:S(2)}) collective-permute-start(bf16[4,16,256]{2,1,0:T(8,128)(2,1)S(1)} %get-tuple-element.50), channel_id=1, source_target_pairs={{0,24},{4,28},{8,16},{12,20},{16,8},{20,12},{24,0},{28,4},{1,25},{... | collective-permute-start | bytes 98312 | tf_op jit(solution)/shard_map/ppermute | solution.py:49
  29.8 5.0 %collective-permute-start.6 = (bf16[4,16,256]{2,1,0:T(8,128)(2,1)S(1)}, bf16[4,16,256]{2,1,0:T(8,128)(2,1)S(1)}, u32[]{:S(2)}, u32[]{:S(2)}) collective-permute-start(bf16[4,16,256]{2,1,0:T(8,128)(2,1)S(1)} %get-tuple-element.49), channel_id=1, source_target_pairs={{0,16},{4,20},{8,24},{12,28},{16,0},{20,4},{24,8},{28,12},{1,17},{... | collective-permute-start | bytes 98312 | tf_op jit(solution)/shard_map/ppermute | solution.py:49
  29.9 4.9 %collective-permute-start.7 = (bf16[4,16,256]{2,1,0:T(8,128)(2,1)S(1)}, bf16[4,16,256]{2,1,0:T(8,128)(2,1)S(1)}, u32[]{:S(2)}, u32[]{:S(2)}) collective-permute-start(bf16[4,16,256]{2,1,0:T(8,128)(2,1)S(1)} %get-tuple-element.48), channel_id=1, source_target_pairs={{0,8},{4,12},{8,0},{12,4},{16,24},{20,28},{24,16},{28,20},{1,9},{5... | collective-permute-start | bytes 98312 | tf_op jit(solution)/shard_map/ppermute | solution.py:49

commit v6 on v5

--- a/solution.py
+++ b/solution.py
@@ -69,7 +69,7 @@
     def __init__(self, own, slots, reg_count):
         self.own, self.slots, self.reg_count = own, slots, reg_count
         self.slot_count = own * slots
-        self.loaded_first = 3 * own * slots // 8
+        self.loaded_first = 4 * own * slots // 8
         self.dense = reg_count * own <= slots
         self.capacity = own * own if self.dense else -(-own * slots // reg_count)
         self.count = self.capacity * reg_count
@@ -154,31 +154,37 @@
         copy.wait()
 
 
+def scorer(entries, numbers, table_ref, costs, held_ref, tau_ref, elasticity_ref):
+    scale = -elasticity_ref[...]
+    rows = [(ref, block) for ref in costs for block in range(ref.shape[0] // entries.own)]
+
+    def score(i):
+        entry = numbers[i]
+        ref, block = rows[i // entries.capacity]
+        slot = entries.slot(table_ref, entry)
+        cost = ref[block * entries.own + entries.place(table_ref, entry)]
+        landed = jnp.dot(cost, held_ref[slot], preferred_element_type=F32) + tau_ref[pl.ds(slot, 1)]
+        value = scale * landed
+        return jnp.where(entries.live(table_ref, entry), value, -jnp.inf) if entries.dense else value
+
+    return score
+
+
 def score_entries(
     entries, distances, table_ref, costs, held_ref, tau_ref, elasticity_ref, weights_ref, top_ref, norm_ref,
     arrive=lambda r: None,
 ):
-    own, capacity = entries.own, entries.capacity
+    own = entries.own
     numbers = entries.numbers(distances)
     count = len(numbers)
-    scale = -elasticity_ref[...]
     lowest = jnp.full(top_ref.shape[1:], LOWEST, F32)
     zero = jnp.zeros(top_ref.shape[1:], F32)
-    rows = [(ref, block) for ref in costs for block in range(ref.shape[0] // own)]
-
-    def score(i):
-        entry = numbers[i]
-        ref, block = rows[i // capacity]
-        slot = entries.slot(table_ref, entry)
-        cost = ref[block * own + entries.place(table_ref, entry)]
-        landed = jnp.dot(cost, held_ref[slot], preferred_element_type=F32) + tau_ref[pl.ds(slot, 1)]
-        return scale * landed
-
+    score = scorer(entries, numbers, table_ref, costs, held_ref, tau_ref, elasticity_ref)
     if entries.dense:
         for r in range(own):
             arrive(r)
             members = [i for i in range(count) if entries.importer(table_ref, numbers[i]) == r]
-            scores = [jnp.where(entries.live(table_ref, numbers[i]), score(i), -jnp.inf) for i in members]
+            scores = [score(i) for i in members]
             top = functools.reduce(jnp.maximum, scores, lowest)
             norm = zero
             for i, value in zip(members, scores):
@@ -229,18 +235,10 @@
     )
 
 
-def far_kernel(entries, distances, table_ref, held_ref, tau_ref, elasticity_ref, cost_ref, weights_ref, top_ref, norm_ref):
-    score_entries(
-        entries, distances, table_ref, [cost_ref], held_ref, tau_ref, elasticity_ref, weights_ref, top_ref, norm_ref
-    )
-
-
-def push_entries(entries, distances, table_ref, adjoint_of, held_ref, total_ref, turned=(), turned_ref=None):
+def push_entries(entries, distances, table_ref, adjoint_of, held_ref, total_ref):
     own, capacity = entries.own, entries.capacity
 
     def pushed(entry):
-        if entry in turned:
-            return jnp.dot(adjoint_of(entry), turned_ref[turned.index(entry)], preferred_element_type=F32)
         return lax.dot_general(
             adjoint_of(entry),
             held_ref[entries.slot(table_ref, entry)],
@@ -260,49 +258,98 @@
             total_ref[block * own + entries.place(table_ref, entry)] += pushed(entry)
 
 
-def adjoint_kernel(entries, pieces, distances, turned, *refs):
-    n = len(pieces)
-    piece_of = {entry: (k, i) for k, piece in enumerate(pieces) for i, entry in enumerate(entries.numbers(piece))}
-    table_ref, held_ref, turned_ref, cotangent_ref = refs[:4]
-    weights, tops, norms = refs[4 : 4 + n], refs[4 + n : 4 + 2 * n], refs[4 + 2 * n : 4 + 3 * n]
-    adjoint_ref, tau_grad_ref, logsum_ref, partial_ref, factor_ref, tau_rows_ref, total_ref = refs[4 + 3 * n :]
+def adjoint_kernel(entries, near_distances, far_distances, group, turned, *refs):
+    table_ref, held_ref, turned_ref, tau_ref, elasticity_ref, cotangent_ref, near_weights, near_top, near_norm = refs[:9]
+    costs = refs[9:-10]
+    adjoint_ref, tau_grad_ref, logsum_ref, partial_ref = refs[-10:-6]
+    far_weights, far_top, far_norm, factor_ref, tau_rows_ref, total_ref = refs[-6:]
     own, capacity = entries.own, entries.capacity
+    near, far = entries.numbers(near_distances), entries.numbers(far_distances)
     tau_rows_ref[...] = jnp.zeros(tau_rows_ref.shape, F32)
-    for r in range(own):
-        top = functools.reduce(jnp.maximum, [ref[r] for ref in tops])
-        shrink = [jnp.exp(ref[r] - top) for ref in tops]
-        norm = sum(ref[r] * factor for ref, factor in zip(norms, shrink))
-        logsum_ref[r] = top + jnp.log(norm)
-        scale = cotangent_ref[r] / norm
-        for k in range(n):
-            factor_ref[k, r] = scale * shrink[k]
-    for k in range(n):
-        factor_ref[k, own] = jnp.zeros(factor_ref.shape[2:], F32)
-
-    def adjoint(entry):
-        k, i = piece_of[entry]
-        value = factor_ref[k, entries.importer(table_ref, entry)] * weights[k][i]
+
+    def rounded(entry, value):
         tau_rows_ref[pl.ds(entries.row(table_ref, entry), 1)] = jnp.sum(value, axis=0, keepdims=True)
         return value.astype(BF16)
 
-    push_entries(entries, distances, table_ref, adjoint, held_ref, total_ref, turned, turned_ref)
+    def pushed(entry, value):
+        if entry in turned:
+            return jnp.dot(value, turned_ref[turned.index(entry)], preferred_element_type=F32)
+        return lax.dot_general(
+            value, held_ref[entries.slot(table_ref, entry)], CONTRACT_LAST, preferred_element_type=F32
+        )
+
+    if entries.dense:
+        score = scorer(entries, far, table_ref, costs, held_ref, tau_ref, elasticity_ref)
+        members = [[i for i, entry in enumerate(far) if entries.importer(None, entry) == r] for r in range(own)]
+
+        def emit(r, entry, value):
+            value = rounded(entry, value)
+            if entry // capacity not in group:
+                adjoint_ref[entry] = value
+                return
+            place = group.index(entry // capacity) * own + entries.place(None, entry)
+            term = pushed(entry, value)
+            total_ref[place] = term if r == 0 else total_ref[place] + term
+
+        for r in range(own + 1):
+            if r < own:
+                for i in members[r]:
+                    far_weights[i] = score(i)
+            if r == 0:
+                continue
+            q = r - 1
+            top = functools.reduce(jnp.maximum, [far_weights[i] for i in members[q]], near_top[q])
+            weights = [jnp.exp(far_weights[i] - top) for i in members[q]]
+            shrink = jnp.exp(near_top[q] - top)
+            norm = sum(weights, near_norm[q] * shrink)
+            logsum_ref[q] = top + jnp.log(norm)
+            scale = cotangent_ref[q] / norm
+            for i, weight in zip(members[q], weights):
+                emit(q, far[i], scale * weight)
+            scale = scale * shrink
+            for i, entry in enumerate(near):
+                if entries.importer(None, entry) == q:
+                    emit(q, entry, scale * near_weights[i])
+    else:
+        score_entries(
+            entries, far_distances, table_ref, costs, held_ref, tau_ref, elasticity_ref, far_weights, far_top, far_norm
+        )
+        for r in range(own):
+            top = jnp.maximum(near_top[r], far_top[r])
+            shrink = [jnp.exp(near_top[r] - top), jnp.exp(far_top[r] - top)]
+            norm = near_norm[r] * shrink[0] + far_norm[r] * shrink[1]
+            logsum_ref[r] = top + jnp.log(norm)
+            for k in range(2):
+                factor_ref[k, r] = cotangent_ref[r] / norm * shrink[k]
+        for k in range(2):
+            factor_ref[k, own] = jnp.zeros(factor_ref.shape[2:], F32)
+        total_ref[...] = jnp.zeros(total_ref.shape, F32)
+        for k, (numbers, weights_ref) in enumerate(((near, near_weights), (far, far_weights))):
+            for i, entry in enumerate(numbers):
+                value = rounded(entry, factor_ref[k, entries.importer(table_ref, entry)] * weights_ref[i])
+                if entry // capacity in group:
+                    place = group.index(entry // capacity) * own + entries.place(table_ref, entry)
+                    total_ref[place] += pushed(entry, value)
+                else:
+                    adjoint_ref[entry] = value
     partial_ref[...] = total_ref[...].astype(BF16)
-    for entry in range(entries.count):
-        if entry // capacity not in distances:
-            adjoint_ref[entry] = adjoint(entry)
     tau_grad_ref[...] = tau_rows_ref[pl.ds(0, entries.slot_count)]
 
 
 def push_kernel(entries, distances, table_ref, held_ref, adjoint_ref, partial_ref, total_ref):
     push_entries(entries, distances, table_ref, lambda entry: adjoint_ref[entry], held_ref, total_ref)
     partial_ref[...] = total_ref[...].astype(partial_ref.dtype)
+
+
+def add_kernel(x_ref, y_ref, out_ref):
+    out_ref[...] = (x_ref[...].astype(F32) + y_ref[...].astype(F32)).astype(out_ref.dtype)
 
 
 def finish_kernel(n, *refs):
     own_sum_ref, received = refs[0], refs[1 : 1 + n]
     io_ref, share_ref, logsum_ref, elasticity_ref, tau_ref, tau_received_ref = refs[1 + n : 7 + n]
     prices_ref, price_grad_ref, wage_grad_ref, tau_grad_ref = refs[7 + n :]
-    tau_grad_ref[...] = tau_ref[...] + tau_received_ref[...]
+    tau_grad_ref[...] = tau_ref[...].astype(F32) + tau_received_ref[...].astype(F32)
     for r in range(own_sum_ref.shape[0]):
         prices_ref[r] = (-logsum_ref[r] / elasticity_ref[...]).astype(BF16)
         cost_adjoint = own_sum_ref[r]
@@ -384,7 +431,7 @@
         if stride > 1:
             near = near + received
             near_distances = sum(reached, distances)
-    pieces = [near_distances] + reached
+    far_distances = sum(reached, [])
 
     def scored(distances):
         return (
@@ -409,39 +456,27 @@
         cost_estimate=effort(blocks.size),
         name="near",
     )(table, in_hbm(blocks), held, tau, elastic, *near)
-    scores = [near_scores]
-    for cost, distances in zip(received, reached):
-        scores.append(
-            pl.pallas_call(
-                functools.partial(far_kernel, entries, distances),
-                out_shape=scored(distances),
-                in_specs=[SMEM] + [VMEM] * 4,
-                out_specs=(VMEM,) * 3,
-                compiler_params=params(2),
-                cost_estimate=effort(blocks.size // len(pieces) * 2),
-                name="far",
-            )(table, held, tau, elastic, cost)
-        )
     partial_dims = (reg_count // radix * own,) + row
     adjoint, tau_grad, logsum, partial = pl.pallas_call(
-        functools.partial(adjoint_kernel, entries, pieces, groups[-1], turned),
+        functools.partial(adjoint_kernel, entries, near_distances, far_distances, groups[-1], turned),
         out_shape=(
             shape((entries.count,) + row, BF16),
             shape((own * slots, sectors), F32),
             shape((own,) + row, F32),
             shape(partial_dims, BF16),
         ),
-        in_specs=[SMEM] + [VMEM] * (3 + 3 * len(pieces)),
+        in_specs=[SMEM] + [VMEM] * (8 + len(received)),
         out_specs=(VMEM,) * 4,
         scratch_shapes=[
-            pltpu.VMEM((len(pieces), own + 1) + row, F32),
+            *[pltpu.VMEM(s.shape, F32) for s in scored(far_distances)],
+            pltpu.VMEM((2, own + 1) + row, F32),
             pltpu.VMEM((own * slots + 8, sectors), F32),
             pltpu.VMEM(partial_dims, F32),
         ],
         compiler_params=params(8),
         cost_estimate=effort(blocks.size),
         name="adjoint",
-    )(table, held, turned_blocks, cotangent, *[score[c] for c in range(3) for score in scores])
+    )(table, held, turned_blocks, tau, elastic, cotangent, *near_scores, *received)
 
     def push(j, dtype):
         return pl.pallas_call(
@@ -476,7 +511,16 @@
         tau_received = jnp.zeros_like(tau_grad)
         distance = 1
         while distance < ep_count:
-            tau_grad = tau_grad + tau_received if distance > 1 else tau_grad
+            if distance > 1:
+                tau_grad = pl.pallas_call(
+                    add_kernel,
+                    out_shape=shape(tau_grad.shape, F32),
+                    in_specs=[VMEM, VMEM],
+                    out_specs=VMEM,
+                    compiler_params=params(1),
+                    cost_estimate=effort(1),
+                    name="add",
+                )(tau_grad, tau_received)
             tau_received = to_peer(tau_grad, distance, "ep", ep_count)
             distance *= 2
     else:

time: 36 us -> 35.4 us (0.983)
  waiting for transfers between devices: 5.26 us -> 4.85 us
  Pallas kernels: 13.7 us -> 13.3 us
    ppermute x4, waiting for transfers between devices: 1.15 us -> 0.55 us  [from_peer(): return lax.ppermute(x, axis, [(peer(i, distance, n), i) for i in range(n)])]
    pallas_call x1, Pallas kernels: 2.97 us -> 3.57 us  [shards(): pl.pallas_call(functools.partial(load_kernel, entries), out_shape=(shape(...]
    pallas_call x1, Pallas kernels: 4.68 us -> 4.11 us  [shards(): pl.pallas_call(functools.partial(near_kernel, entries, near_distances, tu...]
    pallas_call x2, Pallas kernels: 2.88 us -> 2.5 us  [the longest x1 2.46 us: shards(): pl.pallas_call(functools.partial(adjoint_kernel, entries, near_distances,...]
where the time goes in v6:
time: 35.4 us; the launch traced here: 35.2 us
  starting transfers between devices  14.2 us (40%)
  Pallas kernels  13.3 us (38%)
  waiting for transfers between devices  4.85 us (14%)
  matrix products  1.24 us (4%)
  local copies, waits for them, and re-layouts  0.78 us (2%)
  between operations  0.75 us (2%)
    ppermute x4, starting transfers between devices, from_peer(): return lax.ppermute(x, axis, [(peer(i, distance, n), i) for i in range(n)])  7.25 us
    ppermute x6, starting transfers between devices, to_peer(): return lax.ppermute(x, axis, [(i, peer(i, distance, n)) for i in range(n)])  6.92 us
    ppermute x6, waiting for transfers between devices, to_peer(): return lax.ppermute(x, axis, [(i, peer(i, distance, n)) for i in range(n)])  4.3 us
    pallas_call x1, Pallas kernels, shards(): pl.pallas_call(functools.partial(near_kernel, entries, near_distances, tu...  4.11 us
    pallas_call x1, Pallas kernels, shards(): pl.pallas_call(functools.partial(load_kernel, entries), out_shape=(shape(...  3.57 us
    pallas_call x1, Pallas kernels, shards(): pl.pallas_call(functools.partial(adjoint_kernel, entries, near_distances,...  2.46 us
    pallas_call x1, Pallas kernels, push(): pl.pallas_call(functools.partial(push_kernel, entries, groups[j]), out_sh...  2.26 us
    dot_general x1, matrix products, shards(): jnp.einsum('iek,ikj->iej', log_prices, io_coeffs, preferred_element_type=...  1.24 us
  transfers between devices with their start and end apart: 10, of which 4 were waited for; matrix products, arithmetic and copies ran while one was open for 0% of the time, Pallas kernels for 28%

profile of v6, /device:TPU:0, one launch (start us, length us, event | category | flops | bytes accessed | tf_op | source)
XLA Modules:
  0.0 35.2 jit_solution(12952582139243647318)
XLA Ops:
  0.6 0.0 copy-start
  0.6 0.7 %copy-done = bf16[4,16,256]{2,1,0:T(8,128)(2,1)S(1)} copy-done((bf16[4,16,256]{2,1,0:T(8,128)(2,1)S(1)}, bf16[4,16,256]{2,1,0:T(8,128)(2,1)}, u32[]{:S(2)}) %copy-start) | copy-done | bytes 32792
  1.4 1.2 %fusion.cost_ref = bf16[4,16,256]{2,1,0:T(8,128)(2,1)S(1)} fusion(bf16[4,16,256]{2,1,0:T(8,128)(2,1)S(1)} %copy-done, bf16[4,256,256]{2,1,0:T(8,128)(2,1)} %refs_4_.1, f32[4,16]{1,0:T(4,128)} %param.11, f32[4,256]{1,0:T(4,128)} %refs_5_.1), kind=kOutput, calls=%fused_computation.1 | convolution fusion | flops 8437760 | bytes 594176 | tf_op jit(solution)/shard_map/iek,ikj->iej/dot_general | solution.py:387
  2.6 4.1 %collective-permute-start = (bf16[4,16,256]{2,1,0:T(8,128)(2,1)S(1)}, bf16[4,16,256]{2,1,0:T(8,128)(2,1)S(1)}, u32[]{:S(2)}, u32[]{:S(2)}) collective-permute-start(bf16[4,16,256]{2,1,0:T(8,128)(2,1)S(1)} %fusion.cost_ref), channel_id=1, source_target_pairs={{16,0},{20,4},{24,8},{28,12},{0,16},{4,20},{8,24},{12,28},{17,1},{... | collective-permute-start | bytes 98312 | tf_op jit(solution)/shard_map/ppermute | solution.py:45
  6.7 1.3 %collective-permute-start.1 = (bf16[4,16,256]{2,1,0:T(8,128)(2,1)S(1)}, bf16[4,16,256]{2,1,0:T(8,128)(2,1)S(1)}, u32[]{:S(2)}, u32[]{:S(2)}) collective-permute-start(bf16[4,16,256]{2,1,0:T(8,128)(2,1)S(1)} %fusion.cost_ref), channel_id=1, source_target_pairs={{24,0},{28,4},{16,8},{20,12},{8,16},{12,20},{0,24},{4,28},{25,1},{... | collective-permute-start | bytes 98312 | tf_op jit(solution)/shard_map/ppermute | solution.py:45
  8.1 0.2 collective-permute-start.2
  8.3 3.6 %load.1 = (bf16[128,256,256]{2,1,0:T(8,128)(2,1)S(1)}, f32[128,256]{1,0:T(8,128)S(1)}, f32[4,16,256]{2,1,0:T(8,128)S(1)}, f32[1,256]{1,0:T(1,128)S(1)}, bf16[4,16,256]{2,1,0:T(8,128)(2,1)S(1)}, /*index=5*/s32[258]{0:T(512)S(4)}) custom-call(s32[1]{0:T(128)} %bitcast.me_ref, bf16[4,16,256]{2,1,0:T(8,128)(2,1)S(1)} %fusion.cost_ref, ...), custom_call_target="tpu_custom_call" | custom-call | bytes 8388608 | tf_op jit(solution)/shard_map/load/pallas_call | solution.py:390
  11.9 0.0 collective-permute-done.refs_6_
  11.9 0.5 %collective-permute-done.1.refs_7_ = bf16[4,16,256]{2,1,0:T(8,128)(2,1)S(1)} collective-permute-done((bf16[4,16,256]{2,1,0:T(8,128)(2,1)S(1)}, bf16[4,16,256]{2,1,0:T(8,128)(2,1)S(1)}, u32[]{:S(2)}, u32[]{:S(2)}) %collective-permute-start.1) | collective-permute-done | bytes 32800 | tf_op jit(solution)/shard_map/ppermute | solution.py:45
  12.4 0.0 collective-permute-done.2.refs_8_
  12.5 1.6 %collective-permute-start.3 = (bf16[16,16,256]{2,1,0:T(8,128)(2,1)S(1)}, bf16[16,16,256]{2,1,0:T(8,128)(2,1)S(1)}, u32[]{:S(2)}, u32[]{:S(2)}) collective-permute-start(bf16[16,16,256]{2,1,0:T(8,128)(2,1)S(1)} %pad_maximum_fusion), channel_id=1, source_target_pairs={{4,0},{0,4},{12,8},{8,12},{20,16},{16,20},{28,24},{24,28},{5,1},{1... | collective-permute-start | bytes 393224 | tf_op jit(solution)/shard_map/ppermute | solution.py:45
  14.0 4.1 %near.1 = (bf16[128,256,256]{2,1,0:T(8,128)(2,1)S(1)}, f32[64,16,256]{2,1,0:T(8,128)S(1)}, f32[5,16,256]{2,1,0:T(8,128)S(1)}, f32[5,16,256]{2,1,0:T(8,128)S(1)}, bf16[64,256,256]{2,1,0:T(8,128)(2,1)S(1)}) custom-call(s32[258]{0:T(512)S(4)} %get-tuple-element.23.refs_0_.table_ref, bf16[128,256,256]{2,1,0:T(8,128)(2,1)} %bitcast.17, ...), custom_call_target="tpu_custom_call", output_to_operand_aliasing={{0}: (2, {})} | custom-call | bytes 8388608 | tf_op jit(solution)/shard_map/near/pallas_call | solution.py:446
  18.2 0.0 collective-permute-done.3.refs_9_
  18.2 0.0 copy-start.1
  18.2 0.0 copy-start.2
  18.2 2.5 %adjoint.1 = (bf16[128,16,256]{2,1,0:T(8,128)(2,1)S(1)}, f32[128,256]{1,0:T(8,128)S(1)}, f32[4,16,256]{2,1,0:T(8,128)S(1)}, bf16[16,16,256]{2,1,0:T(8,128)(2,1)S(1)}) custom-call(s32[258]{0:T(512)S(4)} %get-tuple-element.23.refs_0_.table_ref, bf16[128,256,256]{2,1,0:T(8,128)(2,1)S(1)} %get-tuple-element.28.refs_1_.held_ref, ...), custom_call_target="tpu_custom_call" | custom-call | bytes 8388608 | tf_op jit(solution)/shard_map/adjoint/pallas_call | solution.py:460
  20.7 0.0 collective-permute-start.8
  20.7 0.9 %collective-permute-start.4 = (bf16[16,16,256]{2,1,0:T(8,128)(2,1)S(1)}, bf16[16,16,256]{2,1,0:T(8,128)(2,1)S(1)}, u32[]{:S(2)}, u32[]{:S(2)}) collective-permute-start(bf16[16,16,256]{2,1,0:T(8,128)(2,1)S(1)} %get-tuple-element.35), channel_id=1, source_target_pairs={{0,4},{4,0},{8,12},{12,8},{16,20},{20,16},{24,28},{28,24},{1,5},{5... | collective-permute-start | bytes 393224 | tf_op jit(solution)/shard_map/ppermute | solution.py:49
  21.6 2.3 %push.1 = f32[16,16,256]{2,1,0:T(8,128)S(1)} custom-call(s32[258]{0:T(512)S(4)} %get-tuple-element.23.refs_0_.table_ref, bf16[128,256,256]{2,1,0:T(8,128)(2,1)S(1)} %get-tuple-element.28.refs_1_.held_ref, bf16[128,16,256]{2,1,0:T(8,128)(2,1)S(1)} %get-tuple-element.34.adjoint_ref), custom_call_target="tpu_custom_call" | custom-call | bytes 8388608 | tf_op jit(solution)/shard_map/push/pallas_call | solution.py:482
  23.8 0.0 collective-permute-done.8.y_ref
  23.9 1.6 %collective-permute-start.9 = (f32[128,256]{1,0:T(8,128)S(1)}, f32[128,256]{1,0:T(8,128)S(1)}, u32[]{:S(2)}, u32[]{:S(2)}) collective-permute-start(f32[128,256]{1,0:T(8,128)S(1)} %add.13.refs_8_), channel_id=1, source_target_pairs={{0,2},{1,3},{2,0},{3,1},{4,6},{5,7},{6,4},{7,5},{8,10},{9,11},{10,... | collective-permute-start | bytes 393224 | tf_op jit(solution)/shard_map/ppermute | solution.py:49
  25.4 1.2 %collective-permute-done.4 = bf16[16,16,256]{2,1,0:T(8,128)(2,1)S(1)} collective-permute-done((bf16[16,16,256]{2,1,0:T(8,128)(2,1)S(1)}, bf16[16,16,256]{2,1,0:T(8,128)(2,1)S(1)}, u32[]{:S(2)}, u32[]{:S(2)}) %collective-permute-start.4) | collective-permute-done | bytes 131104 | tf_op jit(solution)/shard_map/ppermute | solution.py:49
  26.7 2.5 %collective-permute-start.5 = (bf16[4,16,256]{2,1,0:T(8,128)(2,1)S(1)}, bf16[4,16,256]{2,1,0:T(8,128)(2,1)S(1)}, u32[]{:S(2)}, u32[]{:S(2)}) collective-permute-start(bf16[4,16,256]{2,1,0:T(8,128)(2,1)S(1)} %get-tuple-element.44), channel_id=1, source_target_pairs={{0,24},{4,28},{8,16},{12,20},{16,8},{20,12},{24,0},{28,4},{1,25},{... | collective-permute-start | bytes 98312 | tf_op jit(solution)/shard_map/ppermute | solution.py:49
  29.2 0.3 collective-permute-start.6
  29.5 1.7 %collective-permute-start.7 = (bf16[4,16,256]{2,1,0:T(8,128)(2,1)S(1)}, bf16[4,16,256]{2,1,0:T(8,128)(2,1)S(1)}, u32[]{:S(2)}, u32[]{:S(2)}) collective-permute-start(bf16[4,16,256]{2,1,0:T(8,128)(2,1)S(1)} %get-tuple-element.42), channel_id=1, source_target_pairs={{0,8},{4,12},{8,0},{12,4},{16,24},{20,28},{24,16},{28,20},{1,9},{5... | collective-permute-start | bytes 98312 | tf_op jit(solution)/shard_map/ppermute | solution.py:49
  31.2 1.5 %collective-permute-done.5.refs_1_ = bf16[4,16,256]{2,1,0:T(8,128)(2,1)S(1)} collective-permute-done((bf16[4,16,256]{2,1,0:T(8,128)(2,1)S(1)}, bf16[4,16,256]{2,1,0:T(8,128)(2,1)S(1)}, u32[]{:S(2)}, u32[]{:S(2)}) %collective-permute-start.5) | collective-permute-done | bytes 32800 | tf_op jit(solution)/shard_map/ppermute | solution.py:49
  32.7 1.6 %collective-permute-done.6.refs_2_ = bf16[4,16,256]{2,1,0:T(8,128)(2,1)S(1)} collective-permute-done((bf16[4,16,256]{2,1,0:T(8,128)(2,1)S(1)}, bf16[4,16,256]{2,1,0:T(8,128)(2,1)S(1)}, u32[]{:S(2)}, u32[]{:S(2)}) %collective-permute-start.6) | collective-permute-done | bytes 32800 | tf_op jit(solution)/shard_map/ppermute | solution.py:49
  34.3 0.0 collective-permute-done.7.refs_3_
  34.3 0.0 collective-permute-done.9.refs_9_
  34.3 0.0 copy-done.1
  34.3 0.0 copy-done.2
  34.3 0.9 %finish.1 = (bf16[4,16,256]{2,1,0:T(8,128)(2,1)}, f32[4,16,256]{2,1,0:T(8,128)}, f32[4,16]{1,0:T(4,128)}, f32[128,256]{1,0:T(8,128)}) custom-call(f32[4,16,256]{2,1,0:T(8,128)S(1)} %slice_bitcast_fusion.refs_0_, bf16[4,16,256]{2,1,0:T(8,128)(2,1)S(1)} %collective-permute-done.5.refs_1_, bf16[4,16,256]{2,1,0:T(8,128)(2,1)S(1)} %collective-permute-done.6.refs_2_, ...), custom_call_target="tpu_custom_call" | custom-call | tf_op jit(solution)/shard_map/finish/pallas_call | solution.py:530
  (6 shorter events, 0.1 us)
Async XLA Ops:
  0.6 0.8 %copy-start = (bf16[4,16,256]{2,1,0:T(8,128)(2,1)S(1)}, bf16[4,16,256]{2,1,0:T(8,128)(2,1)}, u32[]{:S(2)}) copy-start(bf16[4,16,256]{2,1,0:T(8,128)(2,1)} %param.10) | copy-start | bytes 98308
  2.6 9.2 %collective-permute-start = (bf16[4,16,256]{2,1,0:T(8,128)(2,1)S(1)}, bf16[4,16,256]{2,1,0:T(8,128)(2,1)S(1)}, u32[]{:S(2)}, u32[]{:S(2)}) collective-permute-start(bf16[4,16,256]{2,1,0:T(8,128)(2,1)S(1)} %fusion.cost_ref), channel_id=1, source_target_pairs={{16,0},{20,4},{24,8},{28,12},{0,16},{4,20},{8,24},{12,28},{17,1},{... | collective-permute-start | bytes 98312 | tf_op jit(solution)/shard_map/ppermute | solution.py:45
  6.7 5.7 %collective-permute-start.1 = (bf16[4,16,256]{2,1,0:T(8,128)(2,1)S(1)}, bf16[4,16,256]{2,1,0:T(8,128)(2,1)S(1)}, u32[]{:S(2)}, u32[]{:S(2)}) collective-permute-start(bf16[4,16,256]{2,1,0:T(8,128)(2,1)S(1)} %fusion.cost_ref), channel_id=1, source_target_pairs={{24,0},{28,4},{16,8},{20,12},{8,16},{12,20},{0,24},{4,28},{25,1},{... | collective-permute-start | bytes 98312 | tf_op jit(solution)/shard_map/ppermute | solution.py:45
  8.1 4.4 %collective-permute-start.2 = (bf16[4,16,256]{2,1,0:T(8,128)(2,1)S(1)}, bf16[4,16,256]{2,1,0:T(8,128)(2,1)S(1)}, u32[]{:S(2)}, u32[]{:S(2)}) collective-permute-start(bf16[4,16,256]{2,1,0:T(8,128)(2,1)S(1)} %fusion.cost_ref), channel_id=1, source_target_pairs={{8,0},{12,4},{0,8},{4,12},{24,16},{28,20},{16,24},{20,28},{9,1},{1... | collective-permute-start | bytes 98312 | tf_op jit(solution)/shard_map/ppermute | solution.py:45
  12.5 5.7 %collective-permute-start.3 = (bf16[16,16,256]{2,1,0:T(8,128)(2,1)S(1)}, bf16[16,16,256]{2,1,0:T(8,128)(2,1)S(1)}, u32[]{:S(2)}, u32[]{:S(2)}) collective-permute-start(bf16[16,16,256]{2,1,0:T(8,128)(2,1)S(1)} %pad_maximum_fusion), channel_id=1, source_target_pairs={{4,0},{0,4},{12,8},{8,12},{20,16},{16,20},{28,24},{24,28},{5,1},{1... | collective-permute-start | bytes 393224 | tf_op jit(solution)/shard_map/ppermute | solution.py:45
  18.2 16.1 %copy-start.1 = (bf16[4,256,256]{2,1,0:T(8,128)(2,1)S(1)}, bf16[4,256,256]{2,1,0:T(8,128)(2,1)}, u32[]{:S(2)}) copy-start(bf16[4,256,256]{2,1,0:T(8,128)(2,1)} %refs_4_.1) | copy-start | bytes 1572868
  18.2 16.1 %copy-start.2 = (f32[4,256]{1,0:T(4,128)S(1)}, f32[4,256]{1,0:T(4,128)}, u32[]{:S(2)}) copy-start(f32[4,256]{1,0:T(4,128)} %refs_5_.1) | copy-start | bytes 12292
  20.7 3.2 %collective-permute-start.8 = (f32[128,256]{1,0:T(8,128)S(1)}, f32[128,256]{1,0:T(8,128)S(1)}, u32[]{:S(2)}, u32[]{:S(2)}) collective-permute-start(f32[128,256]{1,0:T(8,128)S(1)} %get-tuple-element.37.x_ref), channel_id=1, source_target_pairs={{0,1},{1,0},{2,3},{3,2},{4,5},{5,4},{6,7},{7,6},{8,9},{9,8},{10,11... | collective-permute-start | bytes 393224 | tf_op jit(solution)/shard_map/ppermute | solution.py:49
  20.7 5.9 %collective-permute-start.4 = (bf16[16,16,256]{2,1,0:T(8,128)(2,1)S(1)}, bf16[16,16,256]{2,1,0:T(8,128)(2,1)S(1)}, u32[]{:S(2)}, u32[]{:S(2)}) collective-permute-start(bf16[16,16,256]{2,1,0:T(8,128)(2,1)S(1)} %get-tuple-element.35), channel_id=1, source_target_pairs={{0,4},{4,0},{8,12},{12,8},{16,20},{20,16},{24,28},{28,24},{1,5},{5... | collective-permute-start | bytes 393224 | tf_op jit(solution)/shard_map/ppermute | solution.py:49
  23.9 10.4 %collective-permute-start.9 = (f32[128,256]{1,0:T(8,128)S(1)}, f32[128,256]{1,0:T(8,128)S(1)}, u32[]{:S(2)}, u32[]{:S(2)}) collective-permute-start(f32[128,256]{1,0:T(8,128)S(1)} %add.13.refs_8_), channel_id=1, source_target_pairs={{0,2},{1,3},{2,0},{3,1},{4,6},{5,7},{6,4},{7,5},{8,10},{9,11},{10,... | collective-permute-start | bytes 393224 | tf_op jit(solution)/shard_map/ppermute | solution.py:49
  26.7 6.0 %collective-permute-start.5 = (bf16[4,16,256]{2,1,0:T(8,128)(2,1)S(1)}, bf16[4,16,256]{2,1,0:T(8,128)(2,1)S(1)}, u32[]{:S(2)}, u32[]{:S(2)}) collective-permute-start(bf16[4,16,256]{2,1,0:T(8,128)(2,1)S(1)} %get-tuple-element.44), channel_id=1, source_target_pairs={{0,24},{4,28},{8,16},{12,20},{16,8},{20,12},{24,0},{28,4},{1,25},{... | collective-permute-start | bytes 98312 | tf_op jit(solution)/shard_map/ppermute | solution.py:49
  29.2 5.1 %collective-permute-start.6 = (bf16[4,16,256]{2,1,0:T(8,128)(2,1)S(1)}, bf16[4,16,256]{2,1,0:T(8,128)(2,1)S(1)}, u32[]{:S(2)}, u32[]{:S(2)}) collective-permute-start(bf16[4,16,256]{2,1,0:T(8,128)(2,1)S(1)} %get-tuple-element.43), channel_id=1, source_target_pairs={{0,16},{4,20},{8,24},{12,28},{16,0},{20,4},{24,8},{28,12},{1,17},{... | collective-permute-start | bytes 98312 | tf_op jit(solution)/shard_map/ppermute | solution.py:49
  29.5 4.8 %collective-permute-start.7 = (bf16[4,16,256]{2,1,0:T(8,128)(2,1)S(1)}, bf16[4,16,256]{2,1,0:T(8,128)(2,1)S(1)}, u32[]{:S(2)}, u32[]{:S(2)}) collective-permute-start(bf16[4,16,256]{2,1,0:T(8,128)(2,1)S(1)} %get-tuple-element.42), channel_id=1, source_target_pairs={{0,8},{4,12},{8,0},{12,4},{16,24},{20,28},{24,16},{28,20},{1,9},{5... | collective-permute-start | bytes 98312 | tf_op jit(solution)/shard_map/ppermute | solution.py:49

commit v7 on v6

--- a/solution.py
+++ b/solution.py
@@ -333,7 +333,7 @@
                 else:
                     adjoint_ref[entry] = value
     partial_ref[...] = total_ref[...].astype(BF16)
-    tau_grad_ref[...] = tau_rows_ref[pl.ds(0, entries.slot_count)]
+    tau_grad_ref[...] = tau_rows_ref[pl.ds(0, entries.slot_count)].astype(tau_grad_ref.dtype)
 
 
 def push_kernel(entries, distances, table_ref, held_ref, adjoint_ref, partial_ref, total_ref):
@@ -461,7 +461,7 @@
         functools.partial(adjoint_kernel, entries, near_distances, far_distances, groups[-1], turned),
         out_shape=(
             shape((entries.count,) + row, BF16),
-            shape((own * slots, sectors), F32),
+            shape((own * slots, sectors), BF16),
             shape((own,) + row, F32),
             shape(partial_dims, BF16),
         ),
@@ -524,7 +524,7 @@
             tau_received = to_peer(tau_grad, distance, "ep", ep_count)
             distance *= 2
     else:
-        tau_grad = lax.psum(tau_grad, "ep")
+        tau_grad = lax.psum(tau_grad.astype(F32), "ep")
         tau_received = jnp.zeros_like(tau_grad)
 
     new_prices, price_grad, wage_grad, tau_grad = pl.pallas_call(

time: 35.4 us -> 34.5 us (0.975)
  waiting for transfers between devices: 4.85 us -> 3.96 us
    ppermute x6, waiting for transfers between devices: 4.3 us -> 3.41 us  [to_peer(): return lax.ppermute(x, axis, [(i, peer(i, distance, n)) for i in range(n)])]
  transfers between devices with their start and end apart: 10 -> 10, of which waited for: 4 -> 4; matrix products, arithmetic and copies ran while one was open for 0% -> 0% of each run, Pallas kernels for 28% -> 29%
where the time goes in v7:
time: 34.5 us; the launch traced here: 34.2 us
  starting transfers between devices  14.1 us (41%)
  Pallas kernels  13.3 us (39%)
  waiting for transfers between devices  3.96 us (11%)
  matrix products  1.24 us (4%)
  local copies, waits for them, and re-layouts  0.78 us (2%)
  between operations  0.74 us (2%)
    ppermute x4, starting transfers between devices, from_peer(): return lax.ppermute(x, axis, [(peer(i, distance, n), i) for i in range(n)])  7.25 us
    ppermute x6, starting transfers between devices, to_peer(): return lax.ppermute(x, axis, [(i, peer(i, distance, n)) for i in range(n)])  6.85 us
    pallas_call x1, Pallas kernels, shards(): pl.pallas_call(functools.partial(near_kernel, entries, near_distances, tu...  4.11 us
    pallas_call x1, Pallas kernels, shards(): pl.pallas_call(functools.partial(load_kernel, entries), out_shape=(shape(...  3.57 us
    ppermute x6, waiting for transfers between devices, to_peer(): return lax.ppermute(x, axis, [(i, peer(i, distance, n)) for i in range(n)])  3.41 us
    pallas_call x1, Pallas kernels, shards(): pl.pallas_call(functools.partial(adjoint_kernel, entries, near_distances,...  2.46 us
    pallas_call x1, Pallas kernels, push(): pl.pallas_call(functools.partial(push_kernel, entries, groups[j]), out_sh...  2.26 us
    dot_general x1, matrix products, shards(): jnp.einsum('iek,ikj->iej', log_prices, io_coeffs, preferred_element_type=...  1.24 us
  transfers between devices with their start and end apart: 10, of which 4 were waited for; matrix products, arithmetic and copies ran while one was open for 0% of the time, Pallas kernels for 29%

profile of v7, /device:TPU:0, one launch (start us, length us, event | category | flops | bytes accessed | tf_op | source)
XLA Modules:
  0.0 34.2 jit_solution(2940473875181225591)
XLA Ops:
  0.6 0.0 copy-start
  0.6 0.7 %copy-done = bf16[4,16,256]{2,1,0:T(8,128)(2,1)S(1)} copy-done((bf16[4,16,256]{2,1,0:T(8,128)(2,1)S(1)}, bf16[4,16,256]{2,1,0:T(8,128)(2,1)}, u32[]{:S(2)}) %copy-start) | copy-done | bytes 32792
  1.4 1.2 %fusion.cost_ref = bf16[4,16,256]{2,1,0:T(8,128)(2,1)S(1)} fusion(bf16[4,16,256]{2,1,0:T(8,128)(2,1)S(1)} %copy-done, bf16[4,256,256]{2,1,0:T(8,128)(2,1)} %refs_4_.1, f32[4,16]{1,0:T(4,128)} %param.11, f32[4,256]{1,0:T(4,128)} %refs_5_.1), kind=kOutput, calls=%fused_computation.1 | convolution fusion | flops 8437760 | bytes 594176 | tf_op jit(solution)/shard_map/iek,ikj->iej/dot_general | solution.py:387
  2.6 4.1 %collective-permute-start = (bf16[4,16,256]{2,1,0:T(8,128)(2,1)S(1)}, bf16[4,16,256]{2,1,0:T(8,128)(2,1)S(1)}, u32[]{:S(2)}, u32[]{:S(2)}) collective-permute-start(bf16[4,16,256]{2,1,0:T(8,128)(2,1)S(1)} %fusion.cost_ref), channel_id=1, source_target_pairs={{16,0},{20,4},{24,8},{28,12},{0,16},{4,20},{8,24},{12,28},{17,1},{... | collective-permute-start | bytes 98312 | tf_op jit(solution)/shard_map/ppermute | solution.py:45
  6.7 1.3 %collective-permute-start.1 = (bf16[4,16,256]{2,1,0:T(8,128)(2,1)S(1)}, bf16[4,16,256]{2,1,0:T(8,128)(2,1)S(1)}, u32[]{:S(2)}, u32[]{:S(2)}) collective-permute-start(bf16[4,16,256]{2,1,0:T(8,128)(2,1)S(1)} %fusion.cost_ref), channel_id=1, source_target_pairs={{24,0},{28,4},{16,8},{20,12},{8,16},{12,20},{0,24},{4,28},{25,1},{... | collective-permute-start | bytes 98312 | tf_op jit(solution)/shard_map/ppermute | solution.py:45
  8.1 0.2 collective-permute-start.2
  8.3 3.6 %load.1 = (bf16[128,256,256]{2,1,0:T(8,128)(2,1)S(1)}, f32[128,256]{1,0:T(8,128)S(1)}, f32[4,16,256]{2,1,0:T(8,128)S(1)}, f32[1,256]{1,0:T(1,128)S(1)}, bf16[4,16,256]{2,1,0:T(8,128)(2,1)S(1)}, /*index=5*/s32[258]{0:T(512)S(4)}) custom-call(s32[1]{0:T(128)} %bitcast.me_ref, bf16[4,16,256]{2,1,0:T(8,128)(2,1)S(1)} %fusion.cost_ref, ...), custom_call_target="tpu_custom_call" | custom-call | bytes 8388608 | tf_op jit(solution)/shard_map/load/pallas_call | solution.py:390
  11.9 0.0 collective-permute-done.refs_6_
  11.9 0.5 %collective-permute-done.1.refs_7_ = bf16[4,16,256]{2,1,0:T(8,128)(2,1)S(1)} collective-permute-done((bf16[4,16,256]{2,1,0:T(8,128)(2,1)S(1)}, bf16[4,16,256]{2,1,0:T(8,128)(2,1)S(1)}, u32[]{:S(2)}, u32[]{:S(2)}) %collective-permute-start.1) | collective-permute-done | bytes 32800 | tf_op jit(solution)/shard_map/ppermute | solution.py:45
  12.4 0.0 collective-permute-done.2.refs_8_
  12.5 1.6 %collective-permute-start.3 = (bf16[16,16,256]{2,1,0:T(8,128)(2,1)S(1)}, bf16[16,16,256]{2,1,0:T(8,128)(2,1)S(1)}, u32[]{:S(2)}, u32[]{:S(2)}) collective-permute-start(bf16[16,16,256]{2,1,0:T(8,128)(2,1)S(1)} %pad_maximum_fusion), channel_id=1, source_target_pairs={{4,0},{0,4},{12,8},{8,12},{20,16},{16,20},{28,24},{24,28},{5,1},{1... | collective-permute-start | bytes 393224 | tf_op jit(solution)/shard_map/ppermute | solution.py:45
  14.0 4.1 %near.1 = (bf16[128,256,256]{2,1,0:T(8,128)(2,1)S(1)}, f32[64,16,256]{2,1,0:T(8,128)S(1)}, f32[5,16,256]{2,1,0:T(8,128)S(1)}, f32[5,16,256]{2,1,0:T(8,128)S(1)}, bf16[64,256,256]{2,1,0:T(8,128)(2,1)S(1)}) custom-call(s32[258]{0:T(512)S(4)} %get-tuple-element.23.refs_0_.table_ref, bf16[128,256,256]{2,1,0:T(8,128)(2,1)} %bitcast.17, ...), custom_call_target="tpu_custom_call", output_to_operand_aliasing={{0}: (2, {})} | custom-call | bytes 8388608 | tf_op jit(solution)/shard_map/near/pallas_call | solution.py:446
  18.2 0.0 collective-permute-done.3.refs_9_
  18.2 0.0 copy-start.1
  18.2 0.0 copy-start.2
  18.2 2.5 %adjoint.1 = (bf16[128,16,256]{2,1,0:T(8,128)(2,1)S(1)}, bf16[128,256]{1,0:T(8,128)(2,1)S(1)}, f32[4,16,256]{2,1,0:T(8,128)S(1)}, bf16[16,16,256]{2,1,0:T(8,128)(2,1)S(1)}) custom-call(s32[258]{0:T(512)S(4)} %get-tuple-element.23.refs_0_.table_ref, bf16[128,256,256]{2,1,0:T(8,128)(2,1)S(1)} %get-tuple-element.28.refs_1_.held_ref, ...), custom_call_target="tpu_custom_call" | custom-call | bytes 8388608 | tf_op jit(solution)/shard_map/adjoint/pallas_call | solution.py:460
  20.7 0.8 %collective-permute-start.4 = (bf16[16,16,256]{2,1,0:T(8,128)(2,1)S(1)}, bf16[16,16,256]{2,1,0:T(8,128)(2,1)S(1)}, u32[]{:S(2)}, u32[]{:S(2)}) collective-permute-start(bf16[16,16,256]{2,1,0:T(8,128)(2,1)S(1)} %get-tuple-element.35), channel_id=1, source_target_pairs={{0,4},{4,0},{8,12},{12,8},{16,20},{20,16},{24,28},{28,24},{1,5},{5... | collective-permute-start | bytes 393224 | tf_op jit(solution)/shard_map/ppermute | solution.py:49
  21.5 0.0 collective-permute-start.8
  21.5 2.3 %push.1 = f32[16,16,256]{2,1,0:T(8,128)S(1)} custom-call(s32[258]{0:T(512)S(4)} %get-tuple-element.23.refs_0_.table_ref, bf16[128,256,256]{2,1,0:T(8,128)(2,1)S(1)} %get-tuple-element.28.refs_1_.held_ref, bf16[128,16,256]{2,1,0:T(8,128)(2,1)S(1)} %get-tuple-element.34.adjoint_ref), custom_call_target="tpu_custom_call" | custom-call | bytes 8388608 | tf_op jit(solution)/shard_map/push/pallas_call | solution.py:482
  23.8 0.0 collective-permute-done.8.y_ref
  23.8 1.6 %collective-permute-start.9 = (f32[128,256]{1,0:T(8,128)S(1)}, f32[128,256]{1,0:T(8,128)S(1)}, u32[]{:S(2)}, u32[]{:S(2)}) collective-permute-start(f32[128,256]{1,0:T(8,128)S(1)} %add.13.refs_8_), channel_id=1, source_target_pairs={{0,2},{1,3},{2,0},{3,1},{4,6},{5,7},{6,4},{7,5},{8,10},{9,11},{10,... | collective-permute-start | bytes 393224 | tf_op jit(solution)/shard_map/ppermute | solution.py:49
  25.4 0.3 collective-permute-done.4
  25.7 2.5 %collective-permute-start.5 = (bf16[4,16,256]{2,1,0:T(8,128)(2,1)S(1)}, bf16[4,16,256]{2,1,0:T(8,128)(2,1)S(1)}, u32[]{:S(2)}, u32[]{:S(2)}) collective-permute-start(bf16[4,16,256]{2,1,0:T(8,128)(2,1)S(1)} %get-tuple-element.44), channel_id=1, source_target_pairs={{0,24},{4,28},{8,16},{12,20},{16,8},{20,12},{24,0},{28,4},{1,25},{... | collective-permute-start | bytes 98312 | tf_op jit(solution)/shard_map/ppermute | solution.py:49
  28.2 0.3 collective-permute-start.6
  28.5 1.7 %collective-permute-start.7 = (bf16[4,16,256]{2,1,0:T(8,128)(2,1)S(1)}, bf16[4,16,256]{2,1,0:T(8,128)(2,1)S(1)}, u32[]{:S(2)}, u32[]{:S(2)}) collective-permute-start(bf16[4,16,256]{2,1,0:T(8,128)(2,1)S(1)} %get-tuple-element.42), channel_id=1, source_target_pairs={{0,8},{4,12},{8,0},{12,4},{16,24},{20,28},{24,16},{28,20},{1,9},{5... | collective-permute-start | bytes 98312 | tf_op jit(solution)/shard_map/ppermute | solution.py:49
  30.2 1.6 %collective-permute-done.5.refs_1_ = bf16[4,16,256]{2,1,0:T(8,128)(2,1)S(1)} collective-permute-done((bf16[4,16,256]{2,1,0:T(8,128)(2,1)S(1)}, bf16[4,16,256]{2,1,0:T(8,128)(2,1)S(1)}, u32[]{:S(2)}, u32[]{:S(2)}) %collective-permute-start.5) | collective-permute-done | bytes 32800 | tf_op jit(solution)/shard_map/ppermute | solution.py:49
  31.8 1.5 %collective-permute-done.6.refs_2_ = bf16[4,16,256]{2,1,0:T(8,128)(2,1)S(1)} collective-permute-done((bf16[4,16,256]{2,1,0:T(8,128)(2,1)S(1)}, bf16[4,16,256]{2,1,0:T(8,128)(2,1)S(1)}, u32[]{:S(2)}, u32[]{:S(2)}) %collective-permute-start.6) | collective-permute-done | bytes 32800 | tf_op jit(solution)/shard_map/ppermute | solution.py:49
  33.3 0.0 collective-permute-done.7.refs_3_
  33.3 0.0 collective-permute-done.9.refs_9_
  33.3 0.0 copy-done.1
  33.3 0.0 copy-done.2
  33.3 0.9 %finish.1 = (bf16[4,16,256]{2,1,0:T(8,128)(2,1)}, f32[4,16,256]{2,1,0:T(8,128)}, f32[4,16]{1,0:T(4,128)}, f32[128,256]{1,0:T(8,128)}) custom-call(f32[4,16,256]{2,1,0:T(8,128)S(1)} %slice_bitcast_fusion.refs_0_, bf16[4,16,256]{2,1,0:T(8,128)(2,1)S(1)} %collective-permute-done.5.refs_1_, bf16[4,16,256]{2,1,0:T(8,128)(2,1)S(1)} %collective-permute-done.6.refs_2_, ...), custom_call_target="tpu_custom_call" | custom-call | tf_op jit(solution)/shard_map/finish/pallas_call | solution.py:530
  (6 shorter events, 0.1 us)
Async XLA Ops:
  0.6 0.8 %copy-start = (bf16[4,16,256]{2,1,0:T(8,128)(2,1)S(1)}, bf16[4,16,256]{2,1,0:T(8,128)(2,1)}, u32[]{:S(2)}) copy-start(bf16[4,16,256]{2,1,0:T(8,128)(2,1)} %param.10) | copy-start | bytes 98308
  2.6 9.2 %collective-permute-start = (bf16[4,16,256]{2,1,0:T(8,128)(2,1)S(1)}, bf16[4,16,256]{2,1,0:T(8,128)(2,1)S(1)}, u32[]{:S(2)}, u32[]{:S(2)}) collective-permute-start(bf16[4,16,256]{2,1,0:T(8,128)(2,1)S(1)} %fusion.cost_ref), channel_id=1, source_target_pairs={{16,0},{20,4},{24,8},{28,12},{0,16},{4,20},{8,24},{12,28},{17,1},{... | collective-permute-start | bytes 98312 | tf_op jit(solution)/shard_map/ppermute | solution.py:45
  6.7 5.7 %collective-permute-start.1 = (bf16[4,16,256]{2,1,0:T(8,128)(2,1)S(1)}, bf16[4,16,256]{2,1,0:T(8,128)(2,1)S(1)}, u32[]{:S(2)}, u32[]{:S(2)}) collective-permute-start(bf16[4,16,256]{2,1,0:T(8,128)(2,1)S(1)} %fusion.cost_ref), channel_id=1, source_target_pairs={{24,0},{28,4},{16,8},{20,12},{8,16},{12,20},{0,24},{4,28},{25,1},{... | collective-permute-start | bytes 98312 | tf_op jit(solution)/shard_map/ppermute | solution.py:45
  8.1 4.4 %collective-permute-start.2 = (bf16[4,16,256]{2,1,0:T(8,128)(2,1)S(1)}, bf16[4,16,256]{2,1,0:T(8,128)(2,1)S(1)}, u32[]{:S(2)}, u32[]{:S(2)}) collective-permute-start(bf16[4,16,256]{2,1,0:T(8,128)(2,1)S(1)} %fusion.cost_ref), channel_id=1, source_target_pairs={{8,0},{12,4},{0,8},{4,12},{24,16},{28,20},{16,24},{20,28},{9,1},{1... | collective-permute-start | bytes 98312 | tf_op jit(solution)/shard_map/ppermute | solution.py:45
  12.5 5.7 %collective-permute-start.3 = (bf16[16,16,256]{2,1,0:T(8,128)(2,1)S(1)}, bf16[16,16,256]{2,1,0:T(8,128)(2,1)S(1)}, u32[]{:S(2)}, u32[]{:S(2)}) collective-permute-start(bf16[16,16,256]{2,1,0:T(8,128)(2,1)S(1)} %pad_maximum_fusion), channel_id=1, source_target_pairs={{4,0},{0,4},{12,8},{8,12},{20,16},{16,20},{28,24},{24,28},{5,1},{1... | collective-permute-start | bytes 393224 | tf_op jit(solution)/shard_map/ppermute | solution.py:45
  18.2 15.1 %copy-start.1 = (bf16[4,256,256]{2,1,0:T(8,128)(2,1)S(1)}, bf16[4,256,256]{2,1,0:T(8,128)(2,1)}, u32[]{:S(2)}) copy-start(bf16[4,256,256]{2,1,0:T(8,128)(2,1)} %refs_4_.1) | copy-start | bytes 1572868
  18.2 15.1 %copy-start.2 = (f32[4,256]{1,0:T(4,128)S(1)}, f32[4,256]{1,0:T(4,128)}, u32[]{:S(2)}) copy-start(f32[4,256]{1,0:T(4,128)} %refs_5_.1) | copy-start | bytes 12292
  20.7 5.0 %collective-permute-start.4 = (bf16[16,16,256]{2,1,0:T(8,128)(2,1)S(1)}, bf16[16,16,256]{2,1,0:T(8,128)(2,1)S(1)}, u32[]{:S(2)}, u32[]{:S(2)}) collective-permute-start(bf16[16,16,256]{2,1,0:T(8,128)(2,1)S(1)} %get-tuple-element.35), channel_id=1, source_target_pairs={{0,4},{4,0},{8,12},{12,8},{16,20},{20,16},{24,28},{28,24},{1,5},{5... | collective-permute-start | bytes 393224 | tf_op jit(solution)/shard_map/ppermute | solution.py:49
  21.5 2.3 %collective-permute-start.8 = (bf16[128,256]{1,0:T(8,128)(2,1)S(1)}, bf16[128,256]{1,0:T(8,128)(2,1)S(1)}, u32[]{:S(2)}, u32[]{:S(2)}) collective-permute-start(bf16[128,256]{1,0:T(8,128)(2,1)S(1)} %get-tuple-element.37.x_ref), channel_id=1, source_target_pairs={{0,1},{1,0},{2,3},{3,2},{4,5},{5,4},{6,7},{7,6},{8,9},{9,8},{10,11... | collective-permute-start | bytes 196616 | tf_op jit(solution)/shard_map/ppermute | solution.py:49
  23.8 9.5 %collective-permute-start.9 = (f32[128,256]{1,0:T(8,128)S(1)}, f32[128,256]{1,0:T(8,128)S(1)}, u32[]{:S(2)}, u32[]{:S(2)}) collective-permute-start(f32[128,256]{1,0:T(8,128)S(1)} %add.13.refs_8_), channel_id=1, source_target_pairs={{0,2},{1,3},{2,0},{3,1},{4,6},{5,7},{6,4},{7,5},{8,10},{9,11},{10,... | collective-permute-start | bytes 393224 | tf_op jit(solution)/shard_map/ppermute | solution.py:49
  25.7 6.1 %collective-permute-start.5 = (bf16[4,16,256]{2,1,0:T(8,128)(2,1)S(1)}, bf16[4,16,256]{2,1,0:T(8,128)(2,1)S(1)}, u32[]{:S(2)}, u32[]{:S(2)}) collective-permute-start(bf16[4,16,256]{2,1,0:T(8,128)(2,1)S(1)} %get-tuple-element.44), channel_id=1, source_target_pairs={{0,24},{4,28},{8,16},{12,20},{16,8},{20,12},{24,0},{28,4},{1,25},{... | collective-permute-start | bytes 98312 | tf_op jit(solution)/shard_map/ppermute | solution.py:49
  28.2 5.1 %collective-permute-start.6 = (bf16[4,16,256]{2,1,0:T(8,128)(2,1)S(1)}, bf16[4,16,256]{2,1,0:T(8,128)(2,1)S(1)}, u32[]{:S(2)}, u32[]{:S(2)}) collective-permute-start(bf16[4,16,256]{2,1,0:T(8,128)(2,1)S(1)} %get-tuple-element.43), channel_id=1, source_target_pairs={{0,16},{4,20},{8,24},{12,28},{16,0},{20,4},{24,8},{28,12},{1,17},{... | collective-permute-start | bytes 98312 | tf_op jit(solution)/shard_map/ppermute | solution.py:49
  28.5 4.8 %collective-permute-start.7 = (bf16[4,16,256]{2,1,0:T(8,128)(2,1)S(1)}, bf16[4,16,256]{2,1,0:T(8,128)(2,1)S(1)}, u32[]{:S(2)}, u32[]{:S(2)}) collective-permute-start(bf16[4,16,256]{2,1,0:T(8,128)(2,1)S(1)} %get-tuple-element.42), channel_id=1, source_target_pairs={{0,8},{4,12},{8,0},{12,4},{16,24},{20,28},{24,16},{28,20},{1,9},{5... | collective-permute-start | bytes 98312 | tf_op jit(solution)/shard_map/ppermute | solution.py:49

commit v8 on v7

--- a/solution.py
+++ b/solution.py
@@ -82,7 +82,7 @@
     def turned(self, distances):
         if not self.dense:
             return []
-        return self.numbers(distances)
+        return [entry for entry in self.numbers(distances) if self.importer(None, entry) < max(self.own - 1, 1)]
 
     def slot(self, table, entry):
         return table[entry]
@@ -235,10 +235,12 @@
     )
 
 
-def push_entries(entries, distances, table_ref, adjoint_of, held_ref, total_ref):
+def push_entries(entries, distances, table_ref, adjoint_of, held_ref, total_ref, turned_ref):
     own, capacity = entries.own, entries.capacity
 
     def pushed(entry):
+        if entry in turned:
+            return jnp.dot(adjoint_of(entry), turned_ref[turned.index(entry)], preferred_element_type=F32)
         return lax.dot_general(
             adjoint_of(entry),
             held_ref[entries.slot(table_ref, entry)],
@@ -246,9 +248,14 @@
             preferred_element_type=F32,
         )
 
+    turned = []
     if entries.dense:
+        turned = [entry for entry in entries.numbers(distances) if entries.importer(None, entry) < own // 2]
         for block, distance in enumerate(distances):
             for place in range(own):
+                for r in range(own // 2):
+                    entry = distance * capacity + r * own + place
+                    turned_ref[turned.index(entry)] = held_ref[entries.slot(table_ref, entry)].T
                 terms = [pushed(distance * capacity + r * own + place) for r in range(own)]
                 total_ref[block * own + place] = sum(terms[1:], terms[0]).astype(total_ref.dtype)
         return
@@ -260,9 +267,10 @@
 
 def adjoint_kernel(entries, near_distances, far_distances, group, turned, *refs):
     table_ref, held_ref, turned_ref, tau_ref, elasticity_ref, cotangent_ref, near_weights, near_top, near_norm = refs[:9]
-    costs = refs[9:-10]
-    adjoint_ref, tau_grad_ref, logsum_ref, partial_ref = refs[-10:-6]
-    far_weights, far_top, far_norm, factor_ref, tau_rows_ref, total_ref = refs[-6:]
+    costs = refs[9:-11]
+    adjoint_ref, tau_grad_ref, logsum_ref, partial_ref = refs[-11:-7]
+    far_weights, far_top, far_norm, factor_ref, tau_rows_ref, total_ref, late_ref = refs[-7:]
+    late = [entry for entry in entries.numbers(group) if entry not in turned] if entries.dense else []
     own, capacity = entries.own, entries.capacity
     near, far = entries.numbers(near_distances), entries.numbers(far_distances)
     tau_rows_ref[...] = jnp.zeros(tau_rows_ref.shape, F32)
@@ -274,6 +282,8 @@
     def pushed(entry, value):
         if entry in turned:
             return jnp.dot(value, turned_ref[turned.index(entry)], preferred_element_type=F32)
+        if entry in late:
+            return jnp.dot(value, late_ref[late.index(entry)], preferred_element_type=F32)
         return lax.dot_general(
             value, held_ref[entries.slot(table_ref, entry)], CONTRACT_LAST, preferred_element_type=F32
         )
@@ -295,6 +305,9 @@
             if r < own:
                 for i in members[r]:
                     far_weights[i] = score(i)
+                for i, entry in enumerate(late):
+                    if r == own // 2:
+                        late_ref[i] = held_ref[entries.slot(table_ref, entry)].T
             if r == 0:
                 continue
             q = r - 1
@@ -336,8 +349,8 @@
     tau_grad_ref[...] = tau_rows_ref[pl.ds(0, entries.slot_count)].astype(tau_grad_ref.dtype)
 
 
-def push_kernel(entries, distances, table_ref, held_ref, adjoint_ref, partial_ref, total_ref):
-    push_entries(entries, distances, table_ref, lambda entry: adjoint_ref[entry], held_ref, total_ref)
+def push_kernel(entries, distances, table_ref, held_ref, adjoint_ref, partial_ref, total_ref, turned_ref):
+    push_entries(entries, distances, table_ref, lambda entry: adjoint_ref[entry], held_ref, total_ref, turned_ref)
     partial_ref[...] = total_ref[...].astype(partial_ref.dtype)
 
 
@@ -472,8 +485,9 @@
             pltpu.VMEM((2, own + 1) + row, F32),
             pltpu.VMEM((own * slots + 8, sectors), F32),
             pltpu.VMEM(partial_dims, F32),
+            pltpu.VMEM((max((len(groups[-1]) * entries.capacity - len(turned)) * entries.dense, 1), sectors, sectors), BF16),
         ],
-        compiler_params=params(8),
+        compiler_params=params(16),
         cost_estimate=effort(blocks.size),
         name="adjoint",
     )(table, held, turned_blocks, tau, elastic, cotangent, *near_scores, *received)
@@ -484,8 +498,11 @@
             out_shape=shape(partial_dims, dtype),
             in_specs=[SMEM, VMEM, VMEM],
             out_specs=VMEM,
-            scratch_shapes=[pltpu.VMEM(partial_dims, F32)],
-            compiler_params=params(8),
+            scratch_shapes=[
+                pltpu.VMEM(partial_dims, F32),
+                pltpu.VMEM((max(len(groups[j]) * own * (own // 2) * entries.dense, 1), sectors, sectors), BF16),
+            ],
+            compiler_params=params(16),
             cost_estimate=effort(blocks.size),
             name="push",
         )(table, held, adjoint)

time: 34.5 us -> 34.4 us (level)
  Pallas kernels: 13.3 us -> 12.8 us
    pallas_call x1, Pallas kernels: 2.26 us -> 1.86 us  [push(): pl.pallas_call(functools.partial(push_kernel, entries, groups[j]), out_sh...]
  transfers between devices with their start and end apart: 10 -> 10, of which waited for: 4 -> 4; matrix products, arithmetic and copies ran while one was open for 0% -> 0% of each run, Pallas kernels for 29% -> 28%
where the time goes in v8:
time: 34.4 us; the launch traced here: 34.1 us
  starting transfers between devices  14.2 us (41%)
  Pallas kernels  12.8 us (37%)
  waiting for transfers between devices  4.23 us (12%)
  matrix products  1.24 us (4%)
  local copies, waits for them, and re-layouts  0.78 us (2%)
  between operations  0.74 us (2%)
    ppermute x4, starting transfers between devices, from_peer(): return lax.ppermute(x, axis, [(peer(i, distance, n), i) for i in range(n)])  7.25 us
    ppermute x6, starting transfers between devices, to_peer(): return lax.ppermute(x, axis, [(i, peer(i, distance, n)) for i in range(n)])  7 us
    pallas_call x1, Pallas kernels, shards(): pl.pallas_call(functools.partial(near_kernel, entries, near_distances, tu...  3.95 us
    ppermute x6, waiting for transfers between devices, to_peer(): return lax.ppermute(x, axis, [(i, peer(i, distance, n)) for i in range(n)])  3.67 us
    pallas_call x1, Pallas kernels, shards(): pl.pallas_call(functools.partial(load_kernel, entries), out_shape=(shape(...  3.57 us
    pallas_call x1, Pallas kernels, shards(): pl.pallas_call(functools.partial(adjoint_kernel, entries, near_distances,...  2.53 us
    pallas_call x1, Pallas kernels, push(): pl.pallas_call(functools.partial(push_kernel, entries, groups[j]), out_sh...  1.86 us
    dot_general x1, matrix products, shards(): jnp.einsum('iek,ikj->iej', log_prices, io_coeffs, preferred_element_type=...  1.24 us
  transfers between devices with their start and end apart: 10, of which 4 were waited for; matrix products, arithmetic and copies ran while one was open for 0% of the time, Pallas kernels for 28%

profile of v8, /device:TPU:0, one launch (start us, length us, event | category | flops | bytes accessed | tf_op | source)
XLA Modules:
  0.0 34.1 jit_solution(16144498070818983114)
XLA Ops:
  0.6 0.0 copy-start
  0.6 0.7 %copy-done = bf16[4,16,256]{2,1,0:T(8,128)(2,1)S(1)} copy-done((bf16[4,16,256]{2,1,0:T(8,128)(2,1)S(1)}, bf16[4,16,256]{2,1,0:T(8,128)(2,1)}, u32[]{:S(2)}) %copy-start) | copy-done | bytes 32792
  1.4 1.2 %fusion.cost_ref = bf16[4,16,256]{2,1,0:T(8,128)(2,1)S(1)} fusion(bf16[4,16,256]{2,1,0:T(8,128)(2,1)S(1)} %copy-done, bf16[4,256,256]{2,1,0:T(8,128)(2,1)} %refs_4_.1, f32[4,16]{1,0:T(4,128)} %param.11, f32[4,256]{1,0:T(4,128)} %refs_5_.1), kind=kOutput, calls=%fused_computation.1 | convolution fusion | flops 8437760 | bytes 594176 | tf_op jit(solution)/shard_map/iek,ikj->iej/dot_general | solution.py:400
  2.6 4.1 %collective-permute-start = (bf16[4,16,256]{2,1,0:T(8,128)(2,1)S(1)}, bf16[4,16,256]{2,1,0:T(8,128)(2,1)S(1)}, u32[]{:S(2)}, u32[]{:S(2)}) collective-permute-start(bf16[4,16,256]{2,1,0:T(8,128)(2,1)S(1)} %fusion.cost_ref), channel_id=1, source_target_pairs={{16,0},{20,4},{24,8},{28,12},{0,16},{4,20},{8,24},{12,28},{17,1},{... | collective-permute-start | bytes 98312 | tf_op jit(solution)/shard_map/ppermute | solution.py:45
  6.7 1.3 %collective-permute-start.1 = (bf16[4,16,256]{2,1,0:T(8,128)(2,1)S(1)}, bf16[4,16,256]{2,1,0:T(8,128)(2,1)S(1)}, u32[]{:S(2)}, u32[]{:S(2)}) collective-permute-start(bf16[4,16,256]{2,1,0:T(8,128)(2,1)S(1)} %fusion.cost_ref), channel_id=1, source_target_pairs={{24,0},{28,4},{16,8},{20,12},{8,16},{12,20},{0,24},{4,28},{25,1},{... | collective-permute-start | bytes 98312 | tf_op jit(solution)/shard_map/ppermute | solution.py:45
  8.1 0.2 collective-permute-start.2
  8.3 3.6 %load.1 = (bf16[128,256,256]{2,1,0:T(8,128)(2,1)S(1)}, f32[128,256]{1,0:T(8,128)S(1)}, f32[4,16,256]{2,1,0:T(8,128)S(1)}, f32[1,256]{1,0:T(1,128)S(1)}, bf16[4,16,256]{2,1,0:T(8,128)(2,1)S(1)}, /*index=5*/s32[258]{0:T(512)S(4)}) custom-call(s32[1]{0:T(128)} %bitcast.me_ref, bf16[4,16,256]{2,1,0:T(8,128)(2,1)S(1)} %fusion.cost_ref, ...), custom_call_target="tpu_custom_call" | custom-call | bytes 8388608 | tf_op jit(solution)/shard_map/load/pallas_call | solution.py:403
  11.9 0.0 collective-permute-done.refs_6_
  11.9 0.5 %collective-permute-done.1.refs_7_ = bf16[4,16,256]{2,1,0:T(8,128)(2,1)S(1)} collective-permute-done((bf16[4,16,256]{2,1,0:T(8,128)(2,1)S(1)}, bf16[4,16,256]{2,1,0:T(8,128)(2,1)S(1)}, u32[]{:S(2)}, u32[]{:S(2)}) %collective-permute-start.1) | collective-permute-done | bytes 32800 | tf_op jit(solution)/shard_map/ppermute | solution.py:45
  12.4 0.0 collective-permute-done.2.refs_8_
  12.5 1.6 %collective-permute-start.3 = (bf16[16,16,256]{2,1,0:T(8,128)(2,1)S(1)}, bf16[16,16,256]{2,1,0:T(8,128)(2,1)S(1)}, u32[]{:S(2)}, u32[]{:S(2)}) collective-permute-start(bf16[16,16,256]{2,1,0:T(8,128)(2,1)S(1)} %pad_maximum_fusion), channel_id=1, source_target_pairs={{4,0},{0,4},{12,8},{8,12},{20,16},{16,20},{28,24},{24,28},{5,1},{1... | collective-permute-start | bytes 393224 | tf_op jit(solution)/shard_map/ppermute | solution.py:45
  14.0 3.9 %near.1 = (bf16[128,256,256]{2,1,0:T(8,128)(2,1)S(1)}, f32[64,16,256]{2,1,0:T(8,128)S(1)}, f32[5,16,256]{2,1,0:T(8,128)S(1)}, f32[5,16,256]{2,1,0:T(8,128)S(1)}, bf16[48,256,256]{2,1,0:T(8,128)(2,1)S(1)}) custom-call(s32[258]{0:T(512)S(4)} %get-tuple-element.23.refs_0_.table_ref, bf16[128,256,256]{2,1,0:T(8,128)(2,1)} %bitcast.17, ...), custom_call_target="tpu_custom_call", output_to_operand_aliasing={{0}: (2, {})} | custom-call | bytes 8388608 | tf_op jit(solution)/shard_map/near/pallas_call | solution.py:459
  18.0 0.0 collective-permute-done.3.refs_9_
  18.0 0.0 copy-start.1
  18.0 0.0 copy-start.2
  18.0 2.5 %adjoint.1 = (bf16[128,16,256]{2,1,0:T(8,128)(2,1)S(1)}, bf16[128,256]{1,0:T(8,128)(2,1)S(1)}, f32[4,16,256]{2,1,0:T(8,128)S(1)}, bf16[16,16,256]{2,1,0:T(8,128)(2,1)S(1)}) custom-call(s32[258]{0:T(512)S(4)} %get-tuple-element.23.refs_0_.table_ref, bf16[128,256,256]{2,1,0:T(8,128)(2,1)S(1)} %get-tuple-element.28.refs_1_.held_ref, ...), custom_call_target="tpu_custom_call" | custom-call | bytes 8388608 | tf_op jit(solution)/shard_map/adjoint/pallas_call | solution.py:473
  20.6 1.0 %collective-permute-start.4 = (bf16[16,16,256]{2,1,0:T(8,128)(2,1)S(1)}, bf16[16,16,256]{2,1,0:T(8,128)(2,1)S(1)}, u32[]{:S(2)}, u32[]{:S(2)}) collective-permute-start(bf16[16,16,256]{2,1,0:T(8,128)(2,1)S(1)} %get-tuple-element.35), channel_id=1, source_target_pairs={{0,4},{4,0},{8,12},{12,8},{16,20},{20,16},{24,28},{28,24},{1,5},{5... | collective-permute-start | bytes 393224 | tf_op jit(solution)/shard_map/ppermute | solution.py:49
  21.6 0.0 collective-permute-start.8
  21.6 1.9 %push.1 = f32[16,16,256]{2,1,0:T(8,128)S(1)} custom-call(s32[258]{0:T(512)S(4)} %get-tuple-element.23.refs_0_.table_ref, bf16[128,256,256]{2,1,0:T(8,128)(2,1)S(1)} %get-tuple-element.28.refs_1_.held_ref, bf16[128,16,256]{2,1,0:T(8,128)(2,1)S(1)} %get-tuple-element.34.adjoint_ref), custom_call_target="tpu_custom_call" | custom-call | bytes 8388608 | tf_op jit(solution)/shard_map/push/pallas_call | solution.py:496
  23.4 0.0 collective-permute-done.8.y_ref
  23.4 1.6 %collective-permute-start.9 = (f32[128,256]{1,0:T(8,128)S(1)}, f32[128,256]{1,0:T(8,128)S(1)}, u32[]{:S(2)}, u32[]{:S(2)}) collective-permute-start(f32[128,256]{1,0:T(8,128)S(1)} %add.13.refs_8_), channel_id=1, source_target_pairs={{0,2},{1,3},{2,0},{3,1},{4,6},{5,7},{6,4},{7,5},{8,10},{9,11},{10,... | collective-permute-start | bytes 393224 | tf_op jit(solution)/shard_map/ppermute | solution.py:49
  25.0 0.6 %collective-permute-done.4 = bf16[16,16,256]{2,1,0:T(8,128)(2,1)S(1)} collective-permute-done((bf16[16,16,256]{2,1,0:T(8,128)(2,1)S(1)}, bf16[16,16,256]{2,1,0:T(8,128)(2,1)S(1)}, u32[]{:S(2)}, u32[]{:S(2)}) %collective-permute-start.4) | collective-permute-done | bytes 131104 | tf_op jit(solution)/shard_map/ppermute | solution.py:49
  25.6 2.5 %collective-permute-start.5 = (bf16[4,16,256]{2,1,0:T(8,128)(2,1)S(1)}, bf16[4,16,256]{2,1,0:T(8,128)(2,1)S(1)}, u32[]{:S(2)}, u32[]{:S(2)}) collective-permute-start(bf16[4,16,256]{2,1,0:T(8,128)(2,1)S(1)} %get-tuple-element.44), channel_id=1, source_target_pairs={{0,24},{4,28},{8,16},{12,20},{16,8},{20,12},{24,0},{28,4},{1,25},{... | collective-permute-start | bytes 98312 | tf_op jit(solution)/shard_map/ppermute | solution.py:49
  28.1 0.3 collective-permute-start.6
  28.4 1.7 %collective-permute-start.7 = (bf16[4,16,256]{2,1,0:T(8,128)(2,1)S(1)}, bf16[4,16,256]{2,1,0:T(8,128)(2,1)S(1)}, u32[]{:S(2)}, u32[]{:S(2)}) collective-permute-start(bf16[4,16,256]{2,1,0:T(8,128)(2,1)S(1)} %get-tuple-element.42), channel_id=1, source_target_pairs={{0,8},{4,12},{8,0},{12,4},{16,24},{20,28},{24,16},{28,20},{1,9},{5... | collective-permute-start | bytes 98312 | tf_op jit(solution)/shard_map/ppermute | solution.py:49
  30.1 1.5 %collective-permute-done.5.refs_1_ = bf16[4,16,256]{2,1,0:T(8,128)(2,1)S(1)} collective-permute-done((bf16[4,16,256]{2,1,0:T(8,128)(2,1)S(1)}, bf16[4,16,256]{2,1,0:T(8,128)(2,1)S(1)}, u32[]{:S(2)}, u32[]{:S(2)}) %collective-permute-start.5) | collective-permute-done | bytes 32800 | tf_op jit(solution)/shard_map/ppermute | solution.py:49
  31.6 1.6 %collective-permute-done.6.refs_2_ = bf16[4,16,256]{2,1,0:T(8,128)(2,1)S(1)} collective-permute-done((bf16[4,16,256]{2,1,0:T(8,128)(2,1)S(1)}, bf16[4,16,256]{2,1,0:T(8,128)(2,1)S(1)}, u32[]{:S(2)}, u32[]{:S(2)}) %collective-permute-start.6) | collective-permute-done | bytes 32800 | tf_op jit(solution)/shard_map/ppermute | solution.py:49
  33.2 0.0 collective-permute-done.7.refs_3_
  33.2 0.0 collective-permute-done.9.refs_9_
  33.2 0.0 copy-done.1
  33.2 0.0 copy-done.2
  33.2 0.9 %finish.1 = (bf16[4,16,256]{2,1,0:T(8,128)(2,1)}, f32[4,16,256]{2,1,0:T(8,128)}, f32[4,16]{1,0:T(4,128)}, f32[128,256]{1,0:T(8,128)}) custom-call(f32[4,16,256]{2,1,0:T(8,128)S(1)} %slice_bitcast_fusion.refs_0_, bf16[4,16,256]{2,1,0:T(8,128)(2,1)S(1)} %collective-permute-done.5.refs_1_, bf16[4,16,256]{2,1,0:T(8,128)(2,1)S(1)} %collective-permute-done.6.refs_2_, ...), custom_call_target="tpu_custom_call" | custom-call | tf_op jit(solution)/shard_map/finish/pallas_call | solution.py:547
  (6 shorter events, 0.1 us)
Async XLA Ops:
  0.6 0.8 %copy-start = (bf16[4,16,256]{2,1,0:T(8,128)(2,1)S(1)}, bf16[4,16,256]{2,1,0:T(8,128)(2,1)}, u32[]{:S(2)}) copy-start(bf16[4,16,256]{2,1,0:T(8,128)(2,1)} %param.10) | copy-start | bytes 98308
  2.6 9.2 %collective-permute-start = (bf16[4,16,256]{2,1,0:T(8,128)(2,1)S(1)}, bf16[4,16,256]{2,1,0:T(8,128)(2,1)S(1)}, u32[]{:S(2)}, u32[]{:S(2)}) collective-permute-start(bf16[4,16,256]{2,1,0:T(8,128)(2,1)S(1)} %fusion.cost_ref), channel_id=1, source_target_pairs={{16,0},{20,4},{24,8},{28,12},{0,16},{4,20},{8,24},{12,28},{17,1},{... | collective-permute-start | bytes 98312 | tf_op jit(solution)/shard_map/ppermute | solution.py:45
  6.7 5.7 %collective-permute-start.1 = (bf16[4,16,256]{2,1,0:T(8,128)(2,1)S(1)}, bf16[4,16,256]{2,1,0:T(8,128)(2,1)S(1)}, u32[]{:S(2)}, u32[]{:S(2)}) collective-permute-start(bf16[4,16,256]{2,1,0:T(8,128)(2,1)S(1)} %fusion.cost_ref), channel_id=1, source_target_pairs={{24,0},{28,4},{16,8},{20,12},{8,16},{12,20},{0,24},{4,28},{25,1},{... | collective-permute-start | bytes 98312 | tf_op jit(solution)/shard_map/ppermute | solution.py:45
  8.1 4.4 %collective-permute-start.2 = (bf16[4,16,256]{2,1,0:T(8,128)(2,1)S(1)}, bf16[4,16,256]{2,1,0:T(8,128)(2,1)S(1)}, u32[]{:S(2)}, u32[]{:S(2)}) collective-permute-start(bf16[4,16,256]{2,1,0:T(8,128)(2,1)S(1)} %fusion.cost_ref), channel_id=1, source_target_pairs={{8,0},{12,4},{0,8},{4,12},{24,16},{28,20},{16,24},{20,28},{9,1},{1... | collective-permute-start | bytes 98312 | tf_op jit(solution)/shard_map/ppermute | solution.py:45
  12.5 5.5 %collective-permute-start.3 = (bf16[16,16,256]{2,1,0:T(8,128)(2,1)S(1)}, bf16[16,16,256]{2,1,0:T(8,128)(2,1)S(1)}, u32[]{:S(2)}, u32[]{:S(2)}) collective-permute-start(bf16[16,16,256]{2,1,0:T(8,128)(2,1)S(1)} %pad_maximum_fusion), channel_id=1, source_target_pairs={{4,0},{0,4},{12,8},{8,12},{20,16},{16,20},{28,24},{24,28},{5,1},{1... | collective-permute-start | bytes 393224 | tf_op jit(solution)/shard_map/ppermute | solution.py:45
  18.0 15.2 %copy-start.1 = (bf16[4,256,256]{2,1,0:T(8,128)(2,1)S(1)}, bf16[4,256,256]{2,1,0:T(8,128)(2,1)}, u32[]{:S(2)}) copy-start(bf16[4,256,256]{2,1,0:T(8,128)(2,1)} %refs_4_.1) | copy-start | bytes 1572868
  18.0 15.2 %copy-start.2 = (f32[4,256]{1,0:T(4,128)S(1)}, f32[4,256]{1,0:T(4,128)}, u32[]{:S(2)}) copy-start(f32[4,256]{1,0:T(4,128)} %refs_5_.1) | copy-start | bytes 12292
  20.6 5.0 %collective-permute-start.4 = (bf16[16,16,256]{2,1,0:T(8,128)(2,1)S(1)}, bf16[16,16,256]{2,1,0:T(8,128)(2,1)S(1)}, u32[]{:S(2)}, u32[]{:S(2)}) collective-permute-start(bf16[16,16,256]{2,1,0:T(8,128)(2,1)S(1)} %get-tuple-element.35), channel_id=1, source_target_pairs={{0,4},{4,0},{8,12},{12,8},{16,20},{20,16},{24,28},{28,24},{1,5},{5... | collective-permute-start | bytes 393224 | tf_op jit(solution)/shard_map/ppermute | solution.py:49
  21.6 1.9 %collective-permute-start.8 = (bf16[128,256]{1,0:T(8,128)(2,1)S(1)}, bf16[128,256]{1,0:T(8,128)(2,1)S(1)}, u32[]{:S(2)}, u32[]{:S(2)}) collective-permute-start(bf16[128,256]{1,0:T(8,128)(2,1)S(1)} %get-tuple-element.37.x_ref), channel_id=1, source_target_pairs={{0,1},{1,0},{2,3},{3,2},{4,5},{5,4},{6,7},{7,6},{8,9},{9,8},{10,11... | collective-permute-start | bytes 196616 | tf_op jit(solution)/shard_map/ppermute | solution.py:49
  23.4 9.8 %collective-permute-start.9 = (f32[128,256]{1,0:T(8,128)S(1)}, f32[128,256]{1,0:T(8,128)S(1)}, u32[]{:S(2)}, u32[]{:S(2)}) collective-permute-start(f32[128,256]{1,0:T(8,128)S(1)} %add.13.refs_8_), channel_id=1, source_target_pairs={{0,2},{1,3},{2,0},{3,1},{4,6},{5,7},{6,4},{7,5},{8,10},{9,11},{10,... | collective-permute-start | bytes 393224 | tf_op jit(solution)/shard_map/ppermute | solution.py:49
  25.6 6.0 %collective-permute-start.5 = (bf16[4,16,256]{2,1,0:T(8,128)(2,1)S(1)}, bf16[4,16,256]{2,1,0:T(8,128)(2,1)S(1)}, u32[]{:S(2)}, u32[]{:S(2)}) collective-permute-start(bf16[4,16,256]{2,1,0:T(8,128)(2,1)S(1)} %get-tuple-element.44), channel_id=1, source_target_pairs={{0,24},{4,28},{8,16},{12,20},{16,8},{20,12},{24,0},{28,4},{1,25},{... | collective-permute-start | bytes 98312 | tf_op jit(solution)/shard_map/ppermute | solution.py:49
  28.1 5.1 %collective-permute-start.6 = (bf16[4,16,256]{2,1,0:T(8,128)(2,1)S(1)}, bf16[4,16,256]{2,1,0:T(8,128)(2,1)S(1)}, u32[]{:S(2)}, u32[]{:S(2)}) collective-permute-start(bf16[4,16,256]{2,1,0:T(8,128)(2,1)S(1)} %get-tuple-element.43), channel_id=1, source_target_pairs={{0,16},{4,20},{8,24},{12,28},{16,0},{20,4},{24,8},{28,12},{1,17},{... | collective-permute-start | bytes 98312 | tf_op jit(solution)/shard_map/ppermute | solution.py:49
  28.4 4.8 %collective-permute-start.7 = (bf16[4,16,256]{2,1,0:T(8,128)(2,1)S(1)}, bf16[4,16,256]{2,1,0:T(8,128)(2,1)S(1)}, u32[]{:S(2)}, u32[]{:S(2)}) collective-permute-start(bf16[4,16,256]{2,1,0:T(8,128)(2,1)S(1)} %get-tuple-element.42), channel_id=1, source_target_pairs={{0,8},{4,12},{8,0},{12,4},{16,24},{20,28},{24,16},{28,20},{1,9},{5... | collective-permute-start | bytes 98312 | tf_op jit(solution)/shard_map/ppermute | solution.py:49

commit v9 on v8

--- a/solution.py
+++ b/solution.py
@@ -69,7 +69,7 @@
     def __init__(self, own, slots, reg_count):
         self.own, self.slots, self.reg_count = own, slots, reg_count
         self.slot_count = own * slots
-        self.loaded_first = 4 * own * slots // 8
+        self.loaded_first = 15 * own * slots // 32
         self.dense = reg_count * own <= slots
         self.capacity = own * own if self.dense else -(-own * slots // reg_count)
         self.count = self.capacity * reg_count

time: 34.4 us -> 34.3 us (level)
  no operation moved by 1% of the time
where the time goes in v9:
time: 34.3 us; the launch traced here: 34.1 us
  starting transfers between devices  14.1 us (41%)
  Pallas kernels  12.8 us (37%)
  waiting for transfers between devices  4.34 us (13%)
  matrix products  1.24 us (4%)
  local copies, waits for them, and re-layouts  0.78 us (2%)
  between operations  0.74 us (2%)
    ppermute x4, starting transfers between devices, from_peer(): return lax.ppermute(x, axis, [(peer(i, distance, n), i) for i in range(n)])  7.25 us
    ppermute x6, starting transfers between devices, to_peer(): return lax.ppermute(x, axis, [(i, peer(i, distance, n)) for i in range(n)])  6.82 us
    pallas_call x1, Pallas kernels, shards(): pl.pallas_call(functools.partial(near_kernel, entries, near_distances, tu...  4.12 us
    ppermute x6, waiting for transfers between devices, to_peer(): return lax.ppermute(x, axis, [(i, peer(i, distance, n)) for i in range(n)])  3.63 us
    pallas_call x1, Pallas kernels, shards(): pl.pallas_call(functools.partial(load_kernel, entries), out_shape=(shape(...  3.42 us
    pallas_call x1, Pallas kernels, shards(): pl.pallas_call(functools.partial(adjoint_kernel, entries, near_distances,...  2.53 us
    pallas_call x1, Pallas kernels, push(): pl.pallas_call(functools.partial(push_kernel, entries, groups[j]), out_sh...  1.86 us
    dot_general x1, matrix products, shards(): jnp.einsum('iek,ikj->iej', log_prices, io_coeffs, preferred_element_type=...  1.24 us
  transfers between devices with their start and end apart: 10, of which 4 were waited for; matrix products, arithmetic and copies ran while one was open for 0% of the time, Pallas kernels for 28%

profile of v9, /device:TPU:0, one launch (start us, length us, event | category | flops | bytes accessed | tf_op | source)
XLA Modules:
  0.0 34.1 jit_solution(15401118325784249097)
XLA Ops:
  0.6 0.0 copy-start
  0.6 0.7 %copy-done = bf16[4,16,256]{2,1,0:T(8,128)(2,1)S(1)} copy-done((bf16[4,16,256]{2,1,0:T(8,128)(2,1)S(1)}, bf16[4,16,256]{2,1,0:T(8,128)(2,1)}, u32[]{:S(2)}) %copy-start) | copy-done | bytes 32792
  1.4 1.2 %fusion.cost_ref = bf16[4,16,256]{2,1,0:T(8,128)(2,1)S(1)} fusion(bf16[4,16,256]{2,1,0:T(8,128)(2,1)S(1)} %copy-done, bf16[4,256,256]{2,1,0:T(8,128)(2,1)} %refs_4_.1, f32[4,16]{1,0:T(4,128)} %param.11, f32[4,256]{1,0:T(4,128)} %refs_5_.1), kind=kOutput, calls=%fused_computation.1 | convolution fusion | flops 8437760 | bytes 594176 | tf_op jit(solution)/shard_map/iek,ikj->iej/dot_general | solution.py:400
  2.6 4.1 %collective-permute-start = (bf16[4,16,256]{2,1,0:T(8,128)(2,1)S(1)}, bf16[4,16,256]{2,1,0:T(8,128)(2,1)S(1)}, u32[]{:S(2)}, u32[]{:S(2)}) collective-permute-start(bf16[4,16,256]{2,1,0:T(8,128)(2,1)S(1)} %fusion.cost_ref), channel_id=1, source_target_pairs={{16,0},{20,4},{24,8},{28,12},{0,16},{4,20},{8,24},{12,28},{17,1},{... | collective-permute-start | bytes 98312 | tf_op jit(solution)/shard_map/ppermute | solution.py:45
  6.7 1.3 %collective-permute-start.1 = (bf16[4,16,256]{2,1,0:T(8,128)(2,1)S(1)}, bf16[4,16,256]{2,1,0:T(8,128)(2,1)S(1)}, u32[]{:S(2)}, u32[]{:S(2)}) collective-permute-start(bf16[4,16,256]{2,1,0:T(8,128)(2,1)S(1)} %fusion.cost_ref), channel_id=1, source_target_pairs={{24,0},{28,4},{16,8},{20,12},{8,16},{12,20},{0,24},{4,28},{25,1},{... | collective-permute-start | bytes 98312 | tf_op jit(solution)/shard_map/ppermute | solution.py:45
  8.1 0.2 collective-permute-start.2
  8.3 3.4 %load.1 = (bf16[128,256,256]{2,1,0:T(8,128)(2,1)S(1)}, f32[128,256]{1,0:T(8,128)S(1)}, f32[4,16,256]{2,1,0:T(8,128)S(1)}, f32[1,256]{1,0:T(1,128)S(1)}, bf16[4,16,256]{2,1,0:T(8,128)(2,1)S(1)}, /*index=5*/s32[258]{0:T(512)S(4)}) custom-call(s32[1]{0:T(128)} %bitcast.me_ref, bf16[4,16,256]{2,1,0:T(8,128)(2,1)S(1)} %fusion.cost_ref, ...), custom_call_target="tpu_custom_call" | custom-call | bytes 8388608 | tf_op jit(solution)/shard_map/load/pallas_call | solution.py:403
  11.7 0.0 collective-permute-done.refs_6_
  11.7 0.7 %collective-permute-done.1.refs_7_ = bf16[4,16,256]{2,1,0:T(8,128)(2,1)S(1)} collective-permute-done((bf16[4,16,256]{2,1,0:T(8,128)(2,1)S(1)}, bf16[4,16,256]{2,1,0:T(8,128)(2,1)S(1)}, u32[]{:S(2)}, u32[]{:S(2)}) %collective-permute-start.1) | collective-permute-done | bytes 32800 | tf_op jit(solution)/shard_map/ppermute | solution.py:45
  12.4 0.0 collective-permute-done.2.refs_8_
  12.5 1.6 %collective-permute-start.3 = (bf16[16,16,256]{2,1,0:T(8,128)(2,1)S(1)}, bf16[16,16,256]{2,1,0:T(8,128)(2,1)S(1)}, u32[]{:S(2)}, u32[]{:S(2)}) collective-permute-start(bf16[16,16,256]{2,1,0:T(8,128)(2,1)S(1)} %pad_maximum_fusion), channel_id=1, source_target_pairs={{4,0},{0,4},{12,8},{8,12},{20,16},{16,20},{28,24},{24,28},{5,1},{1... | collective-permute-start | bytes 393224 | tf_op jit(solution)/shard_map/ppermute | solution.py:45
  14.0 4.1 %near.1 = (bf16[128,256,256]{2,1,0:T(8,128)(2,1)S(1)}, f32[64,16,256]{2,1,0:T(8,128)S(1)}, f32[5,16,256]{2,1,0:T(8,128)S(1)}, f32[5,16,256]{2,1,0:T(8,128)S(1)}, bf16[48,256,256]{2,1,0:T(8,128)(2,1)S(1)}) custom-call(s32[258]{0:T(512)S(4)} %get-tuple-element.23.refs_0_.table_ref, bf16[128,256,256]{2,1,0:T(8,128)(2,1)} %bitcast.17, ...), custom_call_target="tpu_custom_call", output_to_operand_aliasing={{0}: (2, {})} | custom-call | bytes 8388608 | tf_op jit(solution)/shard_map/near/pallas_call | solution.py:459
  18.2 0.0 collective-permute-done.3.refs_9_
  18.2 0.0 copy-start.1
  18.2 0.0 copy-start.2
  18.2 2.5 %adjoint.1 = (bf16[128,16,256]{2,1,0:T(8,128)(2,1)S(1)}, bf16[128,256]{1,0:T(8,128)(2,1)S(1)}, f32[4,16,256]{2,1,0:T(8,128)S(1)}, bf16[16,16,256]{2,1,0:T(8,128)(2,1)S(1)}) custom-call(s32[258]{0:T(512)S(4)} %get-tuple-element.23.refs_0_.table_ref, bf16[128,256,256]{2,1,0:T(8,128)(2,1)S(1)} %get-tuple-element.28.refs_1_.held_ref, ...), custom_call_target="tpu_custom_call" | custom-call | bytes 8388608 | tf_op jit(solution)/shard_map/adjoint/pallas_call | solution.py:473
  20.7 0.8 %collective-permute-start.4 = (bf16[16,16,256]{2,1,0:T(8,128)(2,1)S(1)}, bf16[16,16,256]{2,1,0:T(8,128)(2,1)S(1)}, u32[]{:S(2)}, u32[]{:S(2)}) collective-permute-start(bf16[16,16,256]{2,1,0:T(8,128)(2,1)S(1)} %get-tuple-element.35), channel_id=1, source_target_pairs={{0,4},{4,0},{8,12},{12,8},{16,20},{20,16},{24,28},{28,24},{1,5},{5... | collective-permute-start | bytes 393224 | tf_op jit(solution)/shard_map/ppermute | solution.py:49
  21.5 0.0 collective-permute-start.8
  21.6 1.9 %push.1 = f32[16,16,256]{2,1,0:T(8,128)S(1)} custom-call(s32[258]{0:T(512)S(4)} %get-tuple-element.23.refs_0_.table_ref, bf16[128,256,256]{2,1,0:T(8,128)(2,1)S(1)} %get-tuple-element.28.refs_1_.held_ref, bf16[128,16,256]{2,1,0:T(8,128)(2,1)S(1)} %get-tuple-element.34.adjoint_ref), custom_call_target="tpu_custom_call" | custom-call | bytes 8388608 | tf_op jit(solution)/shard_map/push/pallas_call | solution.py:496
  23.4 0.0 collective-permute-done.8.y_ref
  23.4 1.6 %collective-permute-start.9 = (f32[128,256]{1,0:T(8,128)S(1)}, f32[128,256]{1,0:T(8,128)S(1)}, u32[]{:S(2)}, u32[]{:S(2)}) collective-permute-start(f32[128,256]{1,0:T(8,128)S(1)} %add.13.refs_8_), channel_id=1, source_target_pairs={{0,2},{1,3},{2,0},{3,1},{4,6},{5,7},{6,4},{7,5},{8,10},{9,11},{10,... | collective-permute-start | bytes 393224 | tf_op jit(solution)/shard_map/ppermute | solution.py:49
  25.0 0.7 %collective-permute-done.4 = bf16[16,16,256]{2,1,0:T(8,128)(2,1)S(1)} collective-permute-done((bf16[16,16,256]{2,1,0:T(8,128)(2,1)S(1)}, bf16[16,16,256]{2,1,0:T(8,128)(2,1)S(1)}, u32[]{:S(2)}, u32[]{:S(2)}) %collective-permute-start.4) | collective-permute-done | bytes 131104 | tf_op jit(solution)/shard_map/ppermute | solution.py:49
  25.8 2.3 %collective-permute-start.5 = (bf16[4,16,256]{2,1,0:T(8,128)(2,1)S(1)}, bf16[4,16,256]{2,1,0:T(8,128)(2,1)S(1)}, u32[]{:S(2)}, u32[]{:S(2)}) collective-permute-start(bf16[4,16,256]{2,1,0:T(8,128)(2,1)S(1)} %get-tuple-element.44), channel_id=1, source_target_pairs={{0,24},{4,28},{8,16},{12,20},{16,8},{20,12},{24,0},{28,4},{1,25},{... | collective-permute-start | bytes 98312 | tf_op jit(solution)/shard_map/ppermute | solution.py:49
  28.1 0.3 collective-permute-start.6
  28.4 1.8 %collective-permute-start.7 = (bf16[4,16,256]{2,1,0:T(8,128)(2,1)S(1)}, bf16[4,16,256]{2,1,0:T(8,128)(2,1)S(1)}, u32[]{:S(2)}, u32[]{:S(2)}) collective-permute-start(bf16[4,16,256]{2,1,0:T(8,128)(2,1)S(1)} %get-tuple-element.42), channel_id=1, source_target_pairs={{0,8},{4,12},{8,0},{12,4},{16,24},{20,28},{24,16},{28,20},{1,9},{5... | collective-permute-start | bytes 98312 | tf_op jit(solution)/shard_map/ppermute | solution.py:49
  30.3 1.3 %collective-permute-done.5.refs_1_ = bf16[4,16,256]{2,1,0:T(8,128)(2,1)S(1)} collective-permute-done((bf16[4,16,256]{2,1,0:T(8,128)(2,1)S(1)}, bf16[4,16,256]{2,1,0:T(8,128)(2,1)S(1)}, u32[]{:S(2)}, u32[]{:S(2)}) %collective-permute-start.5) | collective-permute-done | bytes 32800 | tf_op jit(solution)/shard_map/ppermute | solution.py:49
  31.6 1.6 %collective-permute-done.6.refs_2_ = bf16[4,16,256]{2,1,0:T(8,128)(2,1)S(1)} collective-permute-done((bf16[4,16,256]{2,1,0:T(8,128)(2,1)S(1)}, bf16[4,16,256]{2,1,0:T(8,128)(2,1)S(1)}, u32[]{:S(2)}, u32[]{:S(2)}) %collective-permute-start.6) | collective-permute-done | bytes 32800 | tf_op jit(solution)/shard_map/ppermute | solution.py:49
  33.2 0.0 collective-permute-done.7.refs_3_
  33.2 0.0 collective-permute-done.9.refs_9_
  33.2 0.0 copy-done.1
  33.2 0.0 copy-done.2
  33.2 0.9 %finish.1 = (bf16[4,16,256]{2,1,0:T(8,128)(2,1)}, f32[4,16,256]{2,1,0:T(8,128)}, f32[4,16]{1,0:T(4,128)}, f32[128,256]{1,0:T(8,128)}) custom-call(f32[4,16,256]{2,1,0:T(8,128)S(1)} %slice_bitcast_fusion.refs_0_, bf16[4,16,256]{2,1,0:T(8,128)(2,1)S(1)} %collective-permute-done.5.refs_1_, bf16[4,16,256]{2,1,0:T(8,128)(2,1)S(1)} %collective-permute-done.6.refs_2_, ...), custom_call_target="tpu_custom_call" | custom-call | tf_op jit(solution)/shard_map/finish/pallas_call | solution.py:547
  (6 shorter events, 0.1 us)
Async XLA Ops:
  0.6 0.8 %copy-start = (bf16[4,16,256]{2,1,0:T(8,128)(2,1)S(1)}, bf16[4,16,256]{2,1,0:T(8,128)(2,1)}, u32[]{:S(2)}) copy-start(bf16[4,16,256]{2,1,0:T(8,128)(2,1)} %param.10) | copy-start | bytes 98308
  2.6 9.1 %collective-permute-start = (bf16[4,16,256]{2,1,0:T(8,128)(2,1)S(1)}, bf16[4,16,256]{2,1,0:T(8,128)(2,1)S(1)}, u32[]{:S(2)}, u32[]{:S(2)}) collective-permute-start(bf16[4,16,256]{2,1,0:T(8,128)(2,1)S(1)} %fusion.cost_ref), channel_id=1, source_target_pairs={{16,0},{20,4},{24,8},{28,12},{0,16},{4,20},{8,24},{12,28},{17,1},{... | collective-permute-start | bytes 98312 | tf_op jit(solution)/shard_map/ppermute | solution.py:45
  6.7 5.7 %collective-permute-start.1 = (bf16[4,16,256]{2,1,0:T(8,128)(2,1)S(1)}, bf16[4,16,256]{2,1,0:T(8,128)(2,1)S(1)}, u32[]{:S(2)}, u32[]{:S(2)}) collective-permute-start(bf16[4,16,256]{2,1,0:T(8,128)(2,1)S(1)} %fusion.cost_ref), channel_id=1, source_target_pairs={{24,0},{28,4},{16,8},{20,12},{8,16},{12,20},{0,24},{4,28},{25,1},{... | collective-permute-start | bytes 98312 | tf_op jit(solution)/shard_map/ppermute | solution.py:45
  8.1 4.4 %collective-permute-start.2 = (bf16[4,16,256]{2,1,0:T(8,128)(2,1)S(1)}, bf16[4,16,256]{2,1,0:T(8,128)(2,1)S(1)}, u32[]{:S(2)}, u32[]{:S(2)}) collective-permute-start(bf16[4,16,256]{2,1,0:T(8,128)(2,1)S(1)} %fusion.cost_ref), channel_id=1, source_target_pairs={{8,0},{12,4},{0,8},{4,12},{24,16},{28,20},{16,24},{20,28},{9,1},{1... | collective-permute-start | bytes 98312 | tf_op jit(solution)/shard_map/ppermute | solution.py:45
  12.5 5.7 %collective-permute-start.3 = (bf16[16,16,256]{2,1,0:T(8,128)(2,1)S(1)}, bf16[16,16,256]{2,1,0:T(8,128)(2,1)S(1)}, u32[]{:S(2)}, u32[]{:S(2)}) collective-permute-start(bf16[16,16,256]{2,1,0:T(8,128)(2,1)S(1)} %pad_maximum_fusion), channel_id=1, source_target_pairs={{4,0},{0,4},{12,8},{8,12},{20,16},{16,20},{28,24},{24,28},{5,1},{1... | collective-permute-start | bytes 393224 | tf_op jit(solution)/shard_map/ppermute | solution.py:45
  18.2 15.0 %copy-start.1 = (bf16[4,256,256]{2,1,0:T(8,128)(2,1)S(1)}, bf16[4,256,256]{2,1,0:T(8,128)(2,1)}, u32[]{:S(2)}) copy-start(bf16[4,256,256]{2,1,0:T(8,128)(2,1)} %refs_4_.1) | copy-start | bytes 1572868
  18.2 15.0 %copy-start.2 = (f32[4,256]{1,0:T(4,128)S(1)}, f32[4,256]{1,0:T(4,128)}, u32[]{:S(2)}) copy-start(f32[4,256]{1,0:T(4,128)} %refs_5_.1) | copy-start | bytes 12292
  20.7 5.0 %collective-permute-start.4 = (bf16[16,16,256]{2,1,0:T(8,128)(2,1)S(1)}, bf16[16,16,256]{2,1,0:T(8,128)(2,1)S(1)}, u32[]{:S(2)}, u32[]{:S(2)}) collective-permute-start(bf16[16,16,256]{2,1,0:T(8,128)(2,1)S(1)} %get-tuple-element.35), channel_id=1, source_target_pairs={{0,4},{4,0},{8,12},{12,8},{16,20},{20,16},{24,28},{28,24},{1,5},{5... | collective-permute-start | bytes 393224 | tf_op jit(solution)/shard_map/ppermute | solution.py:49
  21.5 1.9 %collective-permute-start.8 = (bf16[128,256]{1,0:T(8,128)(2,1)S(1)}, bf16[128,256]{1,0:T(8,128)(2,1)S(1)}, u32[]{:S(2)}, u32[]{:S(2)}) collective-permute-start(bf16[128,256]{1,0:T(8,128)(2,1)S(1)} %get-tuple-element.37.x_ref), channel_id=1, source_target_pairs={{0,1},{1,0},{2,3},{3,2},{4,5},{5,4},{6,7},{7,6},{8,9},{9,8},{10,11... | collective-permute-start | bytes 196616 | tf_op jit(solution)/shard_map/ppermute | solution.py:49
  23.4 9.7 %collective-permute-start.9 = (f32[128,256]{1,0:T(8,128)S(1)}, f32[128,256]{1,0:T(8,128)S(1)}, u32[]{:S(2)}, u32[]{:S(2)}) collective-permute-start(f32[128,256]{1,0:T(8,128)S(1)} %add.13.refs_8_), channel_id=1, source_target_pairs={{0,2},{1,3},{2,0},{3,1},{4,6},{5,7},{6,4},{7,5},{8,10},{9,11},{10,... | collective-permute-start | bytes 393224 | tf_op jit(solution)/shard_map/ppermute | solution.py:49
  25.8 5.8 %collective-permute-start.5 = (bf16[4,16,256]{2,1,0:T(8,128)(2,1)S(1)}, bf16[4,16,256]{2,1,0:T(8,128)(2,1)S(1)}, u32[]{:S(2)}, u32[]{:S(2)}) collective-permute-start(bf16[4,16,256]{2,1,0:T(8,128)(2,1)S(1)} %get-tuple-element.44), channel_id=1, source_target_pairs={{0,24},{4,28},{8,16},{12,20},{16,8},{20,12},{24,0},{28,4},{1,25},{... | collective-permute-start | bytes 98312 | tf_op jit(solution)/shard_map/ppermute | solution.py:49
  28.1 5.0 %collective-permute-start.6 = (bf16[4,16,256]{2,1,0:T(8,128)(2,1)S(1)}, bf16[4,16,256]{2,1,0:T(8,128)(2,1)S(1)}, u32[]{:S(2)}, u32[]{:S(2)}) collective-permute-start(bf16[4,16,256]{2,1,0:T(8,128)(2,1)S(1)} %get-tuple-element.43), channel_id=1, source_target_pairs={{0,16},{4,20},{8,24},{12,28},{16,0},{20,4},{24,8},{28,12},{1,17},{... | collective-permute-start | bytes 98312 | tf_op jit(solution)/shard_map/ppermute | solution.py:49
  28.4 4.7 %collective-permute-start.7 = (bf16[4,16,256]{2,1,0:T(8,128)(2,1)S(1)}, bf16[4,16,256]{2,1,0:T(8,128)(2,1)S(1)}, u32[]{:S(2)}, u32[]{:S(2)}) collective-permute-start(bf16[4,16,256]{2,1,0:T(8,128)(2,1)S(1)} %get-tuple-element.42), channel_id=1, source_target_pairs={{0,8},{4,12},{8,0},{12,4},{16,24},{20,28},{24,16},{28,20},{1,9},{5... | collective-permute-start | bytes 98312 | tf_op jit(solution)/shard_map/ppermute | solution.py:49
